TPU v7x, 32 devices: a whole 2x2x4 slice. The times are simulated.
32 devices in a mesh: seq: 8 (over y, x, core), head: 4 (over z).
Axes of the slice: x: 2, y: 2, z: 4, core: 2. Of those that a mesh axis runs over, the one named last changes fastest.
Arguments:
- tokens: bfloat16 [8192, 2048], P('seq'), may hold values from -20 to 20
- cotangent: bfloat16 [8192, 2048], P('seq'), may hold values from -6 to 6
- seq_lengths: int32 [2], replicated, may hold values from 128 to 8064, as said below
- attn_master: float32 [4, 2048, 2048], P(None, 'seq', 'head'), may hold values from -0.5 to 0.5
- ffn_master: float32 [3, 2048, 8192], P(None, 'seq', 'head'), may hold values from -0.088388348 to 0.088388348
- gain_master: float32 [2, 2048], P(None, 'seq'), may hold values from 0.3 to 2.5
- attn_first: float32 [4, 2048, 2048], P(None, 'seq', 'head'), may hold values from -0.0017089844 to 0.0017089844
- attn_second: float32 [4, 2048, 2048], P(None, 'seq', 'head'), may hold values from 7.450126e-09 to 5.9601007e-08
- ffn_first: float32 [3, 2048, 8192], P(None, 'seq', 'head'), may hold values from -0.0017089844 to 0.0017089844
- ffn_second: float32 [3, 2048, 8192], P(None, 'seq', 'head'), may hold values from 7.450126e-10 to 5.960101e-09
- gain_first: float32 [2, 2048], P(None, 'seq'), may hold values from -0.0048828125 to 0.0048828125
- gain_second: float32 [2, 2048], P(None, 'seq'), may hold values from 6.705113e-08 to 5.3640906e-07
Outputs:
- layer_output: float32 [8192, 2048], P('seq')
- input_grad: float32 [8192, 2048], P('seq')
- attn_mass: float32 [16, 8192], P('head', 'seq')
- grad_norm: float32 [], replicated
- attn_grad: float32 [4, 2048, 2048], P(None, 'seq', 'head')
- attn_first_new: float32 [4, 2048, 2048], P(None, 'seq', 'head')
- attn_second_new: float32 [4, 2048, 2048], P(None, 'seq', 'head')
- attn_new: float32 [4, 2048, 2048], P(None, 'seq', 'head')
- attn_low: bfloat16 [4, 2048, 2048], P(None, 'seq', 'head')
- ffn_grad: float32 [3, 2048, 8192], P(None, 'seq', 'head')
- ffn_first_new: float32 [3, 2048, 8192], P(None, 'seq', 'head')
- ffn_second_new: float32 [3, 2048, 8192], P(None, 'seq', 'head')
- ffn_new: float32 [3, 2048, 8192], P(None, 'seq', 'head')
- ffn_low: bfloat16 [3, 2048, 8192], P(None, 'seq', 'head')
- gain_grad: float32 [2, 2048], P(None, 'seq')
- gain_first_new: float32 [2, 2048], P(None, 'seq')
- gain_second_new: float32 [2, 2048], P(None, 'seq')
- gain_new: float32 [2, 2048], P(None, 'seq')
- gain_low: bfloat16 [2, 2048], P(None, 'seq')
Inputs may be any that keep to these rules, and one draw needn't show every extreme that they name: `seq_lengths`: two sequences that together hold all 8192 tokens: one has 128 to 1023 tokens and the other the rest; which of the two comes first varies.
All inputs are finite; a program needn't handle non-finite values.
Results may differ from a plain program's by a relative error of at most 0.024.
Values may be sent and summed in bfloat16 or wider, within the bound.
No kernel may reach another device: no remote copies, remote signals or barrier semaphores. Data moves between devices by JAX's collectives and lax.ppermute only.
A program may use at most 320 MiB of HBM per device.

v0:
```python
import math

import jax
import jax.numpy as jnp
from jax import lax
from jax.sharding import PartitionSpec as P

HD = 128
STEP = 10


EPS = 1e-05
CLIP = 1.0
BETA1 = 0.5
BETA2 = 0.5
RATE = 0.03
GAIN_RATE = 0.3
DECAY = 0.1
ADAM_EPS = 1e-08


def sequence_info(seq_lengths, row_count):
    seq_ends = jnp.cumsum(seq_lengths, dtype=jnp.int32)
    seq_starts = seq_ends - seq_lengths
    places = jnp.arange(row_count, dtype=jnp.int32)[:, None]
    seq_first = jnp.sum(
        jnp.where(seq_ends[None, :] <= places, seq_lengths[None, :], 0), axis=1, dtype=jnp.int32
    )
    inside = (seq_starts[None, :] <= places) & (places < seq_ends[None, :])
    seq_len = jnp.sum(jnp.where(inside, seq_lengths[None, :], 0), axis=1, dtype=jnp.int32)
    return (seq_first, seq_len)


def sigmoid_weights(
    query_block, key_block, query_place, query_first, query_bias, key_place, factor
):
    raw = (
        jnp.einsum("rhc,shc->hrs", query_block, key_block, preferred_element_type=jnp.float32)
        * factor
    )
    allowed = (key_place[None, :] >= query_first[:, None]) & (
        key_place[None, :] <= query_place[:, None]
    )
    return jnp.where(allowed[None], jax.nn.sigmoid(raw + query_bias[None, :, None]), 0.0)


def adam_update(gradient, first_moment, second, master, step_rate):
    first_new = BETA1 * first_moment + (1.0 - BETA1) * gradient
    second_new = BETA2 * second + (1.0 - BETA2) * gradient * gradient
    first_hat = first_new / (1.0 - BETA1**STEP)
    second_hat = second_new / (1.0 - BETA2**STEP)
    master_new = master - step_rate * (
        first_hat / (jnp.sqrt(second_hat) + ADAM_EPS) + DECAY * master
    )
    return (first_new, second_new, master_new, master_new.astype(jnp.bfloat16))


def per_device(
    tokens,
    cotangent,
    seq_lengths,
    attn_master,
    ffn_master,
    gain_master,
    attn_first,
    attn_second,
    ffn_first,
    ffn_second,
    gain_first,
    gain_second,
):
    seq_count = lax.axis_size("seq")
    seq_index = lax.axis_index("seq")
    head_index = lax.axis_index("head")
    local_rows = tokens.shape[0]
    total_rows = local_rows * seq_count
    head_width = attn_master.shape[2]
    local_heads = head_width // HD
    block_rows = min(1024, total_rows)
    blocks = total_rows // block_rows
    factor = 1.0 / math.sqrt(HD)
    attn_weight, ffn_weight, gain_weight = (
        lax.all_gather(attn_master.astype(jnp.bfloat16), "seq", axis=1, tiled=True),
        lax.all_gather(ffn_master.astype(jnp.bfloat16), "seq", axis=1, tiled=True),
        lax.all_gather(gain_master.astype(jnp.bfloat16), "seq", axis=1, tiled=True),
    )
    gain_values = gain_weight.astype(jnp.float32)
    seq_first, seq_len = sequence_info(seq_lengths, total_rows)
    seq_bias = -jnp.log(seq_len.astype(jnp.float32))
    row_start = seq_index * local_rows
    own_place = row_start + jnp.arange(local_rows, dtype=jnp.int32)
    residual = tokens.astype(jnp.float32)
    scale_one = lax.rsqrt(jnp.mean(residual * residual, axis=-1, keepdims=True) + EPS)
    unit_one = residual * scale_one
    normed_one = (unit_one * gain_values[0]).astype(jnp.bfloat16)
    projected = jnp.einsum(
        "td,sdc->stc", normed_one, attn_weight[:3], preferred_element_type=jnp.float32
    ).astype(jnp.bfloat16)
    queries = projected[0]
    key_heads = projected[1].reshape(local_rows, local_heads, HD)
    value_heads = projected[2].reshape(local_rows, local_heads, HD)
    all_queries = lax.all_gather(queries, "seq", axis=0, tiled=True)

    def forward_block(block_index):
        block_start = block_index * block_rows
        query_block = lax.dynamic_slice_in_dim(all_queries, block_start, block_rows, 0).reshape(
            block_rows, local_heads, HD
        )
        query_place = block_start + jnp.arange(block_rows, dtype=jnp.int32)
        weights = sigmoid_weights(
            query_block,
            key_heads,
            query_place,
            lax.dynamic_slice_in_dim(seq_first, block_start, block_rows),
            lax.dynamic_slice_in_dim(seq_bias, block_start, block_rows),
            own_place,
            factor,
        )
        mixed_part = jnp.einsum(
            "hrs,shc->hrc",
            weights.astype(jnp.bfloat16),
            value_heads,
            preferred_element_type=jnp.float32,
        )
        return (mixed_part, jnp.sum(weights, axis=2))

    mixed_span, mass_span = lax.map(forward_block, jnp.arange(blocks, dtype=jnp.int32))
    mixed_all = mixed_span.transpose(1, 0, 2, 3).reshape(local_heads, total_rows, HD)
    mass_all = mass_span.transpose(1, 0, 2).reshape(local_heads, total_rows)
    head_out, attn_mass = (
        lax.psum_scatter(mixed_all, "seq", scatter_dimension=1, tiled=True),
        lax.psum_scatter(mass_all, "seq", scatter_dimension=1, tiled=True),
    )
    attn_heads = head_out.transpose(1, 0, 2).reshape(local_rows, head_width).astype(jnp.bfloat16)
    attn_part = lax.dot_general(
        attn_heads, attn_weight[3], (((1,), (1,)), ((), ())), preferred_element_type=jnp.float32
    )
    attn_sum = lax.psum(attn_part, "head")
    resid_one = residual + attn_sum
    scale_two = lax.rsqrt(jnp.mean(resid_one * resid_one, axis=-1, keepdims=True) + EPS)
    unit_two = resid_one * scale_two
    normed_two = (unit_two * gain_values[1]).astype(jnp.bfloat16)
    gate_up = jnp.einsum(
        "td,sdf->stf", normed_two, ffn_weight[:2], preferred_element_type=jnp.float32
    )
    gate_value = gate_up[0]
    up_value = gate_up[1]
    gate_sigmoid = jax.nn.sigmoid(gate_value)
    gate_silu = gate_value * gate_sigmoid
    hidden = (gate_silu * up_value).astype(jnp.bfloat16)
    ffn_part = lax.dot_general(
        hidden, ffn_weight[2], (((1,), (1,)), ((), ())), preferred_element_type=jnp.float32
    )
    ffn_sum = lax.psum(ffn_part.astype(jnp.bfloat16), "head").astype(jnp.float32)
    layer_output = resid_one + ffn_sum
    out_grad = cotangent.astype(jnp.float32)
    hidden_grad = jnp.dot(cotangent, ffn_weight[2], preferred_element_type=jnp.float32)
    down_wgrad = lax.dot_general(
        cotangent, hidden, (((0,), (0,)), ((), ())), preferred_element_type=jnp.float32
    )
    gate_grad = (
        hidden_grad * up_value * (gate_sigmoid + gate_value * gate_sigmoid * (1.0 - gate_sigmoid))
    )
    up_grad = hidden_grad * gate_silu
    gate_up_grad = jnp.stack([gate_grad, up_grad]).astype(jnp.bfloat16)
    two_grad_part = jnp.einsum(
        "stf,sdf->td", gate_up_grad, ffn_weight[:2], preferred_element_type=jnp.float32
    )
    gate_up_wgrad = jnp.einsum(
        "td,stf->sdf", normed_two, gate_up_grad, preferred_element_type=jnp.float32
    )
    normed_two_grad = lax.psum(two_grad_part, "head")
    gain_two_grad = jnp.sum(normed_two_grad * unit_two, axis=0)
    unit_grad_two = normed_two_grad * gain_values[1]
    resid_grad = out_grad + scale_two * (
        unit_grad_two - unit_two * jnp.mean(unit_grad_two * unit_two, axis=-1, keepdims=True)
    )
    branch_low = resid_grad.astype(jnp.bfloat16)
    heads_grad = jnp.dot(branch_low, attn_weight[3], preferred_element_type=jnp.float32).astype(
        jnp.bfloat16
    )
    out_wgrad = lax.dot_general(
        branch_low, attn_heads, (((0,), (0,)), ((), ())), preferred_element_type=jnp.float32
    )
    grad_all, query_again = (
        lax.all_gather(heads_grad, "seq", axis=0, tiled=True),
        lax.all_gather(queries, "seq", axis=0, tiled=True),
    )

    def backward_block(running, block_index):
        block_start = block_index * block_rows
        query_block = lax.dynamic_slice_in_dim(query_again, block_start, block_rows, 0).reshape(
            block_rows, local_heads, HD
        )
        grad_block = lax.dynamic_slice_in_dim(grad_all, block_start, block_rows, 0).reshape(
            block_rows, local_heads, HD
        )
        query_place = block_start + jnp.arange(block_rows, dtype=jnp.int32)
        weights = sigmoid_weights(
            query_block,
            key_heads,
            query_place,
            lax.dynamic_slice_in_dim(seq_first, block_start, block_rows),
            lax.dynamic_slice_in_dim(seq_bias, block_start, block_rows),
            own_place,
            factor,
        )
        weight_grad = jnp.einsum(
            "rhc,shc->hrs", grad_block, value_heads, preferred_element_type=jnp.float32
        )
        score_grad = (weight_grad * weights * (1.0 - weights)).astype(jnp.bfloat16)
        query_part = (
            jnp.einsum("hrs,shc->rhc", score_grad, key_heads, preferred_element_type=jnp.float32)
            * factor
        )
        key_part = (
            jnp.einsum("hrs,rhc->shc", score_grad, query_block, preferred_element_type=jnp.float32)
            * factor
        )
        value_part = jnp.einsum(
            "hrs,rhc->shc",
            weights.astype(jnp.bfloat16),
            grad_block,
            preferred_element_type=jnp.float32,
        )
        return (
            (running[0] + key_part, running[1] + value_part),
            query_part.reshape(block_rows, head_width),
        )

    start_sums = (
        jnp.zeros((local_rows, local_heads, HD), jnp.float32),
        jnp.zeros((local_rows, local_heads, HD), jnp.float32),
    )
    (key_sum, value_sum), query_parts = lax.scan(
        backward_block, start_sums, jnp.arange(blocks, dtype=jnp.int32)
    )
    query_full = query_parts.reshape(total_rows, head_width)
    query_grad = lax.psum_scatter(
        query_full.astype(jnp.bfloat16), "seq", scatter_dimension=0, tiled=True
    ).astype(jnp.float32)
    key_grad = key_sum.reshape(local_rows, head_width)
    value_grad = value_sum.reshape(local_rows, head_width)
    qkv_grad = jnp.stack([query_grad, key_grad, value_grad]).astype(jnp.bfloat16)
    one_grad_part = jnp.einsum(
        "stc,sdc->td", qkv_grad, attn_weight[:3], preferred_element_type=jnp.float32
    )
    qkv_wgrad = jnp.einsum("td,stc->sdc", normed_one, qkv_grad, preferred_element_type=jnp.float32)
    normed_one_grad = lax.psum(one_grad_part.astype(jnp.bfloat16), "head").astype(jnp.float32)
    gain_one_grad = jnp.sum(normed_one_grad * unit_one, axis=0)
    unit_grad_one = normed_one_grad * gain_values[0]
    input_grad = resid_grad + scale_one * (
        unit_grad_one - unit_one * jnp.mean(unit_grad_one * unit_one, axis=-1, keepdims=True)
    )
    attn_raw = jnp.concatenate([qkv_wgrad, out_wgrad[None]], axis=0)
    ffn_raw = jnp.concatenate([gate_up_wgrad, down_wgrad[None]], axis=0)
    gain_raw = jnp.stack([gain_one_grad, gain_two_grad])
    attn_shard, ffn_shard, gain_shard = (
        lax.psum_scatter(
            attn_raw.astype(jnp.bfloat16), "seq", scatter_dimension=1, tiled=True
        ).astype(jnp.float32),
        lax.psum_scatter(
            ffn_raw.astype(jnp.bfloat16), "seq", scatter_dimension=1, tiled=True
        ).astype(jnp.float32),
        lax.psum_scatter(
            gain_raw.astype(jnp.bfloat16), "seq", scatter_dimension=1, tiled=True
        ).astype(jnp.float32),
    )
    squares = (
        jnp.sum(attn_shard * attn_shard)
        + jnp.sum(ffn_shard * ffn_shard)
        + jnp.where(head_index == 0, jnp.sum(gain_shard * gain_shard), 0.0)
    )
    square_sum = lax.psum(squares, ("seq", "head"))
    grad_norm = jnp.sqrt(square_sum)
    clip_factor = jnp.minimum(1.0, CLIP / (grad_norm + 1e-06))
    attn_grad = attn_shard * clip_factor
    ffn_grad = ffn_shard * clip_factor
    gain_grad = gain_shard * clip_factor
    attn_state = adam_update(attn_grad, attn_first, attn_second, attn_master, RATE)
    ffn_state = adam_update(ffn_grad, ffn_first, ffn_second, ffn_master, RATE)
    gain_state = adam_update(gain_grad, gain_first, gain_second, gain_master, GAIN_RATE)
    return (
        layer_output,
        input_grad,
        attn_mass,
        grad_norm,
        attn_grad,
        attn_state[0],
        attn_state[1],
        attn_state[2],
        attn_state[3],
        ffn_grad,
        ffn_state[0],
        ffn_state[1],
        ffn_state[2],
        ffn_state[3],
        gain_grad,
        gain_state[0],
        gain_state[1],
        gain_state[2],
        gain_state[3],
    )


def solution(mesh):
    in_specs = (
        P("seq", None),
        P("seq", None),
        P(),
        P(None, "seq", "head"),
        P(None, "seq", "head"),
        P(None, "seq"),
        P(None, "seq", "head"),
        P(None, "seq", "head"),
        P(None, "seq", "head"),
        P(None, "seq", "head"),
        P(None, "seq"),
        P(None, "seq"),
    )
    out_specs = (
        P("seq", None),
        P("seq", None),
        P("head", "seq"),
        P(),
        P(None, "seq", "head"),
        P(None, "seq", "head"),
        P(None, "seq", "head"),
        P(None, "seq", "head"),
        P(None, "seq", "head"),
        P(None, "seq", "head"),
        P(None, "seq", "head"),
        P(None, "seq", "head"),
        P(None, "seq", "head"),
        P(None, "seq", "head"),
        P(None, "seq"),
        P(None, "seq"),
        P(None, "seq"),
        P(None, "seq"),
        P(None, "seq"),
    )
    return jax.shard_map(
        per_device, mesh=mesh, in_specs=in_specs, out_specs=out_specs, check_vma=False
    )
```

profile of v0, /device:TPU:8, one launch (start us, length us, event | category | flops | bytes accessed | tf_op | source)
XLA Modules:
  0.0 2444.5 jit_solution(3726297652250013185)
XLA Ops:
  23.4 44.3 %all-gather.6.cloned.1.call-done = bf16[4,2048,512]{1,2,0:T(8,128)(2,1)} async-done(((bf16[4,256,512]{1,2,0:T(8,128)(2,1)}), bf16[4,2048,512]{1,2,0:T(8,128)(2,1)}) %all-gather.6.cloned.1.call-update) | async-done | bytes 8388624 | tf_op jit(solution)/shard_map/all_gather | solution.py:83
  82.5 51.6 %all-gather.12.cloned.1.call-done = bf16[1,8192,512]{1,2,0:T(8,128)(2,1)} async-done(((bf16[1,1024,512]{1,2,0:T(8,128)(2,1)}), bf16[1,8192,512]{1,2,0:T(8,128)(2,1)}) %all-gather.12.cloned.1.call-update) | async-done | bytes 8388624 | tf_op jit(solution)/shard_map/all_gather | solution.py:102
  134.2 122.3 %while.28 = (s32[]{:T(128)}, f32[8,4,1024,128]{3,2,0,1:T(8,128)}, f32[8,4,1024]{2,1,0:T(4,128)}, s32[8]{0:T(128)S(1)}, s32[8192]{0:T(1024)S(1)}, /*index=5*/bf16...) while((s32[]{:T(128)}, f32[8,4,1024,128]{3,2,0,1:T(8,128)}, ...), condition=%wide.region_6.7_spmd.clone, body=%wide.region_4.6_spmd.clone.sunk | while | flops 2184181760 | bytes 26304740 | solution.py:127
  256.8 115.8 %reduce-scatter.11.cloned.1.call-done = f32[4,1024,128]{2,1,0:T(8,128)} async-done(((f32[4,8192,128]{2,1,0:T(8,128)}), f32[4,1024,128]{2,1,0:T(8,128)}) %reduce-scatter.11.cloned.1.call-update) | async-done | bytes 2097168 | tf_op jit(solution)/shard_map/reduce_scatter | solution.py:131
  387.7 283.7 %all-reduce.5.cloned.1.call-done = f32[1024,2048]{1,0:T(8,128)} async-done(((f32[1024,2048]{1,0:T(8,128)}), f32[1024,2048]{1,0:T(8,128)}) %all-reduce.5.cloned.1.call-update) | async-done | bytes 8388624 | tf_op jit(solution)/shard_map/psum | solution.py:138
  680.5 119.8 %all-gather.8.cloned.1.call-done = bf16[3,2048,2048]{2,1,0:T(8,128)(2,1)} async-done(((bf16[3,256,2048]{2,1,0:T(8,128)(2,1)}), bf16[3,2048,2048]{2,1,0:T(8,128)(2,1)}) %all-gather.8.cloned.1.call-update) | async-done | bytes 25165840 | tf_op jit(solution)/shard_map/all_gather | solution.py:84
  800.3 25.1 %fusion.35 = f32[2,1024,2048]{2,1,0:T(8,128)} fusion(bf16[3,2048,2048]{2,1,0:T(8,128)(2,1)} %all-gather.8.cloned.1.call-done, f32[1024,2048]{1,0:T(8,128)} %get-tuple-element.436, f32[2048]{0:T(1024)S(1)} %bitcast.214, f32[1024]{0:T(1024)S(1)} %add_rsqrt_fusion), kind=kOutput, calls=%fused_computation.74 | convolution fusion | flops 17186160640 | bytes 41955328 | tf_op jit(solution)/shard_map/td,sdf->stf/dot_general | solution.py:143
  825.5 18.8 fusion.50
  844.3 24.1 fusion.44
  868.5 288.8 %all-reduce.7.cloned.1.call-done = f32[1024,2048]{1,0:T(8,128)} async-done(((f32[1024,2048]{1,0:T(8,128)}), f32[1024,2048]{1,0:T(8,128)}) %all-reduce.7.cloned.1.call-update) | async-done | bytes 8388624 | tf_op jit(solution)/shard_map/psum | solution.py:172
  1157.2 18.2 multiply_reduce_fusion
  1188.5 55.6 %all-gather.10.cloned.1.call-done = bf16[8192,512]{1,0:T(8,128)(2,1)} async-done(((bf16[1024,512]{1,0:T(8,128)(2,1)}), bf16[8192,512]{1,0:T(8,128)(2,1)}) %all-gather.10.cloned.1.call-update) | async-done | bytes 8388624 | tf_op jit(solution)/shard_map/all_gather | solution.py:186
  1244.1 355.0 %while.29 = (s32[]{:T(128)}, f32[1024,4,128]{0,2,1:T(8,128)}, f32[1024,4,128]{0,2,1:T(8,128)}, bf16[8,1024,512]{1,2,0:T(8,128)(2,1)}, s32[8]{0:T(128)S(1)}, /*in...) while((s32[]{:T(128)}, f32[1024,4,128]{0,2,1:T(8,128)}, ...), condition=%wide.region_14.15_spmd.clone, body=%wide.region_13.14_spmd.clone.sunk | while | flops 5421664256 | bytes 157327824 | solution.py:235
  1248.0 10.4 divide_select_fusion.3
  1336.3 10.4 divide_select_fusion.3
  1425.2 10.4 divide_select_fusion.3
  1469.6 10.4 divide_select_fusion.3
  1514.1 10.4 divide_select_fusion.3
  1599.1 11.4 copy.155
  1610.7 17.4 fusion.55
  1631.4 50.6 %reduce-scatter.13.cloned.1.call-done = bf16[1024,512]{1,0:T(8,128)(2,1)} async-done(((bf16[8192,512]{1,0:T(8,128)(2,1)}), bf16[1024,512]{1,0:T(8,128)(2,1)}) %reduce-scatter.13.cloned.1.call-update) | async-done | bytes 1048592 | tf_op jit(solution)/shard_map/reduce_scatter | solution.py:239
  1696.0 16.9 convert_bitcast_fusion.1
  1712.9 26.6 %convert_bitcast_fusion = bf16[2,2048,2048]{1,2,0:T(8,128)(2,1)} fusion(bf16[1,1024,2048]{2,1,0:T(8,128)(2,1)} %get-tuple-element.444, bf16[1,1024,2048]{2,1,0:T(8,128)(2,1)} %get-tuple-element.443, f32[1024,2048]{1,0:T(8,128)} %get-tuple-element.436, f32[2048]{0:T(1024)S(1)} %bitcast.217, f32[1024]{0:T(1024)S(1)} %copy-done.30), kind=kOutput, calls=%fused_computation.25 | convolution fusion | flops 17198743552 | bytes 33566720 | tf_op jit(solution)/shard_map/td,stf->sdf/dot_general | solution.py:169
  1739.5 21.0 pad_maximum_fusion
  1777.8 204.2 %all-reduce.9.cloned.1.call-done = (bf16[1024,2048]{1,0:T(8,128)(2,1)}, bf16[1024,2048]{1,0:T(8,128)(2,1)}) async-done(((bf16[1024,2048]{1,0:T(8,128)(2,1)}, bf16[1024,2048]{1,0:T(8,128)(2,1)}), (bf16[1024,2048]{1,0:T(8,128)(2,1)}, bf16[1024,2048]{1,0:T(8,128)(2,1)})) %all-reduce.9.cloned.1.call-update) | async-done | bytes 8388624 | tf_op jit(solution)/shard_map/psum | solution.py:154
  2020.2 17.8 reduce-scatter.19.cloned.1.call-done
  2039.9 158.7 %reduce-scatter.17.cloned.1.call-done = bf16[3,256,2048]{1,2,0:T(8,128)(2,1)} async-done(((bf16[3,2048,2048]{1,2,0:T(8,128)(2,1)}), bf16[3,256,2048]{1,2,0:T(8,128)(2,1)}) %reduce-scatter.17.cloned.1.call-update) | async-done | bytes 3145744 | tf_op jit(solution)/shard_map/reduce_scatter | solution.py:262
  2202.7 33.5 %reduce-scatter.21.cloned.1.call-done = bf16[256,2]{1,0:T(8,128)(2,1)} async-done(((bf16[2048,2]{1,0:T(8,128)(2,1)}), bf16[256,2]{1,0:T(8,128)(2,1)}) %reduce-scatter.21.cloned.1.call-update) | async-done | bytes 1040
  2238.4 73.0 %reduce-scatter.15.cloned.1.call-done = bf16[4,256,512]{1,2,0:T(8,128)(2,1)} async-done(((bf16[4,2048,512]{1,2,0:T(8,128)(2,1)}), bf16[4,256,512]{1,2,0:T(8,128)(2,1)}) %reduce-scatter.15.cloned.1.call-update) | async-done | bytes 1048592 | tf_op jit(solution)/shard_map/reduce_scatter | solution.py:259
  2315.1 17.0 fusion.22
  2332.0 39.5 %psum.39 = f32[]{:T(128)} all-reduce(f32[]{:T(128)S(6)} %add.196), channel_id=1, replica_groups=mesh['seq'=8,'head'=4] {'seq','head'}, use_global_device_ids=true, to_apply=%region_27.28 | all-reduce | flops 1 | bytes 8 | tf_op jit(solution)/shard_map/psum | solution.py:274
  2391.0 15.2 fusion.86
  (463 shorter events, 613.3 us)
Async XLA Ops:
  7.2 60.5 %all-gather.6.cloned.1.call-start = ((), (), s32[]{:S(2)}) async-start(), calls=%async_computation.6 | async-start | bytes 9437184 | tf_op jit(solution)/shard_map/all_gather | solution.py:83
  9.2 68.8 %copy-start.8 = (f32[4,256,512]{1,2,0:T(8,128)}, f32[4,256,512]{1,2,0:T(8,128)S(1)}, u32[]{:S(2)}) copy-start(f32[4,256,512]{1,2,0:T(8,128)S(1)} %copy.148) | copy-start | bytes 6291460
  10.4 123.8 %all-gather.12.cloned.1.call-start = ((), (), s32[]{:S(2)}) async-start(), calls=%async_computation.15 | async-start | bytes 9437184 | tf_op jit(solution)/shard_map/all_gather | solution.py:102
  22.7 44.9 %copy-start.31 = (f32[1024]{0:T(1024)}, f32[1024]{0:T(1024)S(1)}, u32[]{:S(2)}) copy-start(f32[1024]{0:T(1024)S(1)} %add_rsqrt_fusion.1) | copy-start | bytes 12292
  23.4 44.3 %copy-start.27 = (f32[1,2048]{1,0:T(1,128)}, f32[1,2048]{1,0:T(1,128)S(1)}, u32[]{:S(2)}) copy-start(f32[1,2048]{1,0:T(1,128)S(1)} %get-tuple-element.451) | copy-start | bytes 24580
  79.6 54.6 %copy-start.15 = (bf16[1,1024,512]{1,2,0:T(8,128)(2,1)}, bf16[1,1024,512]{1,2,0:T(8,128)(2,1)S(1)}, u32[]{:S(2)}) copy-start(bf16[1,1024,512]{1,2,0:T(8,128)(2,1)S(1)} %get-tuple-element.447) | copy-start | bytes 3145732
  79.6 293.0 %reduce-scatter.11.cloned.1.call-start = ((), (), s32[]{:S(2)}) async-start(), calls=%async_computation.7 | async-start | bytes 18874368 | tf_op jit(solution)/shard_map/reduce_scatter | solution.py:131
  256.5 415.0 %all-reduce.5.cloned.1.call-start = ((), (), s32[]{:S(2)}) async-start(), calls=%async_computation.8 | async-start | bytes 16777216 | tf_op jit(solution)/shard_map/psum | solution.py:138
  382.7 417.7 %all-gather.8.cloned.1.call-start = ((), (), s32[]{:S(2)}) async-start(), calls=%async_computation.9 | async-start | bytes 28311552 | tf_op jit(solution)/shard_map/all_gather | solution.py:84
  387.7 412.7 %copy-start.25 = (f32[1,2048]{1,0:T(1,128)S(1)}, f32[1,2048]{1,0:T(1,128)}, u32[]{:S(2)}) copy-start(f32[1,2048]{1,0:T(1,128)} %get-tuple-element.450) | copy-start | bytes 24580
  387.7 769.6 %all-reduce.7.cloned.1.call-start = ((), (), s32[]{:S(2)}) async-start(), calls=%async_computation.10 | async-start | bytes 16777216 | tf_op jit(solution)/shard_map/psum | solution.py:172
  680.5 494.9 %copy-start.29 = (f32[1024]{0:T(1024)}, f32[1024]{0:T(1024)S(1)}, u32[]{:S(2)}) copy-start(f32[1024]{0:T(1024)S(1)} %add_rsqrt_fusion) | copy-start | bytes 12292
  800.3 25.1 %copy-start.11 = (bf16[1024,2048]{1,0:T(8,128)(2,1)S(1)}, bf16[1024,2048]{1,0:T(8,128)(2,1)}, u32[]{:S(2)}) copy-start(bf16[1024,2048]{1,0:T(8,128)(2,1)} %param.17) | copy-start | bytes 12582916
  868.4 375.7 %all-gather.10.cloned.1.call-start = ((), (), s32[]{:S(2)}) async-start(), calls=%async_computation.11 | async-start | bytes 9437184 | tf_op jit(solution)/shard_map/all_gather | solution.py:186
  1157.2 18.2 copy-start.6
  1157.2 18.2 copy-start.12
  1188.4 493.6 %reduce-scatter.13.cloned.1.call-start = ((), (), s32[]{:S(2)}) async-start(), calls=%async_computation.12 | async-start | bytes 9437184 | tf_op jit(solution)/shard_map/reduce_scatter | solution.py:239
  1313.7 14.6 slice-start
  1358.2 14.6 slice-start
  1402.6 14.6 slice-start
  1610.6 17.4 copy-start.4
  1610.6 371.3 %all-reduce.9.cloned.1.call-start = ((), (), s32[]{:S(2)}) async-start(), calls=%async_computation.18 | async-start | bytes 16777216 | tf_op jit(solution)/shard_map/psum | solution.py:154
  1628.7 63.7 %copy-start.20 = (bf16[1,1024,512]{2,1,0:T(8,128)(2,1)}, bf16[1,1024,512]{2,1,0:T(8,128)(2,1)S(1)}, u32[]{:S(2)}) copy-start(bf16[1,1024,512]{2,1,0:T(8,128)(2,1)S(1)} %copy.191) | copy-start | bytes 3145732
  1631.4 61.0 %copy-start.22 = (bf16[1,1024,512]{2,1,0:T(8,128)(2,1)}, bf16[1,1024,512]{2,1,0:T(8,128)(2,1)S(1)}, u32[]{:S(2)}) copy-start(bf16[1,1024,512]{2,1,0:T(8,128)(2,1)S(1)} %copy.190) | copy-start | bytes 3145732
  1692.4 345.6 %reduce-scatter.19.cloned.1.call-start = ((), (), s32[]{:S(2)}) async-start(), calls=%async_computation.16 | async-start | bytes 4718592
  1696.0 16.9 copy-start.26
  1696.0 16.9 copy-start.30
  1696.0 502.6 %reduce-scatter.17.cloned.1.call-start = ((), (), s32[]{:S(2)}) async-start(), calls=%async_computation.14 | async-start | bytes 28311552 | tf_op jit(solution)/shard_map/reduce_scatter | solution.py:262
  1760.5 475.7 %reduce-scatter.21.cloned.1.call-start = ((), (), s32[]{:S(2)}) async-start(), calls=%async_computation.17 | async-start | bytes 589824
  1988.0 323.3 %reduce-scatter.15.cloned.1.call-start = ((), (), s32[]{:S(2)}) async-start(), calls=%async_computation.13 | async-start | bytes 9437184 | tf_op jit(solution)/shard_map/reduce_scatter | solution.py:259
  2315.0 57.2 %copy-start.9 = (f32[4,256,512]{1,2,0:T(8,128)S(1)}, f32[4,256,512]{1,2,0:T(8,128)}, u32[]{:S(2)}) copy-start(f32[4,256,512]{1,2,0:T(8,128)} %copy-done.8) | copy-start | bytes 6291460
  2315.1 57.2 %copy-start.13 = (bf16[4,256,512]{1,2,0:T(8,128)(2,1)S(1)}, bf16[4,256,512]{1,2,0:T(8,128)(2,1)}, u32[]{:S(2)}) copy-start(bf16[4,256,512]{1,2,0:T(8,128)(2,1)} %reduce-scatter.15.cloned.1.call-done) | copy-start | bytes 3145732
  (72 other events, 562.5 us)
Sparse Core Ops, SparseCore 0:
  10.5 57.1 all-gather.5
  79.7 54.3 all-gather.11
  256.6 115.9 reduce-scatter.10
  382.8 288.6 all-reduce.4
  673.8 126.4 all-gather.7
  868.6 288.6 all-reduce.6
  1188.5 55.5 all-gather.9
  1610.7 71.2 reduce-scatter.12
  1692.5 289.3 all-reduce.8
  1985.5 52.4 reduce-scatter.18
  2041.6 156.8 reduce-scatter.16
  2202.1 34.1 reduce-scatter.20
  2240.1 71.2 reduce-scatter.14
where the time goes:
time: 2460 us; the launch traced here: 2440 us
  waiting for transfers between devices  1500 us (61%)
  matrix products  568 us (23%)
  local copies, waits for them, and re-layouts  157 us (6%)
  other arithmetic  142 us (6%)
  blocking collectives  48.4 us (2%)
    psum x1, waiting for transfers between devices, per_device(): normed_two_grad = lax.psum(two_grad_part, 'head')  289 us
    psum x1, waiting for transfers between devices, per_device(): attn_sum = lax.psum(attn_part, 'head')  284 us
    psum x1, waiting for transfers between devices, per_device(): lax.psum(ffn_part.astype(jnp.bfloat16), 'head').astype(jnp.float32)  204 us
    reduce_scatter x1, waiting for transfers between devices, per_device(): lax.psum_scatter(ffn_raw.astype(jnp.bfloat16), 'seq', scatter_dimension=1...  159 us
    dot_general x16, matrix products, sigmoid_weights(): jnp.einsum('rhc,shc->hrs', query_block, key_block, preferred_element_type...  138 us
    all_gather x1, waiting for transfers between devices, per_device(): lax.all_gather(ffn_master.astype(jnp.bfloat16), 'seq', axis=1, tiled=True)  120 us
    reduce_scatter x1, waiting for transfers between devices, per_device(): lax.psum_scatter(mixed_all, 'seq', scatter_dimension=1, tiled=True)  116 us
    unnamed x92, local copies, waits for them, and re-layouts  82.6 us
  transfers between devices with their start and end apart: 13, of which 13 were waited for; matrix products, arithmetic and copies ran while one was open for 7% of the time, Pallas kernels for 0%

commit v1 on v0

v1 whole, which is shorter than its diff:
```python
import functools
import math

import jax
import jax.numpy as jnp
from jax import lax
from jax.experimental import pallas as pl
from jax.experimental.pallas import tpu as pltpu
from jax.sharding import PartitionSpec as P

HD = 128
STEP = 10


EPS = 1e-05
CLIP = 1.0
BETA1 = 0.5
BETA2 = 0.5
RATE = 0.03
GAIN_RATE = 0.3
DECAY = 0.1
ADAM_EPS = 1e-08

LOW = jnp.bfloat16
WIDE = jnp.float32
QUERY_FACTOR = -math.log2(math.e) / math.sqrt(HD)
FAR = 30000.0

NN = (((1,), (0,)), ((), ()))
NT = (((1,), (1,)), ((), ()))
TN = (((0,), (0,)), ((), ()))


def dot(left, right, dims=NN):
    return lax.dot_general(left, right, dims, preferred_element_type=WIDE)


def fill_key_columns(key_buf, total_rows, cut):
    rows = 1024

    def step(at, _):
        place = at * rows + lax.broadcasted_iota(jnp.int32, (rows, HD), 0)
        lane = lax.broadcasted_iota(jnp.int32, (rows, HD), 1)
        extra = jnp.where(lane < 3, 1.0, jnp.where((lane == 3) & (place < cut), FAR, 0.0))
        key_buf[pl.ds(pl.multiple_of(at * rows, rows), rows), HD:] = extra.astype(LOW)
        return 0

    lax.fori_loop(0, total_rows // rows, step, 0)


def query_columns(block, start, cut, floats):
    place = start + lax.broadcasted_iota(jnp.int32, (block, HD), 0)
    lane = lax.broadcasted_iota(jnp.int32, (block, HD), 1)
    second = place >= cut

    def part(at):
        return jnp.where(second, floats[3 + at], floats[at])

    extra = jnp.where(
        lane == 0,
        part(0),
        jnp.where(
            lane == 1,
            part(1),
            jnp.where(lane == 2, part(2), jnp.where((lane == 3) & second, 1.0, 0.0)),
        ),
    )
    return extra.astype(LOW)


def key_copies(count, parts, block, part, key_values, key_buf, value_buf, sem):
    for other in range(parts):
        for at in range(count):
            row = pl.multiple_of((at * parts + (part ^ other)) * block, block)
            yield pltpu.make_async_copy(
                key_values[other].at[at, :, 0:HD], key_buf.at[pl.ds(row, block), 0:HD], sem.at[0]
            )
            yield pltpu.make_async_copy(
                key_values[other].at[at, :, HD:], value_buf.at[pl.ds(row, block), 0:HD], sem.at[0]
            )


def forward_kernel(count, parts, block, tile, ints, floats, q_ref, *rest):
    key_values = rest[:parts]
    out_ref, mass_ref, key_buf, value_buf, query_buf, total, sem = rest[parts:]
    total_rows = count * parts * block
    step = pl.program_id(0)
    cut, part = ints[0], ints[1]

    @pl.when(step == 0)
    def _():
        for copy in key_copies(count, parts, block, part, key_values, key_buf, value_buf, sem):
            copy.start()
        fill_key_columns(key_buf, total_rows, cut)
        value_buf[:, HD:] = jnp.ones((total_rows, HD), LOW)
        for copy in key_copies(count, parts, block, part, key_values, key_buf, value_buf, sem):
            copy.wait()

    start = (step * parts + part) * block
    query_buf[:, :HD] = q_ref[...]
    query_buf[:, HD:] = query_columns(block, start, cut, floats)
    total[...] = jnp.zeros_like(total)
    first = jnp.where(start >= cut, cut // tile, 0)
    last = (start + block - 1) // tile

    def walk(at, masked):
        keys = pl.ds(pl.multiple_of(at * tile, tile), tile)
        exponent = dot(query_buf[...], key_buf[keys, :], NT)
        weight = pl.reciprocal(1.0 + jnp.exp2(exponent), approx=True)
        if masked:
            query_place = start + lax.broadcasted_iota(jnp.int32, (block, tile), 0)
            key_place = at * tile + lax.broadcasted_iota(jnp.int32, (block, tile), 1)
            weight = jnp.where(key_place <= query_place, weight, 0.0)
        total[...] += dot(weight.astype(LOW), value_buf[keys, :])

    def body(at, carry):
        walk(at, False)
        return carry

    lax.fori_loop(first, last, body, 0)
    walk(last, True)
    out_ref[...] = total[:, :HD].astype(LOW)
    mass_ref[...] = jnp.transpose(total[:, HD:])[0:1, :]


def attention_forward(ints, floats, queries, key_values):
    count, block, _ = queries.shape
    parts = len(key_values)
    total_rows = count * parts * block
    tile = 1024
    pairs = total_rows * total_rows // (2 * parts)
    return pl.pallas_call(
        functools.partial(forward_kernel, count, parts, block, tile),
        out_shape=[
            jax.ShapeDtypeStruct((count, block, HD), LOW),
            jax.ShapeDtypeStruct((count, 1, block), WIDE),
        ],
        grid_spec=pltpu.PrefetchScalarGridSpec(
            num_scalar_prefetch=2,
            grid=(count,),
            in_specs=[pl.BlockSpec((None, block, HD), lambda i, *_: (i, 0, 0))]
            + [pl.BlockSpec(memory_space=pl.ANY)] * parts,
            out_specs=[
                pl.BlockSpec((None, block, HD), lambda i, *_: (i, 0, 0)),
                pl.BlockSpec((None, 1, block), lambda i, *_: (i, 0, 0)),
            ],
            scratch_shapes=[
                pltpu.VMEM((total_rows, 2 * HD), LOW),
                pltpu.VMEM((total_rows, 2 * HD), LOW),
                pltpu.VMEM((block, 2 * HD), LOW),
                pltpu.VMEM((block, 2 * HD), WIDE),
                pltpu.SemaphoreType.DMA((1,)),
            ],
        ),
        compiler_params=pltpu.CompilerParams(vmem_limit_bytes=48 * 2**20),
        cost_estimate=pl.CostEstimate(
            flops=pairs * 8 * HD, bytes_accessed=total_rows * HD * 8, transcendentals=2 * pairs
        ),
        name="attention_forward",
    )(ints, floats, queries, *key_values)


def backward_kernel(count, parts, block, tile, ints, floats, q_ref, grad_ref, *rest):
    key_values = rest[:parts]
    (q_grad_ref, kv_grad_ref, key_buf, value_buf, turned, query_buf, q_total, k_total, v_total, sem) = (
        rest[parts:]
    )
    total_rows = count * parts * block
    step = pl.program_id(0)
    cut, part = ints[0], ints[1]

    @pl.when(step == 0)
    def _():
        for copy in key_copies(count, parts, block, part, key_values, key_buf, value_buf, sem):
            copy.start()
        fill_key_columns(key_buf, total_rows, cut)
        k_total[...] = jnp.zeros_like(k_total)
        v_total[...] = jnp.zeros_like(v_total)
        for copy in key_copies(count, parts, block, part, key_values, key_buf, value_buf, sem):
            copy.wait()

        def turn(at, carry):
            keys = pl.ds(pl.multiple_of(at * tile, tile), tile)
            turned[:, keys] = jnp.transpose(key_buf[keys, :HD])
            return carry

        lax.fori_loop(0, total_rows // tile, turn, 0)

    start = (step * parts + part) * block
    query_buf[:, :HD] = q_ref[...]
    query_buf[:, HD:] = query_columns(block, start, cut, floats)
    q_total[...] = jnp.zeros_like(q_total)
    first = jnp.where(start >= cut, cut // tile, 0)
    last = (start + block - 1) // tile

    def walk(at, masked):
        keys = pl.ds(pl.multiple_of(at * tile, tile), tile)
        exponent = dot(key_buf[keys, :], query_buf[...], NT)
        weight = pl.reciprocal(1.0 + jnp.exp2(exponent), approx=True)
        if masked:
            key_place = at * tile + lax.broadcasted_iota(jnp.int32, (tile, block), 0)
            query_place = start + lax.broadcasted_iota(jnp.int32, (tile, block), 1)
            weight = jnp.where(key_place <= query_place, weight, 0.0)
        weight_grad = dot(value_buf[keys, :], grad_ref[...], NT)
        score_grad = (weight_grad * (weight * (1.0 - weight))).astype(LOW)
        v_total[keys, :] += dot(weight.astype(LOW), grad_ref[...])
        k_total[keys, :] += dot(score_grad, query_buf[:, :HD])
        q_total[...] += dot(turned[:, keys], score_grad)

    def body(at, carry):
        walk(at, False)
        return carry

    lax.fori_loop(first, last, body, 0)
    walk(last, True)
    q_grad_ref[...] = (jnp.transpose(q_total[...]) * (1.0 / math.sqrt(HD))).astype(LOW)

    @pl.when(step == count - 1)
    def _():
        for owner in range(parts):
            for at in range(count):
                rows = pl.ds((at * parts + owner) * block, block)
                kv_grad_ref[owner, at, :, :HD] = (k_total[rows, :] * (-math.log(2.0))).astype(LOW)
                kv_grad_ref[owner, at, :, HD:] = v_total[rows, :].astype(LOW)


def attention_backward(ints, floats, queries, grads, key_values):
    count, block, _ = queries.shape
    parts = len(key_values)
    total_rows = count * parts * block
    tile = 1024
    pairs = total_rows * total_rows // (2 * parts)
    return pl.pallas_call(
        functools.partial(backward_kernel, count, parts, block, tile),
        out_shape=[
            jax.ShapeDtypeStruct((count, block, HD), LOW),
            jax.ShapeDtypeStruct((parts, count, block, 2 * HD), LOW),
        ],
        grid_spec=pltpu.PrefetchScalarGridSpec(
            num_scalar_prefetch=2,
            grid=(count,),
            in_specs=[pl.BlockSpec((None, block, HD), lambda i, *_: (i, 0, 0))] * 2
            + [pl.BlockSpec(memory_space=pl.ANY)] * parts,
            out_specs=[
                pl.BlockSpec((None, block, HD), lambda i, *_: (i, 0, 0)),
                pl.BlockSpec((parts, count, block, 2 * HD), lambda i, *_: (0, 0, 0, 0)),
            ],
            scratch_shapes=[
                pltpu.VMEM((total_rows, 2 * HD), LOW),
                pltpu.VMEM((total_rows, HD), LOW),
                pltpu.VMEM((HD, total_rows), LOW),
                pltpu.VMEM((block, 2 * HD), LOW),
                pltpu.VMEM((HD, block), WIDE),
                pltpu.VMEM((total_rows, HD), WIDE),
                pltpu.VMEM((total_rows, HD), WIDE),
                pltpu.SemaphoreType.DMA((1,)),
            ],
        ),
        compiler_params=pltpu.CompilerParams(vmem_limit_bytes=60 * 2**20),
        cost_estimate=pl.CostEstimate(
            flops=pairs * 20 * HD, bytes_accessed=total_rows * HD * 16, transcendentals=2 * pairs
        ),
        name="attention_backward",
    )(ints, floats, queries, grads, *key_values)


def attention_scalars(seq_lengths, total_rows, part):
    cut = seq_lengths[0]
    length = jnp.log2(jnp.stack([cut, total_rows - cut]).astype(WIDE))
    high = lax.reduce_precision(length, 8, 7)
    middle = lax.reduce_precision(length - high, 8, 7)
    low = length - high - middle
    return (
        jnp.stack([cut, part]).astype(jnp.int32),
        jnp.stack([high, middle, low], axis=1).reshape(6),
    )


def line_sum(pieces):
    at = lax.axis_index("head")
    count = lax.axis_size("head")
    if count != 4:
        return lax.psum_scatter(
            jnp.stack(pieces), "head", scatter_dimension=0, tiled=False
        ).astype(WIDE)
    low_side = at < 2

    def from_end(step):
        return jnp.where(low_side, pieces[step], pieces[3 - step])

    inward = [(0, 1), (3, 2)]
    far = lax.ppermute(from_end(3), "head", inward)
    middle = lax.ppermute(from_end(2), "head", inward)
    near = lax.ppermute(from_end(1), "head", inward)
    outer = lax.ppermute(from_end(0), "head", [(1, 0), (2, 3)])
    far_sum = (far.astype(WIDE) + from_end(3).astype(WIDE)).astype(LOW)
    middle_sum = (middle.astype(WIDE) + from_end(2).astype(WIDE)).astype(LOW)
    far_in = lax.ppermute(far_sum, "head", [(1, 3), (2, 0)])
    middle_in = lax.ppermute(middle_sum, "head", [(1, 2), (2, 1)])
    at_end = (at == 0) | (at == 3)
    return jnp.where(
        at_end,
        from_end(0).astype(WIDE) + outer.astype(WIDE) + far_in.astype(WIDE),
        from_end(1).astype(WIDE) + near.astype(WIDE) + middle_in.astype(WIDE),
    )


def line_gather(piece):
    count = lax.axis_size("head")
    if count != 4:
        return lax.all_gather(piece, "head", axis=0, tiled=True)
    at = lax.axis_index("head")
    rows = piece.shape[0]
    left_one = lax.ppermute(piece, "head", [(0, 1), (1, 2), (2, 3)])
    right_one = lax.ppermute(piece, "head", [(3, 2), (2, 1), (1, 0)])
    left_two = lax.ppermute(piece, "head", [(0, 2), (1, 3)])
    right_two = lax.ppermute(piece, "head", [(3, 1), (2, 0)])
    left_three = lax.ppermute(left_two, "head", [(2, 3)])
    right_three = lax.ppermute(right_two, "head", [(1, 0)])
    full = jnp.zeros((count * rows,) + piece.shape[1:], piece.dtype)
    for step, part in (
        (-3, left_three),
        (-2, left_two),
        (-1, left_one),
        (3, right_three),
        (2, right_two),
        (1, right_one),
        (0, piece),
    ):
        full = lax.dynamic_update_slice_in_dim(
            full, part, jnp.clip(at + step, 0, count - 1) * rows, 0
        )
    return full


def group_exchange(blocks, parts):
    count = lax.axis_size("seq")
    return [blocks[0]] + [
        lax.ppermute(blocks[k], "seq", [(j, j ^ k) for j in range(count)]) for k in range(1, parts)
    ]


def adam_update(gradient, first_moment, second, master, step_rate):
    first_new = BETA1 * first_moment + (1.0 - BETA1) * gradient
    second_new = BETA2 * second + (1.0 - BETA2) * gradient * gradient
    first_hat = first_new / (1.0 - BETA1**STEP)
    second_hat = second_new / (1.0 - BETA2**STEP)
    master_new = master - step_rate * (
        first_hat / (jnp.sqrt(second_hat) + ADAM_EPS) + DECAY * master
    )
    return (first_new, second_new, master_new, master_new.astype(LOW))


def per_device(
    tokens,
    cotangent,
    seq_lengths,
    attn_master,
    ffn_master,
    gain_master,
    attn_first,
    attn_second,
    ffn_first,
    ffn_second,
    gain_first,
    gain_second,
):
    seq_count = lax.axis_size("seq")
    head_count = lax.axis_size("head")
    seq_index = lax.axis_index("seq")
    head_index = lax.axis_index("head")
    local_rows, width = tokens.shape
    total_rows = local_rows * seq_count
    head_width = attn_master.shape[2]
    hidden_width = ffn_master.shape[2]
    shard_rows = attn_master.shape[1]
    local_heads = head_width // HD
    parts = seq_count // local_heads
    block = local_rows // parts
    part = seq_index % parts
    slice_rows = local_rows // head_count
    slice_start = head_index * slice_rows

    def own_slice(array):
        return lax.dynamic_slice_in_dim(array, slice_start, slice_rows, 0)

    qkv_shard = (
        attn_master[:3]
        .astype(LOW)
        .reshape(3, shard_rows, local_heads, HD)
        .transpose(1, 2, 0, 3)
        .reshape(shard_rows, 3 * head_width)
    )
    rest_shard = jnp.concatenate(
        [ffn_master[0], ffn_master[1], ffn_master[2], attn_master[3]], axis=1
    ).astype(LOW)
    gain_values = lax.all_gather(gain_master.astype(LOW), "seq", axis=1, tiled=True).astype(WIDE)
    qkv_weight = lax.all_gather(qkv_shard, "seq", axis=0, tiled=True)
    rest_weight = lax.all_gather(rest_shard, "seq", axis=0, tiled=True)
    gate_weight = rest_weight[:, :hidden_width]
    up_weight = rest_weight[:, hidden_width : 2 * hidden_width]
    down_weight = rest_weight[:, 2 * hidden_width : 3 * hidden_width]
    out_weight = rest_weight[:, 3 * hidden_width :]

    ints, floats = attention_scalars(seq_lengths, total_rows, part)

    residual = tokens.astype(WIDE)
    scale_one = lax.rsqrt(jnp.mean(residual * residual, axis=-1, keepdims=True) + EPS)
    normed_one = (residual * scale_one * gain_values[0]).astype(LOW)
    column = jnp.arange(3 * head_width, dtype=jnp.int32) % (3 * HD)
    column_factor = jnp.where(column < HD, QUERY_FACTOR, 1.0).astype(WIDE)
    projected = (dot(normed_one, qkv_weight) * column_factor).astype(LOW)

    def to_heads(array):
        columns = array.shape[1] // local_heads
        sent = (
            array.reshape(parts, block, local_heads, columns)
            .transpose(2, 0, 1, 3)
            .reshape(seq_count, block, columns)
        )
        return lax.all_to_all(sent, "seq", split_axis=0, concat_axis=0, tiled=True)

    def from_heads(array):
        columns = array.shape[2]
        got = lax.all_to_all(array, "seq", split_axis=0, concat_axis=0, tiled=True)
        return (
            got.reshape(local_heads, parts, block, columns)
            .transpose(1, 2, 0, 3)
            .reshape(local_rows, local_heads * columns)
        )

    qkv = to_heads(projected)
    head_queries = qkv[:, :, :HD]
    own_key_values = qkv[:, :, HD:]
    key_values = group_exchange([own_key_values] * parts, parts)
    mixed, mass = attention_forward(ints, floats, head_queries, key_values)
    heads_out = from_heads(mixed)
    mass_got = lax.all_to_all(mass, "seq", split_axis=0, concat_axis=0, tiled=True)
    attn_mass = mass_got.reshape(local_heads, local_rows)

    attn_part = dot(heads_out, out_weight, NT).astype(LOW)
    attn_sum = line_sum(jnp.split(attn_part, head_count, axis=0))
    resid_one = own_slice(tokens).astype(WIDE) + attn_sum
    scale_two = lax.rsqrt(jnp.mean(resid_one * resid_one, axis=-1, keepdims=True) + EPS)
    unit_two = resid_one * scale_two
    normed_two = line_gather((unit_two * gain_values[1]).astype(LOW))

    gate_value = dot(normed_two, gate_weight)
    up_value = dot(normed_two, up_weight)
    hidden_grad = dot(cotangent, down_weight)
    gate_sigmoid = jax.nn.sigmoid(gate_value)
    gate_silu = gate_value * gate_sigmoid
    hidden = (gate_silu * up_value).astype(LOW)
    gate_grad = (
        hidden_grad * up_value * (gate_sigmoid + gate_silu * (1.0 - gate_sigmoid))
    ).astype(LOW)
    up_grad = (hidden_grad * gate_silu).astype(LOW)
    two_grad_part = (dot(gate_grad, gate_weight, NT) + dot(up_grad, up_weight, NT)).astype(LOW)
    normed_two_grad = line_sum(jnp.split(two_grad_part, head_count, axis=0))

    ffn_part = dot(hidden, down_weight, NT).astype(LOW)
    ffn_sum = line_sum(jnp.split(ffn_part, head_count, axis=0))
    layer_output = line_gather((resid_one + ffn_sum).astype(LOW)).astype(WIDE)
    ffn_raw = jnp.concatenate(
        [
            dot(normed_two, gate_grad, TN).astype(LOW),
            dot(normed_two, up_grad, TN).astype(LOW),
            dot(cotangent, hidden, TN).astype(LOW),
        ],
        axis=1,
    )
    ffn_shard = lax.psum_scatter(ffn_raw, "seq", scatter_dimension=0, tiled=True).astype(WIDE)

    unit_grad_two = normed_two_grad * gain_values[1]
    resid_grad = own_slice(cotangent).astype(WIDE) + scale_two * (
        unit_grad_two - unit_two * jnp.mean(unit_grad_two * unit_two, axis=-1, keepdims=True)
    )
    branch_low = line_gather(resid_grad.astype(LOW))
    heads_grad = dot(branch_low, out_weight).astype(LOW)
    out_raw = dot(branch_low, heads_out, TN).astype(LOW)

    head_grads = to_heads(heads_grad)
    q_grad, kv_grad = attention_backward(ints, floats, head_queries, head_grads, key_values)
    kv_terms = group_exchange(
        [lax.dynamic_index_in_dim(kv_grad, part ^ k, 0, False) for k in range(parts)], parts
    )
    kv_sum = functools.reduce(lambda a, b: a + b, [t.astype(WIDE) for t in kv_terms]).astype(LOW)
    qkv_grad = from_heads(jnp.concatenate([q_grad, kv_sum], axis=2))

    one_grad_part = dot(qkv_grad, qkv_weight, NT).astype(LOW)
    normed_one_grad = line_sum(jnp.split(one_grad_part, head_count, axis=0))
    attn_raw = jnp.concatenate([dot(normed_one, qkv_grad, TN).astype(LOW), out_raw], axis=1)
    attn_shard = lax.psum_scatter(attn_raw, "seq", scatter_dimension=0, tiled=True).astype(WIDE)

    unit_one = own_slice(tokens).astype(WIDE) * own_slice(scale_one)
    unit_grad_one = normed_one_grad * gain_values[0]
    input_slice = resid_grad + own_slice(scale_one) * (
        unit_grad_one - unit_one * jnp.mean(unit_grad_one * unit_one, axis=-1, keepdims=True)
    )
    input_grad = line_gather(input_slice.astype(LOW)).astype(WIDE)

    own_gain = gain_master.astype(LOW).astype(WIDE)
    gain_terms = jnp.stack(
        [
            jnp.sum(qkv_shard.astype(WIDE) * attn_shard[:, : 3 * head_width], axis=1),
            jnp.sum(
                rest_shard[:, : 2 * hidden_width].astype(WIDE) * ffn_shard[:, : 2 * hidden_width],
                axis=1,
            ),
        ]
    ) / own_gain
    squares = jnp.sum(attn_shard * attn_shard) + jnp.sum(ffn_shard * ffn_shard)
    small = jnp.zeros((2, width + HD), WIDE)
    small = lax.dynamic_update_slice(small, gain_terms, (0, seq_index * shard_rows))
    small = small.at[0, width].set(squares)
    small = lax.psum(small, ("seq", "head"))
    gain_all = small[:, :width]
    gain_shard = lax.dynamic_slice_in_dim(gain_all, seq_index * shard_rows, shard_rows, 1)
    grad_norm = jnp.sqrt(small[0, width] + jnp.sum(gain_all * gain_all))
    clip_factor = jnp.minimum(1.0, CLIP / (grad_norm + 1e-06))

    qkv_shard_grad = (
        attn_shard[:, : 3 * head_width]
        .reshape(shard_rows, local_heads, 3, HD)
        .transpose(2, 0, 1, 3)
        .reshape(3, shard_rows, head_width)
    )
    attn_grad = (
        jnp.concatenate([qkv_shard_grad, attn_shard[None, :, 3 * head_width :]], axis=0) * clip_factor
    )
    ffn_grad = jnp.stack(jnp.split(ffn_shard, 3, axis=1)) * clip_factor
    gain_grad = gain_shard * clip_factor
    attn_state = adam_update(attn_grad, attn_first, attn_second, attn_master, RATE)
    ffn_state = adam_update(ffn_grad, ffn_first, ffn_second, ffn_master, RATE)
    gain_state = adam_update(gain_grad, gain_first, gain_second, gain_master, GAIN_RATE)
    return (
        layer_output,
        input_grad,
        attn_mass,
        grad_norm,
        attn_grad,
        attn_state[0],
        attn_state[1],
        attn_state[2],
        attn_state[3],
        ffn_grad,
        ffn_state[0],
        ffn_state[1],
        ffn_state[2],
        ffn_state[3],
        gain_grad,
        gain_state[0],
        gain_state[1],
        gain_state[2],
        gain_state[3],
    )


def solution(mesh):
    in_specs = (
        P("seq", None),
        P("seq", None),
        P(),
        P(None, "seq", "head"),
        P(None, "seq", "head"),
        P(None, "seq"),
        P(None, "seq", "head"),
        P(None, "seq", "head"),
        P(None, "seq", "head"),
        P(None, "seq", "head"),
        P(None, "seq"),
        P(None, "seq"),
    )
    out_specs = (
        P("seq", None),
        P("seq", None),
        P("head", "seq"),
        P(),
        P(None, "seq", "head"),
        P(None, "seq", "head"),
        P(None, "seq", "head"),
        P(None, "seq", "head"),
        P(None, "seq", "head"),
        P(None, "seq", "head"),
        P(None, "seq", "head"),
        P(None, "seq", "head"),
        P(None, "seq", "head"),
        P(None, "seq", "head"),
        P(None, "seq"),
        P(None, "seq"),
        P(None, "seq"),
        P(None, "seq"),
        P(None, "seq"),
    )
    return jax.shard_map(
        per_device, mesh=mesh, in_specs=in_specs, out_specs=out_specs, check_vma=False
    )
```

time: 2460 us -> 1400 us (0.57)
  waiting for transfers between devices: 1500 us -> 602 us
  matrix products: 568 us -> 166 us
  starting transfers between devices: 0.8 us -> 144 us
  Pallas kernels: 0 us -> 106 us
  blocking collectives: 48.4 us -> 129 us
  local copies, waits for them, and re-layouts: 157 us -> 115 us
  other arithmetic: 142 us -> 105 us
    psum x3 -> x0, waiting for transfers between devices: 777 us -> none  [the longest x1 289 us: per_device(): normed_two_grad = lax.psum(two_grad_part, 'head')]
    ppermute x0 -> x50, waiting for transfers between devices: none -> 479 us  [the longest x4 127 us: line_gather(): left_two = lax.ppermute(piece, 'head', [(0, 2), (1, 3)])]
    dot_general x68 -> x15, matrix products: 568 us -> 166 us  [dot(): return lax.dot_general(left, right, dims, preferred_element_type=WIDE)]
    reduce_scatter x4 -> x2, waiting for transfers between devices: 398 us -> 0.02 us  [the longest x1 0.02 us: per_device(): lax.psum_scatter(ffn_raw, 'seq', scatter_dimension=0, tiled=True)]
    all_gather x4 -> x2, waiting for transfers between devices: 271 us -> 48.9 us  [the longest x1 26.6 us: per_device(): rest_weight = lax.all_gather(rest_shard, 'seq', axis=0, tiled=True)]
    ppermute x0 -> x50, starting transfers between devices: none -> 120 us  [the longest x4 21.4 us: line_gather(): left_one = lax.ppermute(piece, 'head', [(0, 1), (1, 2), (2, 3)])]
    pallas_call x0 -> x2, Pallas kernels: none -> 106 us  [the longest x1 70.1 us: attention_backward(): pl.pallas_call(functools.partial(backward_kernel, count, parts, block, ti...]
    all_to_all x0 -> x4, waiting for transfers between devices: none -> 73.7 us  [the longest x2 58.4 us: from_heads(): got = lax.all_to_all(array, 'seq', split_axis=0, concat_axis=0, tiled=True)]
  transfers between devices with their start and end apart: 13 -> 58, of which waited for: 13 -> 35; matrix products, arithmetic and copies ran while one was open for 7% -> 14% of each run, Pallas kernels for 0% -> 3%
where the time goes in v1:
time: 1400 us; the launch traced here: 1390 us
  waiting for transfers between devices  602 us (43%)
  matrix products  166 us (12%)
  starting transfers between devices  144 us (10%)
  blocking collectives  129 us (9%)
  local copies, waits for them, and re-layouts  115 us (8%)
  Pallas kernels  106 us (8%)
  other arithmetic  105 us (8%)
  between operations  20.7 us (1%)
    dot_general x15, matrix products, dot(): return lax.dot_general(left, right, dims, preferred_element_type=WIDE)  166 us
    ppermute x4, waiting for transfers between devices, line_gather(): left_two = lax.ppermute(piece, 'head', [(0, 2), (1, 3)])  127 us
    ppermute x4, waiting for transfers between devices, line_sum(): far = lax.ppermute(from_end(3), 'head', inward)  79.1 us
    pallas_call x1, Pallas kernels, attention_backward(): pl.pallas_call(functools.partial(backward_kernel, count, parts, block, ti...  70.1 us
    all_to_all x1, blocking collectives, to_heads(): return lax.all_to_all(sent, 'seq', split_axis=0, concat_axis=0, tiled=True)  70 us
    ppermute x4, waiting for transfers between devices, line_sum(): near = lax.ppermute(from_end(1), 'head', inward)  67.1 us
    ppermute x4, waiting for transfers between devices, line_sum(): middle = lax.ppermute(from_end(2), 'head', inward)  66.3 us
    unnamed x98, local copies, waits for them, and re-layouts  65.5 us
  transfers between devices with their start and end apart: 58, of which 35 were waited for; matrix products, arithmetic and copies ran while one was open for 14% of the time, Pallas kernels for 3%

profile of v1, /device:TPU:8, one launch (start us, length us, event | category | flops | bytes accessed | tf_op | source)
XLA Modules:
  0.0 1387.4 jit_solution(18089517796578309920)
XLA Ops:
  35.7 22.3 %all-gather.3.cloned.1.call-done = bf16[2048,1536]{0,1:T(8,128)(2,1)} async-done(((bf16[256,1536]{0,1:T(8,128)(2,1)}), bf16[2048,1536]{0,1:T(8,128)(2,1)}) %all-gather.3.cloned.1.call-update) | async-done | bytes 6291472 | tf_op jit(solution)/shard_map/all_gather | solution.py:398
  74.9 70.0 %all_to_all.25 = bf16[8,512,384]{2,1,0:T(8,128)(2,1)S(1)} all-to-all(bf16[8,512,384]{2,1,0:T(8,128)(2,1)S(1)} %bitcast.92), channel_id=1, replica_groups=mesh['seq'=8,'head'=4] {'seq'}, dimensions={0} | all-to-all | bytes 6291456 | tf_op jit(solution)/shard_map/all_to_all | solution.py:421
  151.1 35.9 %attention_forward.1 = (bf16[8,512,128]{2,1,0:T(8,128)(2,1)}, f32[8,1,512]{2,1,0:T(1,128)}) custom-call(s32[2]{0:T(128)S(1)} %pad_add_fusion.ints, f32[6]{0:T(128)S(1)} %reshape.246.floats, bf16[8,512,128]{2,1,0:T(8,128)(2,1)S(1)} %slice.112.q_ref, bf16[8,512,256]{2,1,0:T(8,128)(2,1)S(1)} %slice.113.rest_0_, bf16[8,512,256]{2,1,0:T(8,128)(2,1)} %collective-permute-done.rest_1_), custom_call_target="tpu_custom_call" | custom-call | flops 17179869184 | bytes 8388608 | tf_op jit(solution)/shard_map/attention_forward/pallas_call | solution.py:132
  190.8 26.8 %all-to-all-done.1 = bf16[8,512,128]{2,1,0:T(8,128)(2,1)S(1)} async-done(((bf16[8,512,128]{2,1,0:T(8,128)(2,1)}), bf16[8,512,128]{2,1,0:T(8,128)(2,1)S(1)}, u32[]{:S(2)}, u32[]{:S(2)}) %all-to-all-start.1) | async-done | bytes 1048608 | tf_op jit(solution)/shard_map/all_to_all | solution.py:425
  218.5 26.6 %all-gather.5.cloned.1.call-done = bf16[2048,6656]{0,1:T(8,128)(2,1)} async-done(((bf16[256,6656]{0,1:T(8,128)(2,1)}), bf16[2048,6656]{0,1:T(8,128)(2,1)}) %all-gather.5.cloned.1.call-update) | async-done | bytes 27262992 | tf_op jit(solution)/shard_map/all_gather | solution.py:399
  259.8 17.3 %collective-permute-done.5 = bf16[256,2048]{1,0:T(8,128)(2,1)S(1)} collective-permute-done((bf16[256,2048]{1,0:T(8,128)(2,1)S(1)}, bf16[256,2048]{1,0:T(8,128)(2,1)S(1)}, u32[]{:S(2)}, u32[]{:S(2)}) %collective-permute-start.5) | collective-permute-done | bytes 1048608 | tf_op jit(solution)/shard_map/ppermute | solution.py:293
  281.9 17.7 %collective-permute-done.2 = bf16[256,2048]{1,0:T(8,128)(2,1)S(1)} collective-permute-done((bf16[256,2048]{1,0:T(8,128)(2,1)S(1)}, bf16[256,2048]{1,0:T(8,128)(2,1)S(1)}, u32[]{:S(2)}, u32[]{:S(2)}) %collective-permute-start.2) | collective-permute-done | bytes 1048608 | tf_op jit(solution)/shard_map/ppermute | solution.py:292
  304.4 17.2 %collective-permute-done.4 = bf16[256,2048]{1,0:T(8,128)(2,1)} collective-permute-done((bf16[256,2048]{1,0:T(8,128)(2,1)S(1)}, bf16[256,2048]{1,0:T(8,128)(2,1)}, u32[]{:S(2)}, u32[]{:S(2)}) %collective-permute-start.4) | collective-permute-done | bytes 1048608 | tf_op jit(solution)/shard_map/ppermute | solution.py:294
  341.7 37.6 %collective-permute-done.7 = bf16[256,2048]{1,0:T(8,128)(2,1)} collective-permute-done((bf16[256,2048]{1,0:T(8,128)(2,1)}, bf16[256,2048]{1,0:T(8,128)(2,1)}, u32[]{:S(2)}, u32[]{:S(2)}) %collective-permute-start.7) | collective-permute-done | bytes 1048608 | tf_op jit(solution)/shard_map/ppermute | solution.py:316
  387.5 14.6 %fusion.6 = f32[2048,1024]{0,1:T(8,128)} fusion(bf16[1024,2048]{1,0:T(8,128)(2,1)} %param.15, bf16[2048,6656]{0,1:T(8,128)(2,1)} %all-gather.5.cloned.1.call-done), kind=kOutput, calls=%fused_computation.21 | convolution fusion | flops 8589934592 | bytes 20971520 | tf_op jit(solution)/shard_map/dot_general | solution.py:35
  411.3 19.1 %collective-permute-done.12 = bf16[256,2048]{1,0:T(8,128)(2,1)S(1)} collective-permute-done((bf16[256,2048]{1,0:T(8,128)(2,1)}, bf16[256,2048]{1,0:T(8,128)(2,1)S(1)}, u32[]{:S(2)}, u32[]{:S(2)}) %collective-permute-start.12) | collective-permute-done | bytes 1048608 | tf_op jit(solution)/shard_map/ppermute | solution.py:315
  446.4 21.4 %fusion.4 = (bf16[1024,2048]{1,0:T(8,128)(2,1)}, bf16[1024,2048]{1,0:T(8,128)(2,1)}, bf16[1024,2048]{1,0:T(8,128)(2,1)}) fusion(f32[2048,1024]{0,1:T(8,128)} %fusion.6, f32[1024,2048]{1,0:T(8,128)} %fusion.16, bf16[1024,2048]{1,0:T(8,128)(2,1)} %copy-done.19, bf16[2048,6656]{0,1:T(8,128)(2,1)} %all-gather.5.cloned.1.call-done), kind=kOutput, calls=%fused_computation.12 | convolution fusion | flops 8619294720 | bytes 41943040 | tf_op jit(solution)/shard_map/dot_general | solution.py:35
  500.9 19.3 %collective-permute-done.29 = bf16[256,2048]{1,0:T(8,128)(2,1)S(1)} collective-permute-done((bf16[256,2048]{1,0:T(8,128)(2,1)S(1)}, bf16[256,2048]{1,0:T(8,128)(2,1)S(1)}, u32[]{:S(2)}, u32[]{:S(2)}) %collective-permute-start.29) | collective-permute-done | bytes 1048608 | tf_op jit(solution)/shard_map/ppermute | solution.py:293
  522.5 20.1 %collective-permute-done.26 = bf16[256,2048]{1,0:T(8,128)(2,1)S(1)} collective-permute-done((bf16[256,2048]{1,0:T(8,128)(2,1)S(1)}, bf16[256,2048]{1,0:T(8,128)(2,1)S(1)}, u32[]{:S(2)}, u32[]{:S(2)}) %collective-permute-start.26) | collective-permute-done | bytes 1048608 | tf_op jit(solution)/shard_map/ppermute | solution.py:292
  544.4 16.6 %collective-permute-done.28 = bf16[256,2048]{1,0:T(8,128)(2,1)S(1)} collective-permute-done((bf16[256,2048]{1,0:T(8,128)(2,1)S(1)}, bf16[256,2048]{1,0:T(8,128)(2,1)S(1)}, u32[]{:S(2)}, u32[]{:S(2)}) %collective-permute-start.28) | collective-permute-done | bytes 1048608 | tf_op jit(solution)/shard_map/ppermute | solution.py:294
  570.5 37.0 %collective-permute-done.31 = bf16[256,2048]{1,0:T(8,128)(2,1)S(1)} collective-permute-done((bf16[256,2048]{1,0:T(8,128)(2,1)S(1)}, bf16[256,2048]{1,0:T(8,128)(2,1)S(1)}, u32[]{:S(2)}, u32[]{:S(2)}) %collective-permute-start.31) | collective-permute-done | bytes 1048608 | tf_op jit(solution)/shard_map/ppermute | solution.py:316
  619.4 16.3 %collective-permute-done.33 = bf16[256,2048]{1,0:T(8,128)(2,1)S(1)} collective-permute-done((bf16[256,2048]{1,0:T(8,128)(2,1)S(1)}, bf16[256,2048]{1,0:T(8,128)(2,1)S(1)}, u32[]{:S(2)}, u32[]{:S(2)}) %collective-permute-start.33) | collective-permute-done | bytes 1048608 | tf_op jit(solution)/shard_map/ppermute | solution.py:314
  640.4 20.6 %collective-permute-done.36 = bf16[256,2048]{1,0:T(8,128)(2,1)S(1)} collective-permute-done((bf16[256,2048]{1,0:T(8,128)(2,1)S(1)}, bf16[256,2048]{1,0:T(8,128)(2,1)S(1)}, u32[]{:S(2)}, u32[]{:S(2)}) %collective-permute-start.36) | collective-permute-done | bytes 1048608 | tf_op jit(solution)/shard_map/ppermute | solution.py:315
  672.6 15.3 %all-to-all-done.2.grad_ref = bf16[8,512,128]{2,1,0:T(8,128)(2,1)S(1)} async-done(((bf16[8,512,128]{2,1,0:T(8,128)(2,1)}), bf16[8,512,128]{2,1,0:T(8,128)(2,1)S(1)}, u32[]{:S(2)}, u32[]{:S(2)}) %all-to-all-start.2) | async-done | bytes 1048608 | tf_op jit(solution)/shard_map/all_to_all | solution.py:421
  688.9 70.1 %attention_backward.1 = (bf16[8,512,128]{2,1,0:T(8,128)(2,1)}, bf16[2,8,512,256]{3,2,1,0:T(8,128)(2,1)}) custom-call(s32[2]{0:T(128)} %copy-done.3, f32[6]{0:T(128)} %copy-done.2, bf16[8,512,128]{2,1,0:T(8,128)(2,1)} %copy-done.1, bf16[8,512,128]{2,1,0:T(8,128)(2,1)} %copy-done.24, bf16[8,512,256]{2,1,0:T(8,128)(2,1)} %copy-done, ...), custom_call_target="tpu_custom_call" | custom-call | flops 42949672960 | bytes 16777216 | tf_op jit(solution)/shard_map/attention_backward/pallas_call | solution.py:233
  780.6 31.6 %all-to-all-done.3 = bf16[8,512,384]{2,1,0:T(8,128)(2,1)S(1)} async-done(((bf16[8,512,384]{2,1,0:T(8,128)(2,1)}), bf16[8,512,384]{2,1,0:T(8,128)(2,1)S(1)}, u32[]{:S(2)}, u32[]{:S(2)}) %all-to-all-start.3) | async-done | bytes 3145760 | tf_op jit(solution)/shard_map/all_to_all | solution.py:425
  835.0 14.4 %convolution_convert_fusion = bf16[2048,2048]{0,1:T(8,128)(2,1)} fusion(bf16[1024,2048]{1,0:T(8,128)(2,1)} %copy-done.19, bf16[1024,2048]{1,0:T(8,128)(2,1)} %get-tuple-element.99), kind=kOutput, calls=%fused_computation.18 | convolution fusion | flops 8594128896 | bytes 16777216 | tf_op jit(solution)/shard_map/dot_general | solution.py:35
  871.9 18.4 %pad_maximum_fusion = bf16[2048,6144]{0,1:T(8,128)(2,1)} fusion(bf16[2048,2048]{0,1:T(8,128)(2,1)} %convert_bitcast_fusion, bf16[2048,2048]{0,1:T(8,128)(2,1)} %convolution_convert_fusion, bf16[2048,2048]{0,1:T(8,128)(2,1)} %convolution_convert_fusion.1), kind=kLoop, calls=%fused_computation | loop fusion | flops 75497472 | bytes 50331648 | tf_op jit(solution)/shard_map/concatenate | solution.py:464
  930.1 20.6 %collective-permute-done.39 = bf16[256,2048]{1,0:T(8,128)(2,1)S(1)} collective-permute-done((bf16[256,2048]{1,0:T(8,128)(2,1)S(1)}, bf16[256,2048]{1,0:T(8,128)(2,1)S(1)}, u32[]{:S(2)}, u32[]{:S(2)}) %collective-permute-start.39) | collective-permute-done | bytes 1048608 | tf_op jit(solution)/shard_map/ppermute | solution.py:292
  953.4 19.8 %collective-permute-done.17 = bf16[256,2048]{1,0:T(8,128)(2,1)S(1)} collective-permute-done((bf16[256,2048]{1,0:T(8,128)(2,1)S(1)}, bf16[256,2048]{1,0:T(8,128)(2,1)S(1)}, u32[]{:S(2)}, u32[]{:S(2)}) %collective-permute-start.17) | collective-permute-done | bytes 1048608 | tf_op jit(solution)/shard_map/ppermute | solution.py:293
  974.9 20.7 %collective-permute-done.14 = bf16[256,2048]{1,0:T(8,128)(2,1)S(1)} collective-permute-done((bf16[256,2048]{1,0:T(8,128)(2,1)S(1)}, bf16[256,2048]{1,0:T(8,128)(2,1)S(1)}, u32[]{:S(2)}, u32[]{:S(2)}) %collective-permute-start.14) | collective-permute-done | bytes 1048608 | tf_op jit(solution)/shard_map/ppermute | solution.py:292
  997.3 20.8 %collective-permute-done.41 = bf16[256,2048]{1,0:T(8,128)(2,1)S(1)} collective-permute-done((bf16[256,2048]{1,0:T(8,128)(2,1)S(1)}, bf16[256,2048]{1,0:T(8,128)(2,1)S(1)}, u32[]{:S(2)}, u32[]{:S(2)}) %collective-permute-start.41) | collective-permute-done | bytes 1048608 | tf_op jit(solution)/shard_map/ppermute | solution.py:294
  1071.0 34.0 %collective-permute-done.19 = bf16[256,2048]{1,0:T(8,128)(2,1)} collective-permute-done((bf16[256,2048]{1,0:T(8,128)(2,1)S(1)}, bf16[256,2048]{1,0:T(8,128)(2,1)}, u32[]{:S(2)}, u32[]{:S(2)}) %collective-permute-start.19) | collective-permute-done | bytes 1048608 | tf_op jit(solution)/shard_map/ppermute | solution.py:316
  1164.3 18.0 %collective-permute-done.44 = bf16[256,2048]{1,0:T(8,128)(2,1)} collective-permute-done((bf16[256,2048]{1,0:T(8,128)(2,1)S(1)}, bf16[256,2048]{1,0:T(8,128)(2,1)}, u32[]{:S(2)}, u32[]{:S(2)}) %collective-permute-start.44) | collective-permute-done | bytes 1048608 | tf_op jit(solution)/shard_map/ppermute | solution.py:316
  1203.6 29.8 %collective-permute-done.48 = bf16[256,2048]{1,0:T(8,128)(2,1)S(1)} collective-permute-done((bf16[256,2048]{1,0:T(8,128)(2,1)S(1)}, bf16[256,2048]{1,0:T(8,128)(2,1)S(1)}, u32[]{:S(2)}, u32[]{:S(2)}) %collective-permute-start.48) | collective-permute-done | bytes 1048608 | tf_op jit(solution)/shard_map/ppermute | solution.py:319
  1267.1 50.0 %psum.7 = f32[2,2176]{1,0:T(2,128)S(1)} all-reduce(f32[2,2176]{1,0:T(2,128)S(1)} %scatter.4), channel_id=1, replica_groups=mesh['seq'=8,'head'=4] {'seq','head'}, use_global_device_ids=true, to_apply=%region_11.12 | all-reduce | flops 4352 | bytes 34816 | tf_op jit(solution)/shard_map/psum | solution.py:516
  1325.3 15.7 %fusion.61 = (bf16[3,256,2048]{1,2,0:T(8,128)(2,1)S(1)}, f32[3,256,2048]{1,2,0:T(8,128)}, f32[3,256,2048]{1,2,0:T(8,128)}, f32[3,256,2048]{1,2,0:T(8,128)}, f32[3,256,2048]{1,2,0:T(8,128)}) fusion(f32[3,256,2048]{1,2,0:T(8,128)} %copy.52, f32[3,256,2048]{1,2,0:T(8,128)} %copy.59, f32[3,256,2048]{1,2,0:T(8,128)} %copy.58, f32[]{:T(128)S(6)} %min.53, ...), kind=kLoop, calls=%fused_computation.172 | loop fusion | flops 28311552 | bytes 53477380 | tf_op jit(solution)/shard_map/convert_element_type | solution.py:351
  (317 shorter events, 531.3 us)
Async XLA Ops:
  7.2 50.9 %all-gather.3.cloned.1.call-start = ((), (), s32[]{:S(2)}) async-start(), calls=%async_computation.7 | async-start | bytes 7077888 | tf_op jit(solution)/shard_map/all_gather | solution.py:398
  10.0 235.0 %all-gather.5.cloned.1.call-start = ((), (), s32[]{:S(2)}) async-start(), calls=%async_computation.8 | async-start | bytes 30670848 | tf_op jit(solution)/shard_map/all_gather | solution.py:399
  250.6 49.0 %collective-permute-start.2 = (bf16[256,2048]{1,0:T(8,128)(2,1)S(1)}, bf16[256,2048]{1,0:T(8,128)(2,1)S(1)}, u32[]{:S(2)}, u32[]{:S(2)}) collective-permute-start(bf16[256,2048]{1,0:T(8,128)(2,1)S(1)} %get-tuple-element.117), channel_id=1, source_target_pairs={{0,1},{3,2},{4,5},{7,6},{8,9},{11,10},{12,13},{15,14},{16,17},{19,... | collective-permute-start | bytes 3145736 | tf_op jit(solution)/shard_map/ppermute | solution.py:292
  251.9 69.7 %collective-permute-start.4 = (bf16[256,2048]{1,0:T(8,128)(2,1)S(1)}, bf16[256,2048]{1,0:T(8,128)(2,1)}, u32[]{:S(2)}, u32[]{:S(2)}) collective-permute-start(bf16[256,2048]{1,0:T(8,128)(2,1)S(1)} %get-tuple-element.118), channel_id=1, source_target_pairs={{0,1},{3,2},{4,5},{7,6},{8,9},{11,10},{12,13},{15,14},{16,17},{19,... | collective-permute-start | bytes 3145736 | tf_op jit(solution)/shard_map/ppermute | solution.py:294
  253.2 68.4 %collective-permute-start.1 = (bf16[256,2048]{1,0:T(8,128)(2,1)S(1)}, bf16[256,2048]{1,0:T(8,128)(2,1)}, u32[]{:S(2)}, u32[]{:S(2)}) collective-permute-start(bf16[256,2048]{1,0:T(8,128)(2,1)S(1)} %get-tuple-element.116), channel_id=1, source_target_pairs={{1,0},{2,3},{5,4},{6,7},{9,8},{10,11},{13,12},{14,15},{17,16},{18,... | collective-permute-start | bytes 3145736 | tf_op jit(solution)/shard_map/ppermute | solution.py:295
  278.5 43.0 %collective-permute-start.6 = (bf16[256,2048]{1,0:T(8,128)(2,1)}, bf16[256,2048]{1,0:T(8,128)(2,1)}, u32[]{:S(2)}, u32[]{:S(2)}) collective-permute-start(bf16[256,2048]{1,0:T(8,128)(2,1)} %add_convert_fusion.8), channel_id=1, source_target_pairs={{1,2},{2,1},{5,6},{6,5},{9,10},{10,9},{13,14},{14,13},{17,18},{18,... | collective-permute-start | bytes 3145736 | tf_op jit(solution)/shard_map/ppermute | solution.py:299
  331.4 47.8 %collective-permute-start.7 = (bf16[256,2048]{1,0:T(8,128)(2,1)}, bf16[256,2048]{1,0:T(8,128)(2,1)}, u32[]{:S(2)}, u32[]{:S(2)}) collective-permute-start(bf16[256,2048]{1,0:T(8,128)(2,1)} %multiply_convert_fusion.2), channel_id=1, source_target_pairs={{0,2},{1,3},{4,6},{5,7},{8,10},{9,11},{12,14},{13,15},{16,18},{17,... | collective-permute-start | bytes 3145736 | tf_op jit(solution)/shard_map/ppermute | solution.py:316
  337.7 42.3 %collective-permute-start.10 = (bf16[256,2048]{1,0:T(8,128)(2,1)}, bf16[256,2048]{1,0:T(8,128)(2,1)S(1)}, u32[]{:S(2)}, u32[]{:S(2)}) collective-permute-start(bf16[256,2048]{1,0:T(8,128)(2,1)} %multiply_convert_fusion.2), channel_id=1, source_target_pairs={{3,1},{2,0},{7,5},{6,4},{11,9},{10,8},{15,13},{14,12},{19,17},{18,... | collective-permute-start | bytes 3145736 | tf_op jit(solution)/shard_map/ppermute | solution.py:317
  339.0 67.0 %collective-permute-start.9 = (bf16[256,2048]{1,0:T(8,128)(2,1)}, bf16[256,2048]{1,0:T(8,128)(2,1)S(1)}, u32[]{:S(2)}, u32[]{:S(2)}) collective-permute-start(bf16[256,2048]{1,0:T(8,128)(2,1)} %multiply_convert_fusion.2), channel_id=1, source_target_pairs={{0,1},{1,2},{2,3},{4,5},{5,6},{6,7},{8,9},{9,10},{10,11},{12,13},{... | collective-permute-start | bytes 3145736 | tf_op jit(solution)/shard_map/ppermute | solution.py:314
  493.5 49.2 %collective-permute-start.26 = (bf16[256,2048]{1,0:T(8,128)(2,1)S(1)}, bf16[256,2048]{1,0:T(8,128)(2,1)S(1)}, u32[]{:S(2)}, u32[]{:S(2)}) collective-permute-start(bf16[256,2048]{1,0:T(8,128)(2,1)S(1)} %get-tuple-element.109), channel_id=1, source_target_pairs={{0,1},{3,2},{4,5},{7,6},{8,9},{11,10},{12,13},{15,14},{16,17},{19,... | collective-permute-start | bytes 3145736 | tf_op jit(solution)/shard_map/ppermute | solution.py:292
  494.8 66.2 %collective-permute-start.28 = (bf16[256,2048]{1,0:T(8,128)(2,1)S(1)}, bf16[256,2048]{1,0:T(8,128)(2,1)S(1)}, u32[]{:S(2)}, u32[]{:S(2)}) collective-permute-start(bf16[256,2048]{1,0:T(8,128)(2,1)S(1)} %get-tuple-element.110), channel_id=1, source_target_pairs={{0,1},{3,2},{4,5},{7,6},{8,9},{11,10},{12,13},{15,14},{16,17},{19,... | collective-permute-start | bytes 3145736 | tf_op jit(solution)/shard_map/ppermute | solution.py:294
  496.1 64.9 %collective-permute-start.25 = (bf16[256,2048]{1,0:T(8,128)(2,1)S(1)}, bf16[256,2048]{1,0:T(8,128)(2,1)S(1)}, u32[]{:S(2)}, u32[]{:S(2)}) collective-permute-start(bf16[256,2048]{1,0:T(8,128)(2,1)S(1)} %get-tuple-element.108), channel_id=1, source_target_pairs={{1,0},{2,3},{5,4},{6,7},{9,8},{10,11},{13,12},{14,15},{17,16},{18,... | collective-permute-start | bytes 3145736 | tf_op jit(solution)/shard_map/ppermute | solution.py:295
  564.9 42.6 %collective-permute-start.31 = (bf16[256,2048]{1,0:T(8,128)(2,1)S(1)}, bf16[256,2048]{1,0:T(8,128)(2,1)S(1)}, u32[]{:S(2)}, u32[]{:S(2)}) collective-permute-start(bf16[256,2048]{1,0:T(8,128)(2,1)S(1)} %fusion.57), channel_id=1, source_target_pairs={{0,2},{1,3},{4,6},{5,7},{8,10},{9,11},{12,14},{13,15},{16,18},{17,... | collective-permute-start | bytes 3145736 | tf_op jit(solution)/shard_map/ppermute | solution.py:316
  569.2 46.1 %collective-permute-start.34 = (bf16[256,2048]{1,0:T(8,128)(2,1)S(1)}, bf16[256,2048]{1,0:T(8,128)(2,1)S(1)}, u32[]{:S(2)}, u32[]{:S(2)}) collective-permute-start(bf16[256,2048]{1,0:T(8,128)(2,1)S(1)} %fusion.57), channel_id=1, source_target_pairs={{3,1},{2,0},{7,5},{6,4},{11,9},{10,8},{15,13},{14,12},{19,17},{18,... | collective-permute-start | bytes 3145736 | tf_op jit(solution)/shard_map/ppermute | solution.py:317
  616.7 44.3 %collective-permute-start.36 = (bf16[256,2048]{1,0:T(8,128)(2,1)S(1)}, bf16[256,2048]{1,0:T(8,128)(2,1)S(1)}, u32[]{:S(2)}, u32[]{:S(2)}) collective-permute-start(bf16[256,2048]{1,0:T(8,128)(2,1)S(1)} %fusion.57), channel_id=1, source_target_pairs={{3,2},{2,1},{1,0},{7,6},{6,5},{5,4},{11,10},{10,9},{9,8},{15,14},{... | collective-permute-start | bytes 3145736 | tf_op jit(solution)/shard_map/ppermute | solution.py:315
  774.3 464.0 %reduce-scatter.3.cloned.1.call-start = ((), (), s32[]{:S(2)}) async-start(), calls=%async_computation.9 | async-start | bytes 9437184 | tf_op jit(solution)/shard_map/reduce_scatter | solution.py:493
  834.9 417.0 %reduce-scatter.5.cloned.1.call-start = ((), (), s32[]{:S(2)}) async-start(), calls=%async_computation.10 | async-start | bytes 28311552 | tf_op jit(solution)/shard_map/reduce_scatter | solution.py:472
  914.3 58.8 %collective-permute-start.17 = (bf16[256,2048]{1,0:T(8,128)(2,1)S(1)}, bf16[256,2048]{1,0:T(8,128)(2,1)S(1)}, u32[]{:S(2)}, u32[]{:S(2)}) collective-permute-start(bf16[256,2048]{1,0:T(8,128)(2,1)S(1)} %get-tuple-element.115), channel_id=1, source_target_pairs={{0,1},{3,2},{4,5},{7,6},{8,9},{11,10},{12,13},{15,14},{16,17},{19,... | collective-permute-start | bytes 3145736 | tf_op jit(solution)/shard_map/ppermute | solution.py:293
  915.6 80.0 %collective-permute-start.14 = (bf16[256,2048]{1,0:T(8,128)(2,1)S(1)}, bf16[256,2048]{1,0:T(8,128)(2,1)S(1)}, u32[]{:S(2)}, u32[]{:S(2)}) collective-permute-start(bf16[256,2048]{1,0:T(8,128)(2,1)S(1)} %get-tuple-element.113), channel_id=1, source_target_pairs={{0,1},{3,2},{4,5},{7,6},{8,9},{11,10},{12,13},{15,14},{16,17},{19,... | collective-permute-start | bytes 3145736 | tf_op jit(solution)/shard_map/ppermute | solution.py:292
  916.9 101.1 %collective-permute-start.41 = (bf16[256,2048]{1,0:T(8,128)(2,1)S(1)}, bf16[256,2048]{1,0:T(8,128)(2,1)S(1)}, u32[]{:S(2)}, u32[]{:S(2)}) collective-permute-start(bf16[256,2048]{1,0:T(8,128)(2,1)S(1)} %get-tuple-element.106), channel_id=1, source_target_pairs={{0,1},{3,2},{4,5},{7,6},{8,9},{11,10},{12,13},{15,14},{16,17},{19,... | collective-permute-start | bytes 3145736 | tf_op jit(solution)/shard_map/ppermute | solution.py:294
  928.2 91.4 %collective-permute-start.38 = (bf16[256,2048]{1,0:T(8,128)(2,1)S(1)}, bf16[256,2048]{1,0:T(8,128)(2,1)S(1)}, u32[]{:S(2)}, u32[]{:S(2)}) collective-permute-start(bf16[256,2048]{1,0:T(8,128)(2,1)S(1)} %get-tuple-element.104), channel_id=1, source_target_pairs={{1,0},{2,3},{5,4},{6,7},{9,8},{10,11},{13,12},{14,15},{17,16},{18,... | collective-permute-start | bytes 3145736 | tf_op jit(solution)/shard_map/ppermute | solution.py:295
  950.7 70.9 %collective-permute-start.43 = (bf16[256,2048]{1,0:T(8,128)(2,1)S(1)}, bf16[256,2048]{1,0:T(8,128)(2,1)S(1)}, u32[]{:S(2)}, u32[]{:S(2)}) collective-permute-start(bf16[256,2048]{1,0:T(8,128)(2,1)S(1)} %add_convert_fusion.1), channel_id=1, source_target_pairs={{1,2},{2,1},{5,6},{6,5},{9,10},{10,9},{13,14},{14,13},{17,18},{18,... | collective-permute-start | bytes 3145736 | tf_op jit(solution)/shard_map/ppermute | solution.py:299
  973.1 49.9 %collective-permute-start.40 = (bf16[256,2048]{1,0:T(8,128)(2,1)S(1)}, bf16[256,2048]{1,0:T(8,128)(2,1)S(1)}, u32[]{:S(2)}, u32[]{:S(2)}) collective-permute-start(bf16[256,2048]{1,0:T(8,128)(2,1)S(1)} %add_convert_fusion.2), channel_id=1, source_target_pairs={{1,3},{2,0},{5,7},{6,4},{9,11},{10,8},{13,15},{14,12},{17,19},{18,... | collective-permute-start | bytes 3145736 | tf_op jit(solution)/shard_map/ppermute | solution.py:298
  1069.7 47.7 %collective-permute-start.22 = (bf16[256,2048]{1,0:T(8,128)(2,1)S(1)}, bf16[256,2048]{1,0:T(8,128)(2,1)}, u32[]{:S(2)}, u32[]{:S(2)}) collective-permute-start(bf16[256,2048]{1,0:T(8,128)(2,1)S(1)} %get-tuple-element.124), channel_id=1, source_target_pairs={{3,1},{2,0},{7,5},{6,4},{11,9},{10,8},{15,13},{14,12},{19,17},{18,... | collective-permute-start | bytes 3145736 | tf_op jit(solution)/shard_map/ppermute | solution.py:317
  1104.9 45.1 %collective-permute-start.20 = (bf16[256,2048]{1,0:T(8,128)(2,1)}, bf16[256,2048]{1,0:T(8,128)(2,1)}, u32[]{:S(2)}, u32[]{:S(2)}) collective-permute-start(bf16[256,2048]{1,0:T(8,128)(2,1)} %collective-permute-done.19), channel_id=1, source_target_pairs={{2,3},{6,7},{10,11},{14,15},{18,19},{22,23},{26,27},{30,31}} | collective-permute-start | bytes 3145736 | tf_op jit(solution)/shard_map/ppermute | solution.py:318
  1106.5 53.2 %collective-permute-start.21 = (bf16[256,2048]{1,0:T(8,128)(2,1)S(1)}, bf16[256,2048]{1,0:T(8,128)(2,1)}, u32[]{:S(2)}, u32[]{:S(2)}) collective-permute-start(bf16[256,2048]{1,0:T(8,128)(2,1)S(1)} %get-tuple-element.124), channel_id=1, source_target_pairs={{0,1},{1,2},{2,3},{4,5},{5,6},{6,7},{8,9},{9,10},{10,11},{12,13},{... | collective-permute-start | bytes 3145736 | tf_op jit(solution)/shard_map/ppermute | solution.py:314
  1113.7 68.5 %collective-permute-start.44 = (bf16[256,2048]{1,0:T(8,128)(2,1)S(1)}, bf16[256,2048]{1,0:T(8,128)(2,1)}, u32[]{:S(2)}, u32[]{:S(2)}) collective-permute-start(bf16[256,2048]{1,0:T(8,128)(2,1)S(1)} %get-tuple-element.123), channel_id=1, source_target_pairs={{0,2},{1,3},{4,6},{5,7},{8,10},{9,11},{12,14},{13,15},{16,18},{17,... | collective-permute-start | bytes 3145736 | tf_op jit(solution)/shard_map/ppermute | solution.py:316
  1116.1 68.3 %collective-permute-start.47 = (bf16[256,2048]{1,0:T(8,128)(2,1)S(1)}, bf16[256,2048]{1,0:T(8,128)(2,1)S(1)}, u32[]{:S(2)}, u32[]{:S(2)}) collective-permute-start(bf16[256,2048]{1,0:T(8,128)(2,1)S(1)} %get-tuple-element.123), channel_id=1, source_target_pairs={{3,1},{2,0},{7,5},{6,4},{11,9},{10,8},{15,13},{14,12},{19,17},{18,... | collective-permute-start | bytes 3145736 | tf_op jit(solution)/shard_map/ppermute | solution.py:317
  1117.4 68.9 %collective-permute-start.23 = (bf16[256,2048]{1,0:T(8,128)(2,1)}, bf16[256,2048]{1,0:T(8,128)(2,1)}, u32[]{:S(2)}, u32[]{:S(2)}) collective-permute-start(bf16[256,2048]{1,0:T(8,128)(2,1)} %collective-permute-done.22), channel_id=1, source_target_pairs={{1,0},{5,4},{9,8},{13,12},{17,16},{21,20},{25,24},{29,28}} | collective-permute-start | bytes 3145736 | tf_op jit(solution)/shard_map/ppermute | solution.py:319
  1159.8 43.7 %collective-permute-start.46 = (bf16[256,2048]{1,0:T(8,128)(2,1)S(1)}, bf16[256,2048]{1,0:T(8,128)(2,1)S(1)}, u32[]{:S(2)}, u32[]{:S(2)}) collective-permute-start(bf16[256,2048]{1,0:T(8,128)(2,1)S(1)} %get-tuple-element.123), channel_id=1, source_target_pairs={{0,1},{1,2},{2,3},{4,5},{5,6},{6,7},{8,9},{9,10},{10,11},{12,13},{... | collective-permute-start | bytes 3145736 | tf_op jit(solution)/shard_map/ppermute | solution.py:314
  1184.4 49.3 %collective-permute-start.49 = (bf16[256,2048]{1,0:T(8,128)(2,1)S(1)}, bf16[256,2048]{1,0:T(8,128)(2,1)S(1)}, u32[]{:S(2)}, u32[]{:S(2)}) collective-permute-start(bf16[256,2048]{1,0:T(8,128)(2,1)S(1)} %get-tuple-element.123), channel_id=1, source_target_pairs={{3,2},{2,1},{1,0},{7,6},{6,5},{5,4},{11,10},{10,9},{9,8},{15,14},{... | collective-permute-start | bytes 3145736 | tf_op jit(solution)/shard_map/ppermute | solution.py:315
  1186.3 47.1 %collective-permute-start.48 = (bf16[256,2048]{1,0:T(8,128)(2,1)S(1)}, bf16[256,2048]{1,0:T(8,128)(2,1)S(1)}, u32[]{:S(2)}, u32[]{:S(2)}) collective-permute-start(bf16[256,2048]{1,0:T(8,128)(2,1)S(1)} %collective-permute-done.47), channel_id=1, source_target_pairs={{1,0},{5,4},{9,8},{13,12},{17,16},{21,20},{25,24},{29,28}} | collective-permute-start | bytes 3145736 | tf_op jit(solution)/shard_map/ppermute | solution.py:319
  (70 other events, 2085.5 us)
Sparse Core Ops, SparseCore 0:
  10.2 47.8 all-gather.2
  60.5 184.4 all-gather.4
  835.0 69.5 reduce-scatter.2
  908.5 156.8 reduce-scatter.4

commit v2 on v1

v2 whole, which is shorter than its diff:
```python
import functools
import math

import jax
import jax.numpy as jnp
from jax import lax
from jax.experimental import pallas as pl
from jax.experimental.pallas import tpu as pltpu
from jax.sharding import PartitionSpec as P

HD = 128
STEP = 10


EPS = 1e-05
CLIP = 1.0
BETA1 = 0.5
BETA2 = 0.5
RATE = 0.03
GAIN_RATE = 0.3
DECAY = 0.1
ADAM_EPS = 1e-08

LOW = jnp.bfloat16
WIDE = jnp.float32
QUERY_FACTOR = -math.log2(math.e) / math.sqrt(HD)
FAR = 30000.0

NN = (((1,), (0,)), ((), ()))
NT = (((1,), (1,)), ((), ()))
TN = (((0,), (0,)), ((), ()))


def dot(left, right, dims=NN):
    return lax.dot_general(left, right, dims, preferred_element_type=WIDE)


def fill_key_columns(key_buf, sizes, cut):
    count, parts, block = sizes

    def step(at, _):
        place = at * block + lax.broadcasted_iota(jnp.int32, (block, HD), 0)
        lane = lax.broadcasted_iota(jnp.int32, (block, HD), 1)
        extra = jnp.where(lane < 3, 1.0, jnp.where((lane == 3) & (place < cut), FAR, 0.0))
        key_buf[pl.ds(pl.multiple_of(at * block, block), block), HD:] = extra.astype(LOW)
        return 0

    lax.fori_loop(0, count * parts, step, 0)


def query_columns(sizes, source, part, cut, floats):
    _, parts, block = sizes
    lane = lax.broadcasted_iota(jnp.int32, (block, HD), 1)
    place = (source * parts + part) * block + lax.broadcasted_iota(jnp.int32, (block, HD), 0)
    second = place >= cut

    def column(at):
        return jnp.where(second, floats[3 + at], floats[at])

    extra = jnp.where(
        lane == 0,
        column(0),
        jnp.where(
            lane == 1,
            column(1),
            jnp.where(lane == 2, column(2), jnp.where((lane == 3) & second, 1.0, 0.0)),
        ),
    )
    return extra.astype(LOW)


def in_causal_order(sizes, part, shape, key_dim):
    key_place = lax.broadcasted_iota(jnp.int32, shape, key_dim)
    query_place = part * sizes[2] + lax.broadcasted_iota(jnp.int32, shape, 1 - key_dim)
    return key_place <= query_place


def key_copies(sizes, part, key_values, key_buf, value_buf, sem):
    count, parts, block = sizes
    for other in range(parts):
        for at in range(count):
            row = pl.multiple_of((at * parts + (part ^ other)) * block, block)
            yield pltpu.make_async_copy(
                key_values[other].at[at, :, 0:HD], key_buf.at[pl.ds(row, block), 0:HD], sem.at[0]
            )
            yield pltpu.make_async_copy(
                key_values[other].at[at, :, HD:], value_buf.at[pl.ds(row, block), 0:HD], sem.at[0]
            )


def forward_kernel(sizes, ints, floats, q_ref, *rest):
    count, parts, block = sizes
    tile = block * parts
    key_values = rest[:parts]
    out_ref, mass_ref, key_buf, value_buf, query_buf, total, sem = rest[parts:]
    step = pl.program_id(0)
    cut, part = ints[0], ints[1]

    @pl.when(step == 0)
    def _():
        for copy in key_copies(sizes, part, key_values, key_buf, value_buf, sem):
            copy.start()
        fill_key_columns(key_buf, sizes, cut)
        value_buf[:, HD:] = jnp.ones((count * tile, HD), LOW)
        for copy in key_copies(sizes, part, key_values, key_buf, value_buf, sem):
            copy.wait()

    query_buf[:, :HD] = q_ref[...]
    query_buf[:, HD:] = query_columns(sizes, step, part, cut, floats)
    total[...] = jnp.zeros_like(total)
    first = jnp.where(step * tile >= cut, cut // tile, 0)

    def walk(at, masked):
        keys = pl.ds(pl.multiple_of(at * tile, tile), tile)
        exponent = dot(query_buf[...], key_buf[keys, :], NT)
        weight = pl.reciprocal(1.0 + jnp.exp2(exponent), approx=True)
        if masked:
            weight = jnp.where(in_causal_order(sizes, part, (block, tile), 1), weight, 0.0)
        total[...] += dot(weight.astype(LOW), value_buf[keys, :])

    def body(at, carry):
        walk(at, False)
        return carry

    lax.fori_loop(first, step, body, 0)
    walk(step, True)
    out_ref[...] = total[:, :HD].astype(LOW)
    mass_ref[...] = jnp.transpose(total[:, HD:])[0:1, :]


def attention_forward(sizes, ints, floats, queries, key_values):
    count, parts, block = sizes
    total_rows = count * parts * block
    pairs = total_rows * total_rows // (2 * parts)
    return pl.pallas_call(
        functools.partial(forward_kernel, sizes),
        out_shape=[
            jax.ShapeDtypeStruct((count, block, HD), LOW),
            jax.ShapeDtypeStruct((count, 1, block), WIDE),
        ],
        grid_spec=pltpu.PrefetchScalarGridSpec(
            num_scalar_prefetch=2,
            grid=(count,),
            in_specs=[pl.BlockSpec((None, block, HD), lambda i, *_: (i, 0, 0))]
            + [pl.BlockSpec(memory_space=pl.ANY)] * parts,
            out_specs=[
                pl.BlockSpec((None, block, HD), lambda i, *_: (i, 0, 0)),
                pl.BlockSpec((None, 1, block), lambda i, *_: (i, 0, 0)),
            ],
            scratch_shapes=[
                pltpu.VMEM((total_rows, 2 * HD), LOW),
                pltpu.VMEM((total_rows, 2 * HD), LOW),
                pltpu.VMEM((block, 2 * HD), LOW),
                pltpu.VMEM((block, 2 * HD), WIDE),
                pltpu.SemaphoreType.DMA((1,)),
            ],
        ),
        compiler_params=pltpu.CompilerParams(vmem_limit_bytes=48 * 2**20),
        cost_estimate=pl.CostEstimate(
            flops=pairs * 8 * HD, bytes_accessed=total_rows * HD * 8, transcendentals=2 * pairs
        ),
        name="attention_forward",
    )(ints, floats, queries, *key_values)


def backward_kernel(sizes, ints, floats, q_ref, grad_ref, *rest):
    count, parts, block = sizes
    tile = block * parts
    key_values = rest[:parts]
    q_grad_ref, *kv_grad_refs = rest[parts : 2 * parts + 1]
    key_buf, value_buf, turned, query_buf, q_total, k_total, v_total, sem = rest[2 * parts + 1 :]
    step = pl.program_id(0)
    cut, part = ints[0], ints[1]

    @pl.when(step == 0)
    def _():
        for copy in key_copies(sizes, part, key_values, key_buf, value_buf, sem):
            copy.start()
        fill_key_columns(key_buf, sizes, cut)
        k_total[...] = jnp.zeros_like(k_total)
        v_total[...] = jnp.zeros_like(v_total)
        for copy in key_copies(sizes, part, key_values, key_buf, value_buf, sem):
            copy.wait()

        def turn(at, carry):
            keys = pl.ds(pl.multiple_of(at * tile, tile), tile)
            turned[:, keys] = jnp.transpose(key_buf[keys, :HD])
            return carry

        lax.fori_loop(0, count, turn, 0)

    query_buf[:, :HD] = q_ref[...]
    query_buf[:, HD:] = query_columns(sizes, step, part, cut, floats)
    q_total[...] = jnp.zeros_like(q_total)
    first = jnp.where(step * tile >= cut, cut // tile, 0)

    def walk(at, masked):
        keys = pl.ds(pl.multiple_of(at * tile, tile), tile)
        exponent = dot(key_buf[keys, :], query_buf[...], NT)
        weight = pl.reciprocal(1.0 + jnp.exp2(exponent), approx=True)
        if masked:
            weight = jnp.where(in_causal_order(sizes, part, (tile, block), 0), weight, 0.0)
        weight_grad = dot(value_buf[keys, :], grad_ref[...], NT)
        score_grad = (weight_grad * (weight * (1.0 - weight))).astype(LOW)
        v_total[keys, :] += dot(weight.astype(LOW), grad_ref[...])
        k_total[keys, :] += dot(score_grad, query_buf[:, :HD])
        q_total[...] += dot(turned[:, keys], score_grad)

    def body(at, carry):
        walk(at, False)
        return carry

    lax.fori_loop(first, step, body, 0)
    walk(step, True)
    q_grad_ref[...] = (jnp.transpose(q_total[...]) * (1.0 / math.sqrt(HD))).astype(LOW)

    @pl.when(step == count - 1)
    def _():
        for other in range(parts):
            for at in range(count):
                row = pl.multiple_of((at * parts + (part ^ other)) * block, block)
                rows = pl.ds(row, block)
                kv_grad_refs[other][at, :, :HD] = (k_total[rows, :] * (-math.log(2.0))).astype(LOW)
                kv_grad_refs[other][at, :, HD:] = v_total[rows, :].astype(LOW)


def attention_backward(sizes, ints, floats, queries, grads, key_values):
    count, parts, block = sizes
    total_rows = count * parts * block
    pairs = total_rows * total_rows // (2 * parts)
    return pl.pallas_call(
        functools.partial(backward_kernel, sizes),
        out_shape=[
            jax.ShapeDtypeStruct((count, block, HD), LOW),
        ]
        + [jax.ShapeDtypeStruct((count, block, 2 * HD), LOW)] * parts,
        grid_spec=pltpu.PrefetchScalarGridSpec(
            num_scalar_prefetch=2,
            grid=(count,),
            in_specs=[pl.BlockSpec((None, block, HD), lambda i, *_: (i, 0, 0))] * 2
            + [pl.BlockSpec(memory_space=pl.ANY)] * parts,
            out_specs=[
                pl.BlockSpec((None, block, HD), lambda i, *_: (i, 0, 0)),
            ]
            + [pl.BlockSpec((count, block, 2 * HD), lambda i, *_: (0, 0, 0))] * parts,
            scratch_shapes=[
                pltpu.VMEM((total_rows, 2 * HD), LOW),
                pltpu.VMEM((total_rows, HD), LOW),
                pltpu.VMEM((HD, total_rows), LOW),
                pltpu.VMEM((block, 2 * HD), LOW),
                pltpu.VMEM((HD, block), WIDE),
                pltpu.VMEM((total_rows, HD), WIDE),
                pltpu.VMEM((total_rows, HD), WIDE),
                pltpu.SemaphoreType.DMA((1,)),
            ],
        ),
        compiler_params=pltpu.CompilerParams(vmem_limit_bytes=60 * 2**20),
        cost_estimate=pl.CostEstimate(
            flops=pairs * 100 * HD, bytes_accessed=total_rows * HD * 16, transcendentals=2 * pairs
        ),
        name="attention_backward",
    )(ints, floats, queries, grads, *key_values)


def attention_scalars(seq_lengths, total_rows, part):
    cut = seq_lengths[0]
    length = jnp.log2(jnp.stack([cut, total_rows - cut]).astype(WIDE))
    high = lax.reduce_precision(length, 8, 7)
    middle = lax.reduce_precision(length - high, 8, 7)
    low = length - high - middle
    return (
        jnp.stack([cut, part]).astype(jnp.int32),
        jnp.stack([high, middle, low], axis=1).reshape(6),
    )


def ffn_kernel(pieces, table, *refs):
    given = refs[:pieces]
    c_ref, gate_w, up_w, down_w = refs[pieces : pieces + 4]
    normed_ref, hidden_ref, gate_ref, up_ref, two_ref, total, sem = refs[pieces + 4 :]
    step = pl.program_id(0)
    rows = normed_ref.shape[0]
    slots = table.shape[0]
    slot_rows = rows // slots

    @pl.when(step == 0)
    def _():
        def each(act):
            for slot in range(slots):
                for piece in range(pieces):

                    @pl.when(table[slot] == piece)
                    def _(slot=slot, piece=piece):
                        act(
                            pltpu.make_async_copy(
                                given[piece],
                                normed_ref.at[pl.ds(slot * slot_rows, slot_rows), :],
                                sem.at[slot],
                            )
                        )

        each(lambda copy: copy.start())
        total[...] = jnp.zeros_like(total)
        each(lambda copy: copy.wait())

    chunk = min(256, rows)
    for at in range(0, rows, chunk):
        here = pl.ds(at, chunk)
        gate = dot(normed_ref[here, :], gate_w[...])
        up = dot(normed_ref[here, :], up_w[...])
        grad = dot(c_ref[here, :], down_w[...])
        sig = 1.0 / (1.0 + jnp.exp(-gate))
        silu = gate * sig
        hidden_ref[here, :] = (silu * up).astype(LOW)
        gate_grad = (grad * up * (sig + silu * (1.0 - sig))).astype(LOW)
        up_grad = (grad * silu).astype(LOW)
        gate_ref[here, :] = gate_grad
        up_ref[here, :] = up_grad
        total[here, :] += dot(gate_grad, gate_w[...], NT) + dot(up_grad, up_w[...], NT)

    @pl.when(step == pl.num_programs(0) - 1)
    def _():
        two_ref[...] = total[...].astype(LOW)


def feed_forward(pieces, order, cotangent, half, weight, hidden_width):
    rows, width = cotangent.shape[0] // 2, cotangent.shape[1]
    step = min(512, hidden_width)
    steps = hidden_width // step
    out = jax.ShapeDtypeStruct((rows, hidden_width), LOW)
    full = jax.ShapeDtypeStruct((rows, width), LOW)
    once = pl.Buffered(1)
    whole = pl.BlockSpec((rows, width), lambda j, *_: (0, 0), pipeline_mode=once)
    return pl.pallas_call(
        functools.partial(ffn_kernel, len(pieces)),
        out_shape=[full, out, out, out, full],
        grid_spec=pltpu.PrefetchScalarGridSpec(
            num_scalar_prefetch=1,
            grid=(steps,),
            in_specs=[pl.BlockSpec(memory_space=pl.ANY)] * len(pieces)
            + [
                pl.BlockSpec((rows, width), lambda j, *_: (half, 0), pipeline_mode=once),
                pl.BlockSpec((width, step), lambda j, *_: (0, j)),
                pl.BlockSpec((width, step), lambda j, *_: (0, steps + j)),
                pl.BlockSpec((width, step), lambda j, *_: (0, 2 * steps + j)),
            ],
            out_specs=[whole]
            + [pl.BlockSpec((rows, step), lambda j, *_: (0, j))] * 3
            + [whole],
            scratch_shapes=[pltpu.VMEM((rows, width), WIDE), pltpu.SemaphoreType.DMA((order.shape[0],))],
        ),
        compiler_params=pltpu.CompilerParams(vmem_limit_bytes=60 * 2**20),
        cost_estimate=pl.CostEstimate(
            flops=10 * rows * width * hidden_width,
            bytes_accessed=6 * width * hidden_width,
            transcendentals=rows * hidden_width,
        ),
        name="feed_forward",
    )(order, *pieces, cotangent, weight, weight, weight)


def ffn_wgrad_kernel(steps, n_a, n_b, c_ref, gate_a, gate_b, up_a, up_b, hid_a, hid_b, out_ref, n_turned, c_turned):
    step = pl.program_id(0)
    half = n_a.shape[0]

    @pl.when(step == 0)
    def _():
        n_turned[:, :half] = jnp.transpose(n_a[...])
        n_turned[:, half:] = jnp.transpose(n_b[...])
        c_turned[...] = jnp.transpose(c_ref[...])

    def product(turned, first, second):
        out_ref[...] = (dot(turned[:, :half], first[...]) + dot(turned[:, half:], second[...])).astype(LOW)

    @pl.when(step < steps)
    def _():
        product(n_turned, gate_a, gate_b)

    @pl.when((step >= steps) & (step < 2 * steps))
    def _():
        product(n_turned, up_a, up_b)

    @pl.when(step >= 2 * steps)
    def _():
        product(c_turned, hid_a, hid_b)


def feed_forward_wgrad(normed, cotangent, gate_grad, up_grad, hidden):
    rows, width = cotangent.shape
    hidden_width = hidden[0].shape[1]
    step = min(512, hidden_width)
    steps = hidden_width // step
    once = pl.Buffered(1)

    def whole(count):
        return pl.BlockSpec((count, width), lambda j: (0, 0), pipeline_mode=once)

    def third(at):
        return pl.BlockSpec((rows // 2, step), lambda j: (0, jnp.clip(j - at * steps, 0, steps - 1)))

    return pl.pallas_call(
        functools.partial(ffn_wgrad_kernel, steps),
        out_shape=jax.ShapeDtypeStruct((width, 3 * hidden_width), LOW),
        grid=(3 * steps,),
        in_specs=[whole(rows // 2), whole(rows // 2), whole(rows)]
        + [third(0)] * 2
        + [third(1)] * 2
        + [third(2)] * 2,
        out_specs=pl.BlockSpec((width, step), lambda j: (0, j)),
        scratch_shapes=[pltpu.VMEM((width, rows), LOW), pltpu.VMEM((width, rows), LOW)],
        compiler_params=pltpu.CompilerParams(vmem_limit_bytes=60 * 2**20),
        cost_estimate=pl.CostEstimate(
            flops=rows * width,
            bytes_accessed=rows * width,
            transcendentals=0,
        ),
        name="feed_forward_wgrad",
    )(*normed, cotangent, *gate_grad, *up_grad, *hidden)


def adam_kernel(clip, grad, first, second, master, grad_out, first_out, second_out, new_out, low_out):
    gradient = grad[...].astype(WIDE) * clip[0]
    grad_out[...] = gradient
    first_new, second_new, master_new, low = adam_update(
        gradient, first[...], second[...], master[...], RATE
    )
    first_out[...] = first_new
    second_out[...] = second_new
    new_out[...] = master_new
    low_out[...] = low


def adam_arrays(clip_factor, grad, first, second, master):
    arrays, rows, columns = master.shape
    step = min(rows, max(16, 2**17 // columns))
    state = pl.BlockSpec((None, step, columns), lambda a, i, *_: (a, i, 0))
    wide = jax.ShapeDtypeStruct(master.shape, WIDE)
    return pl.pallas_call(
        adam_kernel,
        out_shape=[wide] * 4 + [jax.ShapeDtypeStruct(master.shape, LOW)],
        grid_spec=pltpu.PrefetchScalarGridSpec(
            num_scalar_prefetch=1,
            grid=(arrays, rows // step),
            in_specs=[pl.BlockSpec((step, columns), lambda a, i, *_: (i, a))] + [state] * 3,
            out_specs=[state] * 5,
        ),
        compiler_params=pltpu.CompilerParams(vmem_limit_bytes=32 * 2**20),
        cost_estimate=pl.CostEstimate(
            flops=20 * master.size, bytes_accessed=32 * master.size, transcendentals=2 * master.size
        ),
        name="adam",
    )(clip_factor.reshape(1), grad, first, second, master)


def slice_sum(terms):
    count = lax.axis_size("head")
    got = lax.all_to_all(terms, "head", split_axis=0, concat_axis=0, tiled=True)
    rows = terms.shape[0] // count
    return functools.reduce(
        lambda a, b: a + b, [got[j * rows : (j + 1) * rows].astype(WIDE) for j in range(count)]
    )


def added(*terms):
    return functools.reduce(lambda a, b: a + b, [t.astype(WIDE) for t in terms])


def line_sum_begin(terms):
    inward = [(0, 1), (3, 2)]
    far = lax.ppermute(terms[3], "head", inward)
    outer = lax.ppermute(terms[0], "head", [(1, 0), (2, 3)])
    middle = lax.ppermute(terms[2], "head", inward)
    near = lax.ppermute(terms[1], "head", inward)
    return far, outer, middle, near


def line_sum_end(terms, got):
    at = lax.axis_index("head")
    far, outer, middle, near = got
    far_in = lax.ppermute(added(far, terms[3]).astype(LOW), "head", [(1, 3), (2, 0)])
    middle_in = lax.ppermute(added(middle, terms[2]).astype(LOW), "head", [(1, 2), (2, 1)])
    return jnp.where(
        (at == 0) | (at == 3),
        added(terms[0], outer, far_in),
        added(terms[1], near, middle_in),
    )


def gather_step_one(piece):
    return (
        lax.ppermute(piece, "head", [(0, 1), (1, 2), (2, 3)]),
        lax.ppermute(piece, "head", [(3, 2), (2, 1), (1, 0)]),
    )


def gather_step_two(got):
    return (
        lax.ppermute(got[0], "head", [(1, 2), (2, 3)]),
        lax.ppermute(got[1], "head", [(2, 1), (1, 0)]),
    )


def gather_step_three(got):
    at = lax.axis_index("head")
    return (lax.ppermute(jnp.where(at == 2, got[0], got[1]), "head", [(2, 3), (1, 0)]),)


def gathered_pieces(piece, one, two, three):
    away = lax.axis_index("head") - jnp.arange(4, dtype=jnp.int32)
    order = jnp.where(
        away == 0, 0, jnp.where(jnp.abs(away) == 3, 5, jnp.where(away > 0, away, 2 - away))
    )
    return [piece, one[0], two[0], one[1], two[1], three[0]], order


def line_gather_pieces(piece):
    count = lax.axis_size("head")
    if count != 4:
        full = lax.all_gather(piece, "head", axis=0, tiled=True)
        return jnp.split(full, count, axis=0), jnp.arange(count, dtype=jnp.int32)
    one = gather_step_one(piece)
    two = gather_step_two(one)
    return gathered_pieces(piece, one, two, gather_step_three(two))


def line_gather_wide(full, piece, got):
    count = lax.axis_size("head")
    at = lax.axis_index("head")
    rows = piece.shape[1]
    if count != 4:
        every = lax.all_gather(piece, "head", axis=0, tiled=False).astype(WIDE)
        return every.transpose(1, 0, 2, 3).reshape(full.shape)
    one, two, three = got
    for where, part in (
        (at, piece),
        (at - 1, one[0]),
        (at + 1, one[1]),
        (at - 2, two[0]),
        (at + 2, two[1]),
        (jnp.where(at == 0, 3, jnp.where(at == 3, 0, at)), three[0]),
    ):
        there = (where >= 0) & (where < count) & (where != at)
        full = lax.dynamic_update_slice(
            full,
            jnp.where(there, part, piece).astype(WIDE),
            (0, jnp.where(there, where, at) * rows, 0),
        )
    return full


def group_exchange(blocks, parts):
    count = lax.axis_size("seq")
    return [blocks[0]] + [
        lax.ppermute(blocks[k], "seq", [(j, j ^ k) for j in range(count)]) for k in range(1, parts)
    ]


def direct_terms(terms):
    at = lax.axis_index("head")
    count = lax.axis_size("head")
    return [lax.dynamic_index_in_dim(terms, at, 1, False)] + [
        lax.ppermute(
            lax.dynamic_index_in_dim(terms, at ^ k, 1, False),
            "head",
            [(j, j ^ k) for j in range(count)],
        )
        for k in range(1, count)
    ]


def direct_gather(piece):
    at = lax.axis_index("head")
    count = lax.axis_size("head")
    full = jnp.zeros((count,) + piece.shape, piece.dtype)
    for k in range(count):
        term = piece if k == 0 else lax.ppermute(piece, "head", [(j, j ^ k) for j in range(count)])
        full = lax.dynamic_update_index_in_dim(full, term, at ^ k, 0)
    return full


def sum_everywhere(values):
    for axis in ("seq", "head"):
        count = lax.axis_size(axis)
        bit = 1
        while bit < count:
            values = values + lax.ppermute(values, axis, [(j, j ^ bit) for j in range(count)])
            bit *= 2
    return values


def after(value, *others):
    return lax.optimization_barrier((value,) + others)[0]


def adam_update(gradient, first_moment, second, master, step_rate):
    first_new = BETA1 * first_moment + (1.0 - BETA1) * gradient
    second_new = BETA2 * second + (1.0 - BETA2) * gradient * gradient
    first_hat = first_new / (1.0 - BETA1**STEP)
    second_hat = second_new / (1.0 - BETA2**STEP)
    master_new = master - step_rate * (
        first_hat / (jnp.sqrt(second_hat) + ADAM_EPS) + DECAY * master
    )
    return (first_new, second_new, master_new, master_new.astype(LOW))


def per_device(
    tokens,
    cotangent,
    seq_lengths,
    attn_master,
    ffn_master,
    gain_master,
    attn_first,
    attn_second,
    ffn_first,
    ffn_second,
    gain_first,
    gain_second,
):
    seq_count = lax.axis_size("seq")
    head_count = lax.axis_size("head")
    seq_index = lax.axis_index("seq")
    head_index = lax.axis_index("head")
    local_rows, width = tokens.shape
    total_rows = local_rows * seq_count
    head_width = attn_master.shape[2]
    hidden_width = ffn_master.shape[2]
    shard_rows = attn_master.shape[1]
    local_heads = head_width // HD
    parts = seq_count // local_heads
    block = local_rows // parts
    part = seq_index % parts
    slice_rows = local_rows // head_count
    sub = slice_rows // parts
    sizes = (seq_count, parts, block)
    half_parts = parts // 2
    half_rows = local_rows // 2
    quarter_rows = slice_rows // 2

    def own_slice(array):
        columns = array.shape[1]
        return lax.dynamic_slice_in_dim(
            array.reshape(parts, block, columns), head_index * sub, sub, 1
        ).reshape(slice_rows, columns)

    def halves(array):
        return array[: array.shape[0] // 2], array[array.shape[0] // 2 :]

    def by_slices(array):
        rows, columns = array.shape
        return (
            array.reshape(rows // half_rows, half_parts, head_count, sub, columns)
            .transpose(0, 2, 1, 3, 4)
            .reshape(rows, columns)
        )

    qkv_shard = (
        attn_master[:3]
        .astype(LOW)
        .reshape(3, shard_rows, local_heads, HD)
        .transpose(1, 2, 0, 3)
        .reshape(shard_rows, 3 * head_width)
    )
    ffn_shard_low = jnp.concatenate([ffn_master[0], ffn_master[1], ffn_master[2]], axis=1).astype(LOW)
    gain_values = lax.all_gather(gain_master.astype(LOW), "seq", axis=1, tiled=True).astype(WIDE)
    qkv_weight = lax.all_gather(qkv_shard, "seq", axis=0, tiled=True)
    out_rows = (
        direct_gather(attn_master[3].astype(LOW)).transpose(1, 0, 2).reshape(shard_rows, width)
    )

    ints, floats = attention_scalars(seq_lengths, total_rows, part)

    gain_values, out_rows = lax.optimization_barrier((gain_values, out_rows))
    residual = tokens.astype(WIDE)
    scale_one = lax.rsqrt(jnp.mean(residual * residual, axis=-1, keepdims=True) + EPS)
    normed_one = (residual * scale_one * gain_values[0]).astype(LOW)
    column = jnp.arange(3 * head_width, dtype=jnp.int32) % (3 * HD)
    column_factor = jnp.where(column < HD, QUERY_FACTOR, 1.0).astype(WIDE)
    projected = (dot(normed_one, qkv_weight) * column_factor).astype(LOW)

    sent = (
        projected.reshape(parts, block, local_heads, 3 * HD)
        .transpose(2, 0, 1, 3)
        .reshape(seq_count, block, 3 * HD)
    )
    out_weight = lax.all_gather(after(out_rows, sent), "seq", axis=0, tiled=True)
    qkv = lax.all_to_all(sent, "seq", split_axis=0, concat_axis=0, tiled=True)
    head_queries = qkv[:, :, :HD]
    own_key_values = qkv[:, :, HD:]
    key_values = group_exchange([own_key_values] * parts, parts)
    ffn_weight = lax.all_gather(after(ffn_shard_low, key_values[-1]), "seq", axis=0, tiled=True)
    mixed, mass = attention_forward(sizes, ints, floats, head_queries, key_values)

    everywhere = ("seq", "head")
    slices_out = lax.all_to_all(
        mixed.reshape(seq_count * head_count, sub, HD), everywhere, split_axis=0, concat_axis=0, tiled=True
    )
    heads_out = (
        slices_out.reshape(local_heads, parts, head_count, sub, HD)
        .transpose(1, 3, 2, 0, 4)
        .reshape(slice_rows, width)
    )
    mass_high = lax.reduce_precision(mass, 8, 7)
    mass_middle = lax.reduce_precision(mass - mass_high, 8, 7)
    mass_parts = jnp.stack([mass_high, mass_middle, mass - mass_high - mass_middle], axis=1).astype(LOW)
    mass_rows = block // HD
    mass_sent = jnp.pad(
        mass_parts.reshape(seq_count, mass_rows, 3 * HD), ((0, 0), (0, 16 - mass_rows), (0, 0))
    )

    attn_sum = dot(heads_out, out_weight, NT)
    resid_one = own_slice(tokens).astype(WIDE) + attn_sum
    scale_two = lax.rsqrt(jnp.mean(resid_one * resid_one, axis=-1, keepdims=True) + EPS)
    unit_two = resid_one * scale_two
    normed_slice = (unit_two * gain_values[1]).astype(LOW)
    cot_slices = by_slices(cotangent)
    first_slice, second_slice = halves(normed_slice)

    first_pieces, order = line_gather_pieces(first_slice)
    second_pieces, order = line_gather_pieces(second_slice)
    first_pieces[-1], *second_pieces = lax.optimization_barrier((first_pieces[-1], *second_pieces))
    normed_a, hidden_a, gate_a, up_a, two_a = feed_forward(
        first_pieces, order, cot_slices, 0, ffn_weight, hidden_width
    )
    second_pieces[-1] = after(second_pieces[-1], two_a)
    normed_b, hidden_b, gate_b, up_b, two_b = feed_forward(
        second_pieces, order, cot_slices, 1, ffn_weight, hidden_width
    )
    two_sum_a = slice_sum(two_a)
    two_sum_b = slice_sum(two_b)
    two_sum_a, hidden_a, hidden_b = lax.optimization_barrier((two_sum_a, hidden_a, hidden_b))
    ffn_raw = feed_forward_wgrad(
        (normed_a, normed_b), cot_slices, (gate_a, gate_b), (up_a, up_b), (hidden_a, hidden_b)
    )
    ffn_shard = lax.psum_scatter(ffn_raw, "seq", scatter_dimension=0, tiled=True)
    down_weight = ffn_weight[:, 2 * hidden_width :]
    def norm_grad(grad, unit, scale, gain, passed):
        inner = grad * gain
        return passed + scale * (inner - unit * jnp.mean(inner * unit, axis=-1, keepdims=True))

    two_sum_b = after(two_sum_b, ffn_raw)
    cot_own = own_slice(cotangent).astype(WIDE)
    resid_grads = [
        norm_grad(*args, gain_values[1], passed)
        for args, passed in zip(
            zip((two_sum_a, two_sum_b), halves(unit_two), halves(scale_two)), halves(cot_own)
        )
    ]
    branch_low = jnp.concatenate([r.astype(LOW) for r in resid_grads], axis=0)
    heads_grad = dot(branch_low, out_weight).astype(LOW)

    grads_sent = (
        heads_grad.reshape(parts, sub, head_count, local_heads, HD)
        .transpose(3, 0, 2, 1, 4)
        .reshape(seq_count * head_count, sub, HD)
    )
    head_grads = lax.all_to_all(
        grads_sent, everywhere, split_axis=0, concat_axis=0, tiled=True
    ).reshape(seq_count, block, HD)
    out_raw = dot(branch_low, heads_out, TN).astype(LOW)
    out_mine = lax.psum_scatter(out_raw, "seq", scatter_dimension=0, tiled=True)
    hidden_a, hidden_b, grads_sent = lax.optimization_barrier((hidden_a, hidden_b, grads_sent))
    ffn_part = jnp.stack(
        [dot(hidden_a, down_weight, NT).astype(LOW), dot(hidden_b, down_weight, NT).astype(LOW)]
    )
    ffn_terms = direct_terms(
        after(ffn_part, head_grads).reshape(2, head_count, quarter_rows, width)
    )
    early_terms, late_terms = ffn_terms[:3], ffn_terms[3:]
    q_grad, *kv_grads = attention_backward(sizes, ints, floats, head_queries, head_grads, key_values)
    kv_grads, early_terms = lax.optimization_barrier((kv_grads, early_terms))
    kv_terms = group_exchange(kv_grads, parts)
    kv_sum = functools.reduce(lambda a, b: a + b, [t.astype(WIDE) for t in kv_terms]).astype(LOW)
    returned = lax.all_to_all(
        jnp.concatenate([jnp.concatenate([q_grad, kv_sum], axis=2), mass_sent], axis=1),
        "seq",
        split_axis=0,
        concat_axis=0,
        tiled=True,
    )
    ffn_sum = added(*early_terms, *late_terms).reshape(slice_rows, width)
    layer_slice = (resid_one + ffn_sum).astype(LOW).reshape(parts, sub, width)
    line = head_count == 4
    layer_one = gather_step_one(layer_slice) if line else ()
    returned, layer_one = lax.optimization_barrier((returned, layer_one))
    grads_back = returned[:, :block]
    mass_got = returned[:, block : block + mass_rows].astype(WIDE).reshape(local_heads, parts, 3, block)
    attn_mass = jnp.sum(mass_got, axis=2).reshape(local_heads, local_rows)
    qkv_grad = (
        grads_back.reshape(local_heads, parts, block, 3 * HD)
        .transpose(1, 2, 0, 3)
        .reshape(local_rows, 3 * head_width)
    )

    one_grad_part = (
        dot(qkv_grad, qkv_weight, NT).astype(LOW).reshape(parts, head_count, sub, width)
    )
    if line:
        forward = jnp.arange(4, dtype=jnp.int32)
        order = jnp.where(head_index < 2, forward, 3 - forward)
        terms = [lax.dynamic_index_in_dim(one_grad_part, order[k], 1, False) for k in range(4)]
        got = line_sum_begin(terms)
        first, qkv_grad = lax.optimization_barrier((got[0], qkv_grad))
        normed_one_grad = line_sum_end(terms, (first,) + got[1:])
    else:
        normed_one_grad = lax.psum_scatter(
            one_grad_part, "head", scatter_dimension=1, tiled=True
        ).astype(WIDE)
    qkv_raw = dot(normed_one, qkv_grad, TN).astype(LOW)
    qkv_raw, ffn_shard, out_mine = lax.optimization_barrier((qkv_raw, ffn_shard, out_mine))
    qkv_mine = lax.psum_scatter(qkv_raw, "seq", scatter_dimension=0, tiled=True)
    normed_one_grad, out_mine = lax.optimization_barrier((normed_one_grad, out_mine))
    out_terms = jnp.stack(
        [out_mine[:, j * head_width : (j + 1) * head_width] for j in range(head_count)]
    )
    out_own = added(*direct_terms(out_terms[None])).astype(LOW)[0]
    normed_one_grad = normed_one_grad.reshape(slice_rows, width)
    own_scale = own_slice(scale_one)
    unit_one = own_slice(tokens).astype(WIDE) * own_scale
    input_slice = norm_grad(
        normed_one_grad, unit_one, own_scale, gain_values[0], jnp.concatenate(resid_grads, axis=0)
    )
    input_slice = input_slice.astype(LOW).reshape(parts, sub, width)
    input_one = gather_step_one(input_slice) if line else ()
    layer_two = gather_step_two(layer_one) if line else ()
    input_one, layer_two, out_own = lax.optimization_barrier((input_one, layer_two, out_own))
    input_two = gather_step_two(input_one) if line else ()
    layer_three = gather_step_three(layer_two) if line else ()
    own_gain = gain_master.astype(LOW).astype(WIDE)
    qkv_wide = qkv_mine.astype(WIDE)
    ffn_wide = ffn_shard.astype(WIDE)
    gain_two_term = (
        jnp.sum(
            ffn_shard_low[:, : 2 * hidden_width].astype(WIDE) * ffn_wide[:, : 2 * hidden_width], axis=1
        )
        / own_gain[1]
    )
    gain_one_term = jnp.sum(qkv_shard.astype(WIDE) * qkv_wide, axis=1) / own_gain[0]
    out_wide = out_own.astype(WIDE)
    squares = jnp.sum(ffn_wide * ffn_wide) + jnp.sum(out_wide * out_wide) + jnp.sum(qkv_wide * qkv_wide)
    row = jnp.arange(2 * seq_count + 8, dtype=jnp.int32)[:, None]
    small = jnp.where(
        row == seq_index,
        gain_one_term[None, :],
        jnp.where(
            row == seq_count + seq_index,
            gain_two_term[None, :],
            jnp.where(row == 2 * seq_count, squares / shard_rows, 0.0),
        ),
    )
    small = sum_everywhere(small)
    gain_all = small[: 2 * seq_count]
    gain_shard = jnp.stack(
        [
            lax.dynamic_index_in_dim(gain_all, seq_index, 0, False),
            lax.dynamic_index_in_dim(gain_all, seq_count + seq_index, 0, False),
        ]
    )
    grad_norm = jnp.sqrt(jnp.sum(small[2 * seq_count]) + jnp.sum(gain_all * gain_all))
    clip_factor = jnp.minimum(1.0, CLIP / (grad_norm + 1e-06))

    attn_grads = jnp.concatenate(
        [
            qkv_mine.reshape(shard_rows, local_heads, 3, HD)
            .transpose(0, 2, 1, 3)
            .reshape(shard_rows, 3 * head_width),
            out_own,
        ],
        axis=1,
    )
    input_two, layer_three, clip_factor, attn_grads = lax.optimization_barrier(
        (input_two, layer_three, clip_factor, attn_grads)
    )
    input_three = gather_step_three(input_two) if line else ()
    blank = jnp.zeros((parts, block, width), WIDE)
    layer_output = line_gather_wide(blank, layer_slice, (layer_one, layer_two, layer_three))
    layer_output = layer_output.reshape(local_rows, width)
    input_grad = line_gather_wide(blank, input_slice, (input_one, input_two, input_three))
    input_grad = input_grad.reshape(local_rows, width)
    gain_grad = gain_shard * clip_factor
    ffn_state = adam_arrays(clip_factor, ffn_shard, ffn_first, ffn_second, ffn_master)
    attn_state = adam_arrays(clip_factor, attn_grads, attn_first, attn_second, attn_master)
    gain_state = adam_update(gain_grad, gain_first, gain_second, gain_master, GAIN_RATE)
    return (
        layer_output,
        input_grad,
        attn_mass,
        grad_norm,
        attn_state[0],
        attn_state[1],
        attn_state[2],
        attn_state[3],
        attn_state[4],
        ffn_state[0],
        ffn_state[1],
        ffn_state[2],
        ffn_state[3],
        ffn_state[4],
        gain_grad,
        gain_state[0],
        gain_state[1],
        gain_state[2],
        gain_state[3],
    )


def solution(mesh):
    in_specs = (
        P("seq", None),
        P("seq", None),
        P(),
        P(None, "seq", "head"),
        P(None, "seq", "head"),
        P(None, "seq"),
        P(None, "seq", "head"),
        P(None, "seq", "head"),
        P(None, "seq", "head"),
        P(None, "seq", "head"),
        P(None, "seq"),
        P(None, "seq"),
    )
    out_specs = (
        P("seq", None),
        P("seq", None),
        P("head", "seq"),
        P(),
        P(None, "seq", "head"),
        P(None, "seq", "head"),
        P(None, "seq", "head"),
        P(None, "seq", "head"),
        P(None, "seq", "head"),
        P(None, "seq", "head"),
        P(None, "seq", "head"),
        P(None, "seq", "head"),
        P(None, "seq", "head"),
        P(None, "seq", "head"),
        P(None, "seq"),
        P(None, "seq"),
        P(None, "seq"),
        P(None, "seq"),
        P(None, "seq"),
    )
    return jax.shard_map(
        per_device, mesh=mesh, in_specs=in_specs, out_specs=out_specs, check_vma=False
    )
```

time: 1400 us -> 981 us (0.70)
  waiting for transfers between devices: 602 us -> 295 us
  Pallas kernels: 106 us -> 228 us
  matrix products: 166 us -> 63.8 us
  blocking collectives: 129 us -> 60.5 us
  local copies, waits for them, and re-layouts: 115 us -> 64.5 us
  other arithmetic: 105 us -> 81.1 us
    ppermute x48 -> x40, waiting for transfers between devices: 473 us -> 203 us  [the longest x6 64.9 us: direct_terms(): lax.ppermute(lax.dynamic_index_in_dim(terms, at ^ k, 1, False), 'head', [...]
    pallas_call x2 -> x7, Pallas kernels: 106 us -> 228 us  [the longest x1 71.4 us: attention_backward(): pl.pallas_call(functools.partial(backward_kernel, sizes), out_shape=[jax....]
    dot_general x15 -> x8, matrix products: 166 us -> 63.8 us  [dot(): return lax.dot_general(left, right, dims, preferred_element_type=WIDE)]
    psum x1 -> x0, blocking collectives: 50 us -> none  [per_device(): small = lax.psum(small, ('seq', 'head'))]
    unnamed x98 -> x133, local copies, waits for them, and re-layouts: 65.5 us -> 22.5 us
    all_to_all x4 -> x5, waiting for transfers between devices: 73.7 us -> 46.8 us  [the longest x1 23.5 us: per_device(): lax.all_to_all(mixed.reshape(seq_count * head_count, sub, HD), everywhere...]
    dynamic_update_slice x2 -> x12, other arithmetic: 0.27 us -> 25.9 us  [line_gather_wide(): lax.dynamic_update_slice(full, jnp.where(there, part, piece).astype(WIDE)...]
    convert_element_type x3 -> x1, other arithmetic: 24.6 us -> 0.62 us  [adam_update(): return (first_new, second_new, master_new, master_new.astype(LOW))]
  transfers between devices with their start and end apart: 58 -> 53, of which waited for: 35 -> 32; matrix products, arithmetic and copies ran while one was open for 14% -> 16% of each run, Pallas kernels for 3% -> 20%
where the time goes in v2:
time: 981 us; the launch traced here: 970 us
  waiting for transfers between devices  295 us (30%)
  Pallas kernels  228 us (23%)
  starting transfers between devices  149 us (15%)
  other arithmetic  81.1 us (8%)
  local copies, waits for them, and re-layouts  64.5 us (7%)
  matrix products  63.8 us (7%)
  blocking collectives  60.5 us (6%)
  between operations  28.3 us (3%)
    pallas_call x1, Pallas kernels, attention_backward(): pl.pallas_call(functools.partial(backward_kernel, sizes), out_shape=[jax....  71.4 us
    pallas_call x2, Pallas kernels, feed_forward(): pl.pallas_call(functools.partial(ffn_kernel, len(pieces)), out_shape=[ful...  66.7 us
    ppermute x6, waiting for transfers between devices, direct_terms(): lax.ppermute(lax.dynamic_index_in_dim(terms, at ^ k, 1, False), 'head', [...  64.9 us
    dot_general x8, matrix products, dot(): return lax.dot_general(left, right, dims, preferred_element_type=WIDE)  63.8 us
    all_to_all x1, blocking collectives, per_device(): qkv = lax.all_to_all(sent, 'seq', split_axis=0, concat_axis=0, tiled=True)  51.6 us
    pallas_call x1, Pallas kernels, feed_forward_wgrad(): pl.pallas_call(functools.partial(ffn_wgrad_kernel, steps), out_shape=jax....  37.8 us
    pallas_call x1, Pallas kernels, attention_forward(): pl.pallas_call(functools.partial(forward_kernel, sizes), out_shape=[jax.S...  35.8 us
    dynamic_update_slice x12, other arithmetic, line_gather_wide(): lax.dynamic_update_slice(full, jnp.where(there, part, piece).astype(WIDE)...  25.9 us
  transfers between devices with their start and end apart: 53, of which 32 were waited for; matrix products, arithmetic and copies ran while one was open for 16% of the time, Pallas kernels for 20%

profile of v2, /device:TPU:8, one launch (start us, length us, event | category | flops | bytes accessed | tf_op | source)
XLA Modules:
  0.0 970.4 jit_solution(6360042208118233619)
XLA Ops:
  18.6 8.9 all_gather.12
  37.5 20.5 %all-gather.4.cloned.1.call-done = bf16[2048,1536]{0,1:T(8,128)(2,1)} async-done(((bf16[256,1536]{0,1:T(8,128)(2,1)}), bf16[2048,1536]{0,1:T(8,128)(2,1)}) %all-gather.4.cloned.1.call-update) | async-done | bytes 6291472 | tf_op jit(solution)/shard_map/all_gather | solution.py:666
  58.0 11.3 %multiply_convert_fusion = bf16[1024,1536]{1,0:T(8,128)(2,1)} fusion(bf16[2048,1536]{0,1:T(8,128)(2,1)} %all-gather.4.cloned.1.call-done, f32[1536]{0:T(1024)S(1)} %fusion.35, bf16[1024,2048]{1,0:T(8,128)(2,1)} %param.12, f32[2048]{0:T(1024)S(1)} %bitcast.178, f32[1024]{0:T(1024)S(1)} %add_rsqrt_fusion), kind=kOutput, calls=%fused_computation.14 | convolution fusion | flops 6453985280 | bytes 13649920 | tf_op jit(solution)/shard_map/dot_general | solution.py:35
  77.9 51.6 %all_to_all.38 = bf16[8,512,384]{2,1,0:T(8,128)(2,1)S(1)} all-to-all(bf16[8,512,384]{2,1,0:T(8,128)(2,1)S(1)} %bitcast.152), channel_id=1, replica_groups=mesh['seq'=8,'head'=4] {'seq'}, dimensions={0} | all-to-all | bytes 6291456 | tf_op jit(solution)/shard_map/all_to_all | solution.py:687
  141.3 35.8 %attention_forward.1 = (bf16[8,512,128]{2,1,0:T(8,128)(2,1)}, f32[8,1,512]{2,1,0:T(1,128)S(1)}) custom-call(s32[2]{0:T(128)S(1)} %pad_add_fusion.ints, f32[6]{0:T(128)S(1)} %reshape.399.floats, bf16[8,512,128]{2,1,0:T(8,128)(2,1)S(1)} %slice.197.q_ref, bf16[8,512,256]{2,1,0:T(8,128)(2,1)S(1)} %slice.198.rest_0_, ...), custom_call_target="tpu_custom_call" | custom-call | flops 17179869184 | bytes 8388608 | tf_op jit(solution)/shard_map/attention_forward/pallas_call | solution.py:135
  184.5 23.5 %all-to-all-done.1 = bf16[32,128,128]{2,1,0:T(8,128)(2,1)S(1)} async-done(((bf16[32,128,128]{2,1,0:T(8,128)(2,1)}), bf16[32,128,128]{2,1,0:T(8,128)(2,1)S(1)}, u32[]{:S(2)}, u32[]{:S(2)}) %all-to-all-start.1) | async-done | bytes 1048608 | tf_op jit(solution)/shard_map/all_to_all | solution.py:695
  209.7 6.8 multiply_reduce_fusion.2
  281.7 8.8 collective-permute-done.8.refs_5_
  296.2 33.3 %feed_forward.2 = (bf16[512,2048]{1,0:T(8,128)(2,1)}, bf16[512,2048]{1,0:T(8,128)(2,1)}, bf16[512,2048]{1,0:T(8,128)(2,1)}, bf16[512,2048]{1,0:T(8,128)(2,1)}, bf16[512,2048]{1,0:T(8,128)(2,1)}) custom-call(s32[4]{0:T(128)} %compare_select_fusion.3.table, bf16[128,2048]{1,0:T(8,128)(2,1)} %copy-done.40, bf16[128,2048]{1,0:T(8,128)(2,1)} %collective-permute-done.4.refs_1_, ...), custom_call_target="tpu_custom_call" | custom-call | flops 21474836480 | bytes 25165824 | tf_op jit(solution)/shard_map/feed_forward/pallas_call | solution.py:334
  334.8 33.4 %feed_forward.3 = (bf16[512,2048]{1,0:T(8,128)(2,1)}, bf16[512,2048]{1,0:T(8,128)(2,1)}, bf16[512,2048]{1,0:T(8,128)(2,1)}, bf16[512,2048]{1,0:T(8,128)(2,1)}, bf16[512,2048]{1,0:T(8,128)(2,1)}) custom-call(s32[4]{0:T(128)} %compare_select_fusion.3.table, bf16[128,2048]{1,0:T(8,128)(2,1)} %copy-done.39, bf16[128,2048]{1,0:T(8,128)(2,1)} %collective-permute-done.9.refs_1_, ...), custom_call_target="tpu_custom_call" | custom-call | flops 21474836480 | bytes 25165824 | tf_op jit(solution)/shard_map/feed_forward/pallas_call | solution.py:334
  368.1 12.1 %all-to-all-done.2 = bf16[4,128,2048]{2,1,0:T(8,128)(2,1)} async-done(((bf16[4,128,2048]{2,1,0:T(8,128)(2,1)}), bf16[4,128,2048]{2,1,0:T(8,128)(2,1)}, u32[]{:S(2)}, u32[]{:S(2)}) %all-to-all-start.2) | async-done | bytes 2097184 | tf_op jit(solution)/shard_map/all_to_all | solution.py:457
  380.2 7.8 all-to-all-start.3
  388.0 8.3 reduce-scatter.6.cloned.1.call-start
  400.9 37.8 %feed_forward_wgrad.1 = bf16[2048,6144]{1,0:T(8,128)(2,1)} custom-call(bf16[512,2048]{1,0:T(8,128)(2,1)} %get-tuple-element.106.n_a, bf16[512,2048]{1,0:T(8,128)(2,1)} %get-tuple-element.107.n_b, bf16[1024,2048]{1,0:T(8,128)(2,1)} %c_ref.1, bf16[512,2048]{1,0:T(8,128)(2,1)} %get-tuple-element.108.gate_a, bf16[512,2048]{1,0:T(8,128)(2,1)} %get-tuple-element.109.gate_b, ...), custom_call_target="tpu_custom_call" | custom-call | flops 2097152 | bytes 2097152 | tf_op jit(solution)/shard_map/feed_forward_wgrad/pallas_call | solution.py:401
  451.0 6.7 convolution_convert_fusion.3
  465.9 8.5 fusion.19
  474.4 8.8 fusion.16
  485.6 6.7 all-to-all-done.4
  498.3 71.4 %attention_backward.1 = (bf16[8,512,128]{2,1,0:T(8,128)(2,1)}, bf16[8,512,256]{2,1,0:T(8,128)(2,1)}, bf16[8,512,256]{2,1,0:T(8,128)(2,1)}) custom-call(s32[2]{0:T(128)} %copy-done.11, f32[6]{0:T(128)} %copy-done.10, bf16[8,512,128]{2,1,0:T(8,128)(2,1)} %copy-done.9, bf16[8,512,128]{2,1,0:T(8,128)(2,1)} %bitcast.174, bf16[8,512,256]{2,1,0:T(8,128)(2,1)} %copy-done.6, ...), custom_call_target="tpu_custom_call" | custom-call | flops 214748364800 | bytes 16777216 | tf_op jit(solution)/shard_map/attention_backward/pallas_call | solution.py:231
  583.1 35.8 %collective-permute-done.16 = bf16[2,128,2048]{2,1,0:T(8,128)(2,1)} collective-permute-done((bf16[2,128,2048]{2,1,0:T(8,128)(2,1)}, bf16[2,128,2048]{2,1,0:T(8,128)(2,1)}, u32[]{:S(2)}, u32[]{:S(2)}) %collective-permute-start.16) | collective-permute-done | bytes 1048608 | tf_op jit(solution)/shard_map/ppermute | solution.py:562
  637.0 11.7 %collective-permute-done.18 = bf16[2,128,2048]{2,1,0:T(8,128)(2,1)} collective-permute-done((bf16[2,128,2048]{2,1,0:T(8,128)(2,1)S(1)}, bf16[2,128,2048]{2,1,0:T(8,128)(2,1)}, u32[]{:S(2)}, u32[]{:S(2)}) %collective-permute-start.18) | collective-permute-done | bytes 1048608 | tf_op jit(solution)/shard_map/ppermute | solution.py:491
  662.3 6.9 convolution_convert_fusion.2
  673.2 22.4 %collective-permute-done.21 = bf16[2,128,2048]{2,1,0:T(8,128)(2,1)} collective-permute-done((bf16[2,128,2048]{2,1,0:T(8,128)(2,1)S(1)}, bf16[2,128,2048]{2,1,0:T(8,128)(2,1)}, u32[]{:S(2)}, u32[]{:S(2)}) %collective-permute-start.21) | collective-permute-done | bytes 1048608 | tf_op jit(solution)/shard_map/ppermute | solution.py:470
  695.6 9.1 convolution_convert_fusion.1
  704.7 16.4 %reduce-scatter.4.cloned.1.call-done.grad = bf16[256,6144]{1,0:T(8,128)(2,1)} async-done(((bf16[2048,6144]{1,0:T(8,128)(2,1)}), bf16[256,6144]{1,0:T(8,128)(2,1)}) %reduce-scatter.4.cloned.1.call-update) | async-done | bytes 3145744 | tf_op jit(solution)/shard_map/reduce_scatter | solution.py:735
  741.8 10.3 %collective-permute-done.24 = bf16[2,128,2048]{2,1,0:T(8,128)(2,1)S(1)} collective-permute-done((bf16[2,128,2048]{2,1,0:T(8,128)(2,1)S(1)}, bf16[2,128,2048]{2,1,0:T(8,128)(2,1)S(1)}, u32[]{:S(2)}, u32[]{:S(2)}) %collective-permute-start.24) | collective-permute-done | bytes 1048608 | tf_op jit(solution)/shard_map/ppermute | solution.py:472
  759.2 17.2 %collective-permute-done.20 = bf16[2,128,2048]{2,1,0:T(8,128)(2,1)S(1)} collective-permute-done((bf16[2,128,2048]{2,1,0:T(8,128)(2,1)S(1)}, bf16[2,128,2048]{2,1,0:T(8,128)(2,1)S(1)}, u32[]{:S(2)}, u32[]{:S(2)}) %collective-permute-start.20) | collective-permute-done | bytes 1048608 | tf_op jit(solution)/shard_map/ppermute | solution.py:471
  782.8 20.7 %collective-permute-done.25 = bf16[2,128,2048]{2,1,0:T(8,128)(2,1)S(1)} collective-permute-done((bf16[2,128,2048]{2,1,0:T(8,128)(2,1)S(1)}, bf16[2,128,2048]{2,1,0:T(8,128)(2,1)S(1)}, u32[]{:S(2)}, u32[]{:S(2)}) %collective-permute-start.25) | collective-permute-done | bytes 1048608 | tf_op jit(solution)/shard_map/ppermute | solution.py:481
  826.1 24.6 %collective-permute-done.31 = bf16[1,256,512]{2,1,0:T(8,128)(2,1)S(1)} collective-permute-done((bf16[1,256,512]{2,1,0:T(8,128)(2,1)S(1)}, bf16[1,256,512]{2,1,0:T(8,128)(2,1)S(1)}, u32[]{:S(2)}, u32[]{:S(2)}) %collective-permute-start.31) | collective-permute-done | bytes 262176 | tf_op jit(solution)/shard_map/ppermute | solution.py:562
  850.7 8.9 collective-permute-start.32
  869.8 6.4 collective-permute-start.35
  937.3 12.1 %adam.3 = (f32[3,256,2048]{2,1,0:T(8,128)}, f32[3,256,2048]{2,1,0:T(8,128)}, f32[3,256,2048]{2,1,0:T(8,128)}, f32[3,256,2048]{2,1,0:T(8,128)}, bf16[3,256,2048]{2,1,0:T(8,128)(2,1)}) custom-call(f32[1]{0:T(128)} %bitcast.70.clip, bf16[256,6144]{1,0:T(8,128)(2,1)S(1)} %copy-done, f32[3,256,2048]{2,1,0:T(8,128)S(1)} %copy-done.2, ...), custom_call_target="tpu_custom_call" | custom-call | flops 31457280 | bytes 50331648 | tf_op jit(solution)/shard_map/adam/pallas_call | solution.py:438
  (345 shorter events, 338.1 us)
Async XLA Ops:
  7.2 50.8 %all-gather.4.cloned.1.call-start = ((), (), s32[]{:S(2)}) async-start(), calls=%async_computation.9 | async-start | bytes 7077888 | tf_op jit(solution)/shard_map/all_gather | solution.py:666
  10.0 199.7 %all-gather.6.cloned.1.call-start = ((), (), s32[]{:S(2)}) async-start(), calls=%async_computation.10 | async-start | bytes 9437184 | tf_op jit(solution)/shard_map/all_gather | solution.py:686
  14.4 23.1 %collective-permute-start.2 = (bf16[256,512]{0,1:T(8,128)(2,1)S(1)}, bf16[256,512]{0,1:T(8,128)(2,1)S(1)}, u32[]{:S(2)}, u32[]{:S(2)}) collective-permute-start(bf16[256,512]{0,1:T(8,128)(2,1)S(1)} %bitcast.173), channel_id=1, source_target_pairs={{0,3},{1,2},{2,1},{3,0},{4,7},{5,6},{6,5},{7,4},{8,11},{9,10},{10,... | collective-permute-start | bytes 786440 | tf_op jit(solution)/shard_map/ppermute | solution.py:576
  77.8 218.4 %all-gather.8.cloned.1.call-start = ((), (), s32[]{:S(2)}) async-start(), calls=%async_computation.11 | async-start | bytes 28311552 | tf_op jit(solution)/shard_map/all_gather | solution.py:691
  177.1 30.9 %all-to-all-start.1 = ((bf16[32,128,128]{2,1,0:T(8,128)(2,1)}), bf16[32,128,128]{2,1,0:T(8,128)(2,1)S(1)}, u32[]{:S(2)}, u32[]{:S(2)}) async-start(bf16[32,128,128]{2,1,0:T(8,128)(2,1)} %bitcast.17), calls=%async_computation.1 | async-start | bytes 2097152 | tf_op jit(solution)/shard_map/all_to_all | solution.py:695
  329.6 50.6 %all-to-all-start.2 = ((bf16[4,128,2048]{2,1,0:T(8,128)(2,1)}), bf16[4,128,2048]{2,1,0:T(8,128)(2,1)}, u32[]{:S(2)}, u32[]{:S(2)}) async-start(bf16[4,128,2048]{2,1,0:T(8,128)(2,1)} %bitcast.169), calls=%async_computation.2 | async-start | bytes 4194304 | tf_op jit(solution)/shard_map/all_to_all | solution.py:457
  380.2 58.5 %all-to-all-start.3 = ((bf16[4,128,2048]{2,1,0:T(8,128)(2,1)}), bf16[4,128,2048]{2,1,0:T(8,128)(2,1)}, u32[]{:S(2)}, u32[]{:S(2)}) async-start(bf16[4,128,2048]{2,1,0:T(8,128)(2,1)} %bitcast.168), calls=%async_computation.3 | async-start | bytes 4194304 | tf_op jit(solution)/shard_map/all_to_all | solution.py:457
  388.0 316.7 %reduce-scatter.6.cloned.1.call-start = ((), (), s32[]{:S(2)}) async-start(), calls=%async_computation.13 | async-start | bytes 9437184 | tf_op jit(solution)/shard_map/reduce_scatter | solution.py:761
  449.8 271.3 %reduce-scatter.4.cloned.1.call-start = ((), (), s32[]{:S(2)}) async-start(), calls=%async_computation.12 | async-start | bytes 28311552 | tf_op jit(solution)/shard_map/reduce_scatter | solution.py:735
  461.1 31.2 %all-to-all-start.4 = ((bf16[32,128,128]{2,1,0:T(8,128)(2,1)}), bf16[32,128,128]{2,1,0:T(8,128)(2,1)S(1)}, u32[]{:S(2)}, u32[]{:S(2)}) async-start(bf16[32,128,128]{2,1,0:T(8,128)(2,1)} %bitcast.33), calls=%async_computation.4 | async-start | bytes 2097152 | tf_op jit(solution)/shard_map/all_to_all | solution.py:757
  497.1 72.6 %collective-permute-start.14 = (bf16[2,128,2048]{2,1,0:T(8,128)(2,1)}, bf16[2,128,2048]{2,1,0:T(8,128)(2,1)}, u32[]{:S(2)}, u32[]{:S(2)}) collective-permute-start(bf16[2,128,2048]{2,1,0:T(8,128)(2,1)} %get-tuple-element.184), channel_id=1, source_target_pairs={{0,1},{1,0},{2,3},{3,2},{4,5},{5,4},{6,7},{7,6},{8,9},{9,8},{10,11... | collective-permute-start | bytes 3145736 | tf_op jit(solution)/shard_map/ppermute | solution.py:562
  497.1 72.6 %collective-permute-start.15 = (bf16[2,128,2048]{2,1,0:T(8,128)(2,1)}, bf16[2,128,2048]{2,1,0:T(8,128)(2,1)}, u32[]{:S(2)}, u32[]{:S(2)}) collective-permute-start(bf16[2,128,2048]{2,1,0:T(8,128)(2,1)} %get-tuple-element.182), channel_id=1, source_target_pairs={{0,2},{1,3},{2,0},{3,1},{4,6},{5,7},{6,4},{7,5},{8,10},{9,11},{10,... | collective-permute-start | bytes 3145736 | tf_op jit(solution)/shard_map/ppermute | solution.py:562
  570.0 48.9 %collective-permute-start.16 = (bf16[2,128,2048]{2,1,0:T(8,128)(2,1)}, bf16[2,128,2048]{2,1,0:T(8,128)(2,1)}, u32[]{:S(2)}, u32[]{:S(2)}) collective-permute-start(bf16[2,128,2048]{2,1,0:T(8,128)(2,1)} %get-tuple-element.183), channel_id=1, source_target_pairs={{0,3},{1,2},{2,1},{3,0},{4,7},{5,6},{6,5},{7,4},{8,11},{9,10},{10,... | collective-permute-start | bytes 3145736 | tf_op jit(solution)/shard_map/ppermute | solution.py:562
  578.2 78.6 %all-to-all-start.5 = ((bf16[8,528,384]{2,1,0:T(8,128)(2,1)}), bf16[8,528,384]{2,1,0:T(8,128)(2,1)}, u32[]{:S(2)}, u32[]{:S(2)}) async-start(bf16[8,528,384]{2,1,0:T(8,128)(2,1)} %fusion.9), calls=%async_computation.5 | async-start | bytes 6488064 | tf_op jit(solution)/shard_map/all_to_all | solution.py:774
  582.9 299.7 %reduce-scatter.8.cloned.1.call-start = ((), (), s32[]{:S(2)}) async-start(), calls=%async_computation.14 | async-start | bytes 7077888 | tf_op jit(solution)/shard_map/reduce_scatter | solution.py:811
  621.8 27.0 %collective-permute-start.18 = (bf16[2,128,2048]{2,1,0:T(8,128)(2,1)S(1)}, bf16[2,128,2048]{2,1,0:T(8,128)(2,1)}, u32[]{:S(2)}, u32[]{:S(2)}) collective-permute-start(bf16[2,128,2048]{2,1,0:T(8,128)(2,1)S(1)} %bitcast.139), channel_id=1, source_target_pairs={{0,1},{1,2},{2,3},{4,5},{5,6},{6,7},{8,9},{9,10},{10,11},{12,13},{... | collective-permute-start | bytes 3145736 | tf_op jit(solution)/shard_map/ppermute | solution.py:491
  625.4 26.8 %collective-permute-start.19 = (bf16[2,128,2048]{2,1,0:T(8,128)(2,1)S(1)}, bf16[2,128,2048]{2,1,0:T(8,128)(2,1)}, u32[]{:S(2)}, u32[]{:S(2)}) collective-permute-start(bf16[2,128,2048]{2,1,0:T(8,128)(2,1)S(1)} %bitcast.140), channel_id=1, source_target_pairs={{3,2},{2,1},{1,0},{7,6},{6,5},{5,4},{11,10},{10,9},{9,8},{15,14},{... | collective-permute-start | bytes 3145736 | tf_op jit(solution)/shard_map/ppermute | solution.py:492
  671.9 23.7 %collective-permute-start.21 = (bf16[2,128,2048]{2,1,0:T(8,128)(2,1)S(1)}, bf16[2,128,2048]{2,1,0:T(8,128)(2,1)}, u32[]{:S(2)}, u32[]{:S(2)}) collective-permute-start(bf16[2,128,2048]{2,1,0:T(8,128)(2,1)S(1)} %get-tuple-element.181), channel_id=1, source_target_pairs={{0,1},{3,2},{4,5},{7,6},{8,9},{11,10},{12,13},{15,14},{16,17},{19,... | collective-permute-start | bytes 3145736 | tf_op jit(solution)/shard_map/ppermute | solution.py:470
  724.2 27.9 %collective-permute-start.24 = (bf16[2,128,2048]{2,1,0:T(8,128)(2,1)S(1)}, bf16[2,128,2048]{2,1,0:T(8,128)(2,1)S(1)}, u32[]{:S(2)}, u32[]{:S(2)}) collective-permute-start(bf16[2,128,2048]{2,1,0:T(8,128)(2,1)S(1)} %copy-done.29), channel_id=1, source_target_pairs={{0,1},{3,2},{4,5},{7,6},{8,9},{11,10},{12,13},{15,14},{16,17},{19,... | collective-permute-start | bytes 3145736 | tf_op jit(solution)/shard_map/ppermute | solution.py:472
  727.0 49.3 %collective-permute-start.20 = (bf16[2,128,2048]{2,1,0:T(8,128)(2,1)S(1)}, bf16[2,128,2048]{2,1,0:T(8,128)(2,1)S(1)}, u32[]{:S(2)}, u32[]{:S(2)}) collective-permute-start(bf16[2,128,2048]{2,1,0:T(8,128)(2,1)S(1)} %get-tuple-element.178), channel_id=1, source_target_pairs={{1,0},{2,3},{5,4},{6,7},{9,8},{10,11},{13,12},{14,15},{17,16},{18,... | collective-permute-start | bytes 3145736 | tf_op jit(solution)/shard_map/ppermute | solution.py:471
  731.8 48.9 %collective-permute-start.23 = (bf16[2,128,2048]{2,1,0:T(8,128)(2,1)S(1)}, bf16[2,128,2048]{2,1,0:T(8,128)(2,1)S(1)}, u32[]{:S(2)}, u32[]{:S(2)}) collective-permute-start(bf16[2,128,2048]{2,1,0:T(8,128)(2,1)S(1)} %copy-done.28), channel_id=1, source_target_pairs={{0,1},{3,2},{4,5},{7,6},{8,9},{11,10},{12,13},{15,14},{16,17},{19,... | collective-permute-start | bytes 3145736 | tf_op jit(solution)/shard_map/ppermute | solution.py:473
  733.1 134.3 %collective-permute-start.28 = (bf16[2,128,2048]{2,1,0:T(8,128)(2,1)}, bf16[2,128,2048]{2,1,0:T(8,128)(2,1)}, u32[]{:S(2)}, u32[]{:S(2)}) collective-permute-start(bf16[2,128,2048]{2,1,0:T(8,128)(2,1)} %collective-permute-done.18), channel_id=1, source_target_pairs={{1,2},{2,3},{5,6},{6,7},{9,10},{10,11},{13,14},{14,15},{17,18},{18... | collective-permute-start | bytes 3145736 | tf_op jit(solution)/shard_map/ppermute | solution.py:498
  739.3 43.5 %collective-permute-start.22 = (bf16[2,128,2048]{2,1,0:T(8,128)(2,1)S(1)}, bf16[2,128,2048]{2,1,0:T(8,128)(2,1)S(1)}, u32[]{:S(2)}, u32[]{:S(2)}) collective-permute-start(bf16[2,128,2048]{2,1,0:T(8,128)(2,1)S(1)} %add_convert_fusion.3), channel_id=1, source_target_pairs={{1,3},{2,0},{5,7},{6,4},{9,11},{10,8},{13,15},{14,12},{17,19},{18,... | collective-permute-start | bytes 3145736 | tf_op jit(solution)/shard_map/ppermute | solution.py:480
  752.5 51.0 %collective-permute-start.25 = (bf16[2,128,2048]{2,1,0:T(8,128)(2,1)S(1)}, bf16[2,128,2048]{2,1,0:T(8,128)(2,1)S(1)}, u32[]{:S(2)}, u32[]{:S(2)}) collective-permute-start(bf16[2,128,2048]{2,1,0:T(8,128)(2,1)S(1)} %add_convert_fusion.2), channel_id=1, source_target_pairs={{1,2},{2,1},{5,6},{6,5},{9,10},{10,9},{13,14},{14,13},{17,18},{18,... | collective-permute-start | bytes 3145736 | tf_op jit(solution)/shard_map/ppermute | solution.py:481
  776.3 91.1 %collective-permute-start.29 = (bf16[2,128,2048]{2,1,0:T(8,128)(2,1)}, bf16[2,128,2048]{2,1,0:T(8,128)(2,1)}, u32[]{:S(2)}, u32[]{:S(2)}) collective-permute-start(bf16[2,128,2048]{2,1,0:T(8,128)(2,1)} %collective-permute-done.19), channel_id=1, source_target_pairs={{2,1},{1,0},{6,5},{5,4},{10,9},{9,8},{14,13},{13,12},{18,17},{17,1... | collective-permute-start | bytes 3145736 | tf_op jit(solution)/shard_map/ppermute | solution.py:499
  813.9 53.5 %collective-permute-start.26 = (bf16[2,128,2048]{2,1,0:T(8,128)(2,1)}, bf16[2,128,2048]{2,1,0:T(8,128)(2,1)}, u32[]{:S(2)}, u32[]{:S(2)}) collective-permute-start(bf16[2,128,2048]{2,1,0:T(8,128)(2,1)} %get-tuple-element.167), channel_id=1, source_target_pairs={{0,1},{1,2},{2,3},{4,5},{5,6},{6,7},{8,9},{9,10},{10,11},{12,13},{... | collective-permute-start | bytes 3145736 | tf_op jit(solution)/shard_map/ppermute | solution.py:491
  818.3 49.1 %collective-permute-start.27 = (bf16[2,128,2048]{2,1,0:T(8,128)(2,1)}, bf16[2,128,2048]{2,1,0:T(8,128)(2,1)}, u32[]{:S(2)}, u32[]{:S(2)}) collective-permute-start(bf16[2,128,2048]{2,1,0:T(8,128)(2,1)} %get-tuple-element.167), channel_id=1, source_target_pairs={{3,2},{2,1},{1,0},{7,6},{6,5},{5,4},{11,10},{10,9},{9,8},{15,14},{... | collective-permute-start | bytes 3145736 | tf_op jit(solution)/shard_map/ppermute | solution.py:492
  823.3 27.3 %collective-permute-start.31 = (bf16[1,256,512]{2,1,0:T(8,128)(2,1)S(1)}, bf16[1,256,512]{2,1,0:T(8,128)(2,1)S(1)}, u32[]{:S(2)}, u32[]{:S(2)}) collective-permute-start(bf16[1,256,512]{2,1,0:T(8,128)(2,1)S(1)} %copy-done.50), channel_id=1, source_target_pairs={{0,2},{1,3},{2,0},{3,1},{4,6},{5,7},{6,4},{7,5},{8,10},{9,11},{10,... | collective-permute-start | bytes 786440 | tf_op jit(solution)/shard_map/ppermute | solution.py:562
  869.8 50.4 %collective-permute-start.35 = (bf16[2,128,2048]{2,1,0:T(8,128)(2,1)}, bf16[2,128,2048]{2,1,0:T(8,128)(2,1)}, u32[]{:S(2)}, u32[]{:S(2)}) collective-permute-start(bf16[2,128,2048]{2,1,0:T(8,128)(2,1)} %broadcast_select_fusion.1), channel_id=1, source_target_pairs={{2,3},{1,0},{6,7},{5,4},{10,11},{9,8},{14,15},{13,12},{18,19},{17,... | collective-permute-start | bytes 3145736 | tf_op jit(solution)/shard_map/ppermute | solution.py:505
  876.1 44.1 %collective-permute-start.33 = (bf16[2,128,2048]{2,1,0:T(8,128)(2,1)}, bf16[2,128,2048]{2,1,0:T(8,128)(2,1)}, u32[]{:S(2)}, u32[]{:S(2)}) collective-permute-start(bf16[2,128,2048]{2,1,0:T(8,128)(2,1)} %collective-permute-done.26), channel_id=1, source_target_pairs={{1,2},{2,3},{5,6},{6,7},{9,10},{10,11},{13,14},{14,15},{17,18},{18... | collective-permute-start | bytes 3145736 | tf_op jit(solution)/shard_map/ppermute | solution.py:498
  878.4 41.8 %collective-permute-start.34 = (bf16[2,128,2048]{2,1,0:T(8,128)(2,1)}, bf16[2,128,2048]{2,1,0:T(8,128)(2,1)}, u32[]{:S(2)}, u32[]{:S(2)}) collective-permute-start(bf16[2,128,2048]{2,1,0:T(8,128)(2,1)} %collective-permute-done.27), channel_id=1, source_target_pairs={{2,1},{1,0},{6,5},{5,4},{10,9},{9,8},{14,13},{13,12},{18,17},{17,1... | collective-permute-start | bytes 3145736 | tf_op jit(solution)/shard_map/ppermute | solution.py:499
  921.6 37.5 %collective-permute-start.41 = (bf16[2,128,2048]{2,1,0:T(8,128)(2,1)S(1)}, bf16[2,128,2048]{2,1,0:T(8,128)(2,1)S(1)}, u32[]{:S(2)}, u32[]{:S(2)}) collective-permute-start(bf16[2,128,2048]{2,1,0:T(8,128)(2,1)S(1)} %broadcast_select_fusion), channel_id=1, source_target_pairs={{2,3},{1,0},{6,7},{5,4},{10,11},{9,8},{14,15},{13,12},{18,19},{17,... | collective-permute-start | bytes 3145736 | tf_op jit(solution)/shard_map/ppermute | solution.py:505
  (84 other events, 1331.7 us)
Sparse Core Ops, SparseCore 0:
  10.1 47.8 all-gather.3
  78.0 79.0 all-gather.5
  159.6 136.6 all-gather.7
  449.9 75.5 reduce-scatter.5
  529.4 191.6 reduce-scatter.3
  725.3 61.7 reduce-scatter.7

commit v3 on v2

--- a/solution.py
+++ b/solution.py
@@ -69,8 +69,8 @@
     return extra.astype(LOW)
 
 
-def in_causal_order(sizes, part, shape, key_dim):
-    key_place = lax.broadcasted_iota(jnp.int32, shape, key_dim)
+def in_causal_order(sizes, part, shape, key_dim, first_key=0):
+    key_place = first_key + lax.broadcasted_iota(jnp.int32, shape, key_dim)
     query_place = part * sizes[2] + lax.broadcasted_iota(jnp.int32, shape, 1 - key_dim)
     return key_place <= query_place
 
@@ -166,9 +166,12 @@
 def backward_kernel(sizes, ints, floats, q_ref, grad_ref, *rest):
     count, parts, block = sizes
     tile = block * parts
+    chunk = min(256, tile)
     key_values = rest[:parts]
     q_grad_ref, *kv_grad_refs = rest[parts : 2 * parts + 1]
-    key_buf, value_buf, turned, query_buf, q_total, k_total, v_total, sem = rest[2 * parts + 1 :]
+    key_buf, value_buf, query_buf, q_turned, grad_turned, q_total, k_total, v_total, sem = rest[
+        2 * parts + 1 :
+    ]
     step = pl.program_id(0)
     cut, part = ints[0], ints[1]
 
@@ -182,29 +185,42 @@
         for copy in key_copies(sizes, part, key_values, key_buf, value_buf, sem):
             copy.wait()
 
-        def turn(at, carry):
-            keys = pl.ds(pl.multiple_of(at * tile, tile), tile)
-            turned[:, keys] = jnp.transpose(key_buf[keys, :HD])
-            return carry
-
-        lax.fori_loop(0, count, turn, 0)
-
     query_buf[:, :HD] = q_ref[...]
     query_buf[:, HD:] = query_columns(sizes, step, part, cut, floats)
+    q_turned[...] = jnp.transpose(q_ref[...])
+    grad_turned[...] = jnp.transpose(grad_ref[...])
     q_total[...] = jnp.zeros_like(q_total)
     first = jnp.where(step * tile >= cut, cut // tile, 0)
 
     def walk(at, masked):
-        keys = pl.ds(pl.multiple_of(at * tile, tile), tile)
-        exponent = dot(key_buf[keys, :], query_buf[...], NT)
-        weight = pl.reciprocal(1.0 + jnp.exp2(exponent), approx=True)
-        if masked:
-            weight = jnp.where(in_causal_order(sizes, part, (tile, block), 0), weight, 0.0)
-        weight_grad = dot(value_buf[keys, :], grad_ref[...], NT)
-        score_grad = (weight_grad * (weight * (1.0 - weight))).astype(LOW)
-        v_total[keys, :] += dot(weight.astype(LOW), grad_ref[...])
-        k_total[keys, :] += dot(score_grad, query_buf[:, :HD])
-        q_total[...] += dot(turned[:, keys], score_grad)
+        base = pl.multiple_of(at * tile, tile)
+
+        def products(place):
+            keys = pl.ds(base + place, chunk)
+            return (
+                dot(query_buf[...], key_buf[keys, :], NT),
+                dot(grad_ref[...], value_buf[keys, :], NT),
+            )
+
+        score_grads = []
+        following = products(0)
+        for place in range(0, tile, chunk):
+            exponent, weight_grad = following
+            if place + chunk < tile:
+                following = products(place + chunk)
+            weight = pl.reciprocal(1.0 + jnp.exp2(exponent), approx=True)
+            if masked:
+                weight = jnp.where(
+                    in_causal_order(sizes, part, (block, chunk), 1, place), weight, 0.0
+                )
+            score_grad = (weight_grad * (weight - weight * weight)).astype(LOW)
+            keys = pl.ds(base + place, chunk)
+            v_total[:, keys] += dot(grad_turned[...], weight.astype(LOW))
+            k_total[:, keys] += dot(q_turned[...], score_grad)
+            score_grads.append(score_grad)
+        q_total[...] += dot(
+            jnp.concatenate(score_grads, axis=1), key_buf[pl.ds(base, tile), :HD]
+        )
 
     def body(at, carry):
         walk(at, False)
@@ -212,7 +228,7 @@
 
     lax.fori_loop(first, step, body, 0)
     walk(step, True)
-    q_grad_ref[...] = (jnp.transpose(q_total[...]) * (1.0 / math.sqrt(HD))).astype(LOW)
+    q_grad_ref[...] = (q_total[...] * (1.0 / math.sqrt(HD))).astype(LOW)
 
     @pl.when(step == count - 1)
     def _():
@@ -220,8 +236,10 @@
             for at in range(count):
                 row = pl.multiple_of((at * parts + (part ^ other)) * block, block)
                 rows = pl.ds(row, block)
-                kv_grad_refs[other][at, :, :HD] = (k_total[rows, :] * (-math.log(2.0))).astype(LOW)
-                kv_grad_refs[other][at, :, HD:] = v_total[rows, :].astype(LOW)
+                kv_grad_refs[other][at, :, :HD] = jnp.transpose(
+                    k_total[:, rows] * (-math.log(2.0))
+                ).astype(LOW)
+                kv_grad_refs[other][at, :, HD:] = jnp.transpose(v_total[:, rows]).astype(LOW)
 
 
 def attention_backward(sizes, ints, floats, queries, grads, key_values):
@@ -246,11 +264,12 @@
             scratch_shapes=[
                 pltpu.VMEM((total_rows, 2 * HD), LOW),
                 pltpu.VMEM((total_rows, HD), LOW),
-                pltpu.VMEM((HD, total_rows), LOW),
                 pltpu.VMEM((block, 2 * HD), LOW),
-                pltpu.VMEM((HD, block), WIDE),
-                pltpu.VMEM((total_rows, HD), WIDE),
-                pltpu.VMEM((total_rows, HD), WIDE),
+                pltpu.VMEM((HD, block), LOW),
+                pltpu.VMEM((HD, block), LOW),
+                pltpu.VMEM((block, HD), WIDE),
+                pltpu.VMEM((HD, total_rows), WIDE),
+                pltpu.VMEM((HD, total_rows), WIDE),
                 pltpu.SemaphoreType.DMA((1,)),
             ],
         ),
@@ -465,24 +484,34 @@
     return functools.reduce(lambda a, b: a + b, [t.astype(WIDE) for t in terms])
 
 
-def line_sum_begin(terms):
-    inward = [(0, 1), (3, 2)]
-    far = lax.ppermute(terms[3], "head", inward)
-    outer = lax.ppermute(terms[0], "head", [(1, 0), (2, 3)])
-    middle = lax.ppermute(terms[2], "head", inward)
-    near = lax.ppermute(terms[1], "head", inward)
-    return far, outer, middle, near
-
-
-def line_sum_end(terms, got):
+INWARD = [(0, 1), (3, 2)]
+ACROSS = [(1, 2), (2, 1)]
+OUTWARD = [(1, 0), (2, 3)]
+
+
+def sum_step_one(terms):
+    return (lax.ppermute(terms[3], "head", INWARD),)
+
+
+def sum_step_two(terms, got):
+    far = added(got[0], terms[3]).astype(LOW)
+    return (lax.ppermute(terms[2], "head", INWARD), lax.ppermute(far, "head", ACROSS))
+
+
+def sum_step_three(terms, got):
+    middle = added(got[0], terms[2]).astype(LOW)
+    far = added(got[1], terms[0]).astype(LOW)
+    return (
+        lax.ppermute(terms[1], "head", INWARD),
+        lax.ppermute(middle, "head", ACROSS),
+        lax.ppermute(far, "head", OUTWARD),
+    )
+
+
+def sum_last(terms, got):
     at = lax.axis_index("head")
-    far, outer, middle, near = got
-    far_in = lax.ppermute(added(far, terms[3]).astype(LOW), "head", [(1, 3), (2, 0)])
-    middle_in = lax.ppermute(added(middle, terms[2]).astype(LOW), "head", [(1, 2), (2, 1)])
     return jnp.where(
-        (at == 0) | (at == 3),
-        added(terms[0], outer, far_in),
-        added(terms[1], near, middle_in),
+        (at == 0) | (at == 3), added(terms[0], got[2]), added(terms[1], got[0], got[1])
     )
 
 
@@ -782,7 +811,12 @@
     layer_slice = (resid_one + ffn_sum).astype(LOW).reshape(parts, sub, width)
     line = head_count == 4
     layer_one = gather_step_one(layer_slice) if line else ()
-    returned, layer_one = lax.optimization_barrier((returned, layer_one))
+    out_terms = (
+        out_mine.reshape(shard_rows, head_count, head_width)
+        .transpose(1, 0, 2)
+        .reshape(head_count, out_mine.size // head_count // width, width)
+    )
+    returned, layer_one, out_terms = lax.optimization_barrier((returned, layer_one, out_terms))
     grads_back = returned[:, :block]
     mass_got = returned[:, block : block + mass_rows].astype(WIDE).reshape(local_heads, parts, 3, block)
     attn_mass = jnp.sum(mass_got, axis=2).reshape(local_heads, local_rows)
@@ -792,28 +826,49 @@
         .reshape(local_rows, 3 * head_width)
     )
 
-    one_grad_part = (
-        dot(qkv_grad, qkv_weight, NT).astype(LOW).reshape(parts, head_count, sub, width)
-    )
+    one_grad_part = dot(qkv_grad, qkv_weight, NT).astype(LOW).reshape(parts, head_count, sub, width)
     if line:
         forward = jnp.arange(4, dtype=jnp.int32)
         order = jnp.where(head_index < 2, forward, 3 - forward)
-        terms = [lax.dynamic_index_in_dim(one_grad_part, order[k], 1, False) for k in range(4)]
-        got = line_sum_begin(terms)
-        first, qkv_grad = lax.optimization_barrier((got[0], qkv_grad))
-        normed_one_grad = line_sum_end(terms, (first,) + got[1:])
+        terms = [
+            jnp.concatenate(
+                [
+                    lax.dynamic_index_in_dim(one_grad_part, order[k], 1, False).reshape(
+                        slice_rows, width
+                    ),
+                    lax.dynamic_index_in_dim(out_terms, order[k], 0, False),
+                ],
+                axis=0,
+            )
+            for k in range(4)
+        ]
+        got = sum_step_one(terms)
+        layer_two = gather_step_two(layer_one)
+        got, layer_two, terms, qkv_grad = lax.optimization_barrier((got, layer_two, terms, qkv_grad))
+        got = sum_step_two(terms, got)
+        layer_three = gather_step_three(layer_two)
+        qkv_raw = dot(normed_one, qkv_grad, TN).astype(LOW)
+        got, layer_three, terms, qkv_raw, ffn_shard = lax.optimization_barrier(
+            (got, layer_three, terms, qkv_raw, ffn_shard)
+        )
+        got = sum_step_three(terms, got)
+        got, layer_three = lax.optimization_barrier((got, layer_three))
+        summed = sum_last(terms, got)
     else:
-        normed_one_grad = lax.psum_scatter(
-            one_grad_part, "head", scatter_dimension=1, tiled=True
+        layer_two = layer_three = ()
+        qkv_raw = dot(normed_one, qkv_grad, TN).astype(LOW)
+        summed = jnp.concatenate(
+            [
+                lax.psum_scatter(one_grad_part, "head", scatter_dimension=1, tiled=True).reshape(
+                    slice_rows, width
+                ),
+                lax.psum_scatter(out_terms, "head", scatter_dimension=0, tiled=False),
+            ],
+            axis=0,
         ).astype(WIDE)
-    qkv_raw = dot(normed_one, qkv_grad, TN).astype(LOW)
-    qkv_raw, ffn_shard, out_mine = lax.optimization_barrier((qkv_raw, ffn_shard, out_mine))
     qkv_mine = lax.psum_scatter(qkv_raw, "seq", scatter_dimension=0, tiled=True)
-    normed_one_grad, out_mine = lax.optimization_barrier((normed_one_grad, out_mine))
-    out_terms = jnp.stack(
-        [out_mine[:, j * head_width : (j + 1) * head_width] for j in range(head_count)]
-    )
-    out_own = added(*direct_terms(out_terms[None])).astype(LOW)[0]
+    normed_one_grad = summed[:slice_rows]
+    out_own = summed[slice_rows:].astype(LOW).reshape(shard_rows, head_width)
     normed_one_grad = normed_one_grad.reshape(slice_rows, width)
     own_scale = own_slice(scale_one)
     unit_one = own_slice(tokens).astype(WIDE) * own_scale
@@ -822,10 +877,7 @@
     )
     input_slice = input_slice.astype(LOW).reshape(parts, sub, width)
     input_one = gather_step_one(input_slice) if line else ()
-    layer_two = gather_step_two(layer_one) if line else ()
-    input_one, layer_two, out_own = lax.optimization_barrier((input_one, layer_two, out_own))
     input_two = gather_step_two(input_one) if line else ()
-    layer_three = gather_step_three(layer_two) if line else ()
     own_gain = gain_master.astype(LOW).astype(WIDE)
     qkv_wide = qkv_mine.astype(WIDE)
     ffn_wide = ffn_shard.astype(WIDE)
@@ -868,9 +920,7 @@
         ],
         axis=1,
     )
-    input_two, layer_three, clip_factor, attn_grads = lax.optimization_barrier(
-        (input_two, layer_three, clip_factor, attn_grads)
-    )
+    input_two, clip_factor, attn_grads = lax.optimization_barrier((input_two, clip_factor, attn_grads))
     input_three = gather_step_three(input_two) if line else ()
     blank = jnp.zeros((parts, block, width), WIDE)
     layer_output = line_gather_wide(blank, layer_slice, (layer_one, layer_two, layer_three))

time: 981 us -> 903 us (0.920)
  waiting for transfers between devices: 295 us -> 240 us
  starting transfers between devices: 149 us -> 125 us
    ppermute x6, waiting for transfers between devices: 72.6 us -> 35 us  [the longest x1 12.3 us: sum_step_two(): lax.ppermute(far, 'head', ACROSS)]
    ppermute x6 -> x3, waiting for transfers between devices: 64.9 us -> 34.1 us  [direct_terms(): lax.ppermute(lax.dynamic_index_in_dim(terms, at ^ k, 1, False), 'head', [...]
    reduce_scatter x1, waiting for transfers between devices: 16.4 us -> 0.01 us  [per_device(): lax.psum_scatter(ffn_raw, 'seq', scatter_dimension=0, tiled=True)]
    ppermute x4, waiting for transfers between devices: 2.5 us -> 17.7 us  [gather_step_two(): lax.ppermute(got[0], 'head', [(1, 2), (2, 3)])]
    ppermute x6 -> x3, starting transfers between devices: 14.7 us -> 3.59 us  [direct_terms(): lax.ppermute(lax.dynamic_index_in_dim(terms, at ^ k, 1, False), 'head', [...]
  transfers between devices with their start and end apart: 53 -> 50, of which waited for: 32 -> 34; matrix products, arithmetic and copies ran while one was open for 16% -> 18% of each run, Pallas kernels for 20% -> 21%
where the time goes in v3:
time: 903 us; the launch traced here: 893 us
  waiting for transfers between devices  240 us (27%)
  Pallas kernels  219 us (24%)
  starting transfers between devices  125 us (14%)
  other arithmetic  87.2 us (10%)
  local copies, waits for them, and re-layouts  70.8 us (8%)
  matrix products  62.6 us (7%)
  blocking collectives  60.5 us (7%)
  between operations  28 us (3%)
    pallas_call x2, Pallas kernels, feed_forward(): pl.pallas_call(functools.partial(ffn_kernel, len(pieces)), out_shape=[ful...  66.7 us
    dot_general x8, matrix products, dot(): return lax.dot_general(left, right, dims, preferred_element_type=WIDE)  62.6 us
    pallas_call x1, Pallas kernels, attention_backward(): pl.pallas_call(functools.partial(backward_kernel, sizes), out_shape=[jax....  61.9 us
    all_to_all x1, blocking collectives, per_device(): qkv = lax.all_to_all(sent, 'seq', split_axis=0, concat_axis=0, tiled=True)  51.6 us
    pallas_call x1, Pallas kernels, feed_forward_wgrad(): pl.pallas_call(functools.partial(ffn_wgrad_kernel, steps), out_shape=jax....  37.7 us
    pallas_call x1, Pallas kernels, attention_forward(): pl.pallas_call(functools.partial(forward_kernel, sizes), out_shape=[jax.S...  35.8 us
    ppermute x3, waiting for transfers between devices, direct_terms(): lax.ppermute(lax.dynamic_index_in_dim(terms, at ^ k, 1, False), 'head', [...  34.1 us
    dynamic_update_slice x12, other arithmetic, line_gather_wide(): lax.dynamic_update_slice(full, jnp.where(there, part, piece).astype(WIDE)...  31.5 us
  transfers between devices with their start and end apart: 50, of which 34 were waited for; matrix products, arithmetic and copies ran while one was open for 18% of the time, Pallas kernels for 21%

profile of v3, /device:TPU:8, one launch (start us, length us, event | category | flops | bytes accessed | tf_op | source)
XLA Modules:
  0.0 892.8 jit_solution(10330441188846296717)
XLA Ops:
  18.7 8.9 all_gather.12
  37.6 20.4 %all-gather.4.cloned.1.call-done = bf16[2048,1536]{0,1:T(8,128)(2,1)} async-done(((bf16[256,1536]{0,1:T(8,128)(2,1)}), bf16[2048,1536]{0,1:T(8,128)(2,1)}) %all-gather.4.cloned.1.call-update) | async-done | bytes 6291472 | tf_op jit(solution)/shard_map/all_gather | solution.py:695
  58.0 11.3 %multiply_convert_fusion = bf16[1024,1536]{1,0:T(8,128)(2,1)} fusion(bf16[2048,1536]{0,1:T(8,128)(2,1)} %all-gather.4.cloned.1.call-done, f32[1536]{0:T(1024)S(1)} %fusion.43, bf16[1024,2048]{1,0:T(8,128)(2,1)} %param.12, f32[2048]{0:T(1024)S(1)} %bitcast.184, f32[1024]{0:T(1024)S(1)} %add_rsqrt_fusion), kind=kOutput, calls=%fused_computation.14 | convolution fusion | flops 6453985280 | bytes 13649920 | tf_op jit(solution)/shard_map/dot_general | solution.py:35
  69.3 6.2 reshape.385
  77.9 51.6 %all_to_all.38 = bf16[8,512,384]{2,1,0:T(8,128)(2,1)S(1)} all-to-all(bf16[8,512,384]{2,1,0:T(8,128)(2,1)S(1)} %bitcast.155), channel_id=1, replica_groups=mesh['seq'=8,'head'=4] {'seq'}, dimensions={0} | all-to-all | bytes 6291456 | tf_op jit(solution)/shard_map/all_to_all | solution.py:716
  141.3 35.8 %attention_forward.1 = (bf16[8,512,128]{2,1,0:T(8,128)(2,1)}, f32[8,1,512]{2,1,0:T(1,128)S(1)}) custom-call(s32[2]{0:T(128)S(1)} %pad_add_fusion.ints, f32[6]{0:T(128)S(1)} %reshape.381.floats, bf16[8,512,128]{2,1,0:T(8,128)(2,1)S(1)} %slice.194.q_ref, bf16[8,512,256]{2,1,0:T(8,128)(2,1)S(1)} %slice.195.rest_0_, ...), custom_call_target="tpu_custom_call" | custom-call | flops 17179869184 | bytes 8388608 | tf_op jit(solution)/shard_map/attention_forward/pallas_call | solution.py:135
  183.0 24.9 %all-to-all-done.1 = bf16[32,128,128]{2,1,0:T(8,128)(2,1)S(1)} async-done(((bf16[32,128,128]{2,1,0:T(8,128)(2,1)}), bf16[32,128,128]{2,1,0:T(8,128)(2,1)S(1)}, u32[]{:S(2)}, u32[]{:S(2)}) %all-to-all-start.1) | async-done | bytes 1048608 | tf_op jit(solution)/shard_map/all_to_all | solution.py:724
  209.6 6.2 multiply_reduce_fusion.1
  281.2 8.8 collective-permute-done.8.refs_5_
  290.0 6.2 all-gather.8.cloned.1.call-done.refs_7_.refs_8_.refs_9_
  296.2 33.3 %feed_forward.2 = (bf16[512,2048]{1,0:T(8,128)(2,1)}, bf16[512,2048]{1,0:T(8,128)(2,1)}, bf16[512,2048]{1,0:T(8,128)(2,1)}, bf16[512,2048]{1,0:T(8,128)(2,1)}, bf16[512,2048]{1,0:T(8,128)(2,1)}) custom-call(s32[4]{0:T(128)} %compare_select_fusion.3.table, bf16[128,2048]{1,0:T(8,128)(2,1)} %copy-done.41, bf16[128,2048]{1,0:T(8,128)(2,1)} %collective-permute-done.4.refs_1_, ...), custom_call_target="tpu_custom_call" | custom-call | flops 21474836480 | bytes 25165824 | tf_op jit(solution)/shard_map/feed_forward/pallas_call | solution.py:353
  334.8 33.4 %feed_forward.3 = (bf16[512,2048]{1,0:T(8,128)(2,1)}, bf16[512,2048]{1,0:T(8,128)(2,1)}, bf16[512,2048]{1,0:T(8,128)(2,1)}, bf16[512,2048]{1,0:T(8,128)(2,1)}, bf16[512,2048]{1,0:T(8,128)(2,1)}) custom-call(s32[4]{0:T(128)} %compare_select_fusion.3.table, bf16[128,2048]{1,0:T(8,128)(2,1)} %copy-done.40, bf16[128,2048]{1,0:T(8,128)(2,1)} %collective-permute-done.9.refs_1_, ...), custom_call_target="tpu_custom_call" | custom-call | flops 21474836480 | bytes 25165824 | tf_op jit(solution)/shard_map/feed_forward/pallas_call | solution.py:353
  368.1 12.1 %all-to-all-done.2 = bf16[4,128,2048]{2,1,0:T(8,128)(2,1)} async-done(((bf16[4,128,2048]{2,1,0:T(8,128)(2,1)}), bf16[4,128,2048]{2,1,0:T(8,128)(2,1)}, u32[]{:S(2)}, u32[]{:S(2)}) %all-to-all-start.2) | async-done | bytes 2097184 | tf_op jit(solution)/shard_map/all_to_all | solution.py:476
  380.2 7.8 all-to-all-start.3
  393.1 37.7 %feed_forward_wgrad.1 = bf16[2048,6144]{1,0:T(8,128)(2,1)} custom-call(bf16[512,2048]{1,0:T(8,128)(2,1)} %get-tuple-element.114.n_a, bf16[512,2048]{1,0:T(8,128)(2,1)} %get-tuple-element.115.n_b, bf16[1024,2048]{1,0:T(8,128)(2,1)} %c_ref.1, bf16[512,2048]{1,0:T(8,128)(2,1)} %get-tuple-element.116.gate_a, bf16[512,2048]{1,0:T(8,128)(2,1)} %get-tuple-element.117.gate_b, ...), custom_call_target="tpu_custom_call" | custom-call | flops 2097152 | bytes 2097152 | tf_op jit(solution)/shard_map/feed_forward_wgrad/pallas_call | solution.py:420
  438.9 5.8 convolution_convert_fusion.1
  453.7 6.5 all-to-all-start.4
  460.3 8.8 fusion.19
  469.1 8.8 fusion.16
  480.4 6.4 all-to-all-done.4
  492.7 61.9 %attention_backward.1 = (bf16[8,512,128]{2,1,0:T(8,128)(2,1)}, bf16[8,512,256]{2,1,0:T(8,128)(2,1)}, bf16[8,512,256]{2,1,0:T(8,128)(2,1)}) custom-call(s32[2]{0:T(128)} %copy-done.11, f32[6]{0:T(128)} %copy-done.10, bf16[8,512,128]{2,1,0:T(8,128)(2,1)} %copy-done.9, bf16[8,512,128]{2,1,0:T(8,128)(2,1)} %bitcast.180, bf16[8,512,256]{2,1,0:T(8,128)(2,1)} %copy-done.6, ...), custom_call_target="tpu_custom_call" | custom-call | flops 214748364800 | bytes 16777216 | tf_op jit(solution)/shard_map/attention_backward/pallas_call | solution.py:249
  569.8 34.1 %collective-permute-done.16 = bf16[2,128,2048]{2,1,0:T(8,128)(2,1)} collective-permute-done((bf16[2,128,2048]{2,1,0:T(8,128)(2,1)}, bf16[2,128,2048]{2,1,0:T(8,128)(2,1)}, u32[]{:S(2)}, u32[]{:S(2)}) %collective-permute-start.16) | collective-permute-done | bytes 1048608 | tf_op jit(solution)/shard_map/ppermute | solution.py:591
  624.9 8.9 collective-permute-done.18
  637.0 6.2 all-to-all-done.5
  649.5 6.8 convolution_convert_fusion.2
  666.4 15.3 %collective-permute-done.21 = bf16[2,128,2048]{2,1,0:T(8,128)(2,1)S(1)} collective-permute-done((bf16[2,128,2048]{2,1,0:T(8,128)(2,1)}, bf16[2,128,2048]{2,1,0:T(8,128)(2,1)S(1)}, u32[]{:S(2)}, u32[]{:S(2)}) %collective-permute-start.21) | collective-permute-done | bytes 1048608 | tf_op jit(solution)/shard_map/ppermute | solution.py:527
  696.9 9.1 %convolution_convert_fusion = bf16[2048,1536]{1,0:T(8,128)(2,1)} fusion(bf16[1024,1536]{1,0:T(8,128)(2,1)S(1)} %bitcast.172, bf16[1024,2048]{1,0:T(8,128)(2,1)S(1)} %copy-done.26, f32[2048]{0:T(1024)S(1)} %bitcast.185, f32[1024]{0:T(1024)S(1)} %copy-done.54), kind=kOutput, calls=%fused_computation.5 | convolution fusion | flops 6453985280 | bytes 13643776 | tf_op jit(solution)/shard_map/dot_general | solution.py:35
  708.1 12.3 %collective-permute-done.24 = bf16[320,2048]{1,0:T(8,128)(2,1)} collective-permute-done((bf16[320,2048]{1,0:T(8,128)(2,1)}, bf16[320,2048]{1,0:T(8,128)(2,1)}, u32[]{:S(2)}, u32[]{:S(2)}) %collective-permute-start.24) | collective-permute-done | bytes 1310752 | tf_op jit(solution)/shard_map/ppermute | solution.py:498
  756.1 9.0 %collective-permute-done.28 = bf16[320,2048]{1,0:T(8,128)(2,1)S(1)} collective-permute-done((bf16[320,2048]{1,0:T(8,128)(2,1)S(1)}, bf16[320,2048]{1,0:T(8,128)(2,1)S(1)}, u32[]{:S(2)}, u32[]{:S(2)}) %collective-permute-start.28) | collective-permute-done | bytes 1310752 | tf_op jit(solution)/shard_map/ppermute | solution.py:507
  765.1 7.0 collective-permute-done.27
  827.4 9.8 %collective-permute-done.36 = f32[24,256]{1,0:T(8,128)S(1)} collective-permute-done((f32[24,256]{1,0:T(8,128)S(1)}, f32[24,256]{1,0:T(8,128)S(1)}, u32[]{:S(2)}, u32[]{:S(2)}) %collective-permute-start.36) | collective-permute-done | bytes 24608 | tf_op jit(solution)/shard_map/ppermute | solution.py:615
  858.7 12.1 %adam.3 = (f32[3,256,2048]{2,1,0:T(8,128)}, f32[3,256,2048]{2,1,0:T(8,128)}, f32[3,256,2048]{2,1,0:T(8,128)}, f32[3,256,2048]{2,1,0:T(8,128)}, bf16[3,256,2048]{2,1,0:T(8,128)(2,1)}) custom-call(f32[1]{0:T(128)} %bitcast.71.clip, bf16[256,6144]{1,0:T(8,128)(2,1)S(1)} %copy-done, f32[3,256,2048]{2,1,0:T(8,128)S(1)} %copy-done.2, ...), custom_call_target="tpu_custom_call" | custom-call | flops 31457280 | bytes 50331648 | tf_op jit(solution)/shard_map/adam/pallas_call | solution.py:457
  (345 shorter events, 331.3 us)
Async XLA Ops:
  7.2 50.8 %all-gather.4.cloned.1.call-start = ((), (), s32[]{:S(2)}) async-start(), calls=%async_computation.9 | async-start | bytes 7077888 | tf_op jit(solution)/shard_map/all_gather | solution.py:695
  10.0 199.6 %all-gather.6.cloned.1.call-start = ((), (), s32[]{:S(2)}) async-start(), calls=%async_computation.10 | async-start | bytes 9437184 | tf_op jit(solution)/shard_map/all_gather | solution.py:715
  14.4 23.1 %collective-permute-start.2 = (bf16[256,512]{0,1:T(8,128)(2,1)S(1)}, bf16[256,512]{0,1:T(8,128)(2,1)S(1)}, u32[]{:S(2)}, u32[]{:S(2)}) collective-permute-start(bf16[256,512]{0,1:T(8,128)(2,1)S(1)} %bitcast.179), channel_id=1, source_target_pairs={{0,3},{1,2},{2,1},{3,0},{4,7},{5,6},{6,5},{7,4},{8,11},{9,10},{10,... | collective-permute-start | bytes 786440 | tf_op jit(solution)/shard_map/ppermute | solution.py:605
  77.9 218.4 %all-gather.8.cloned.1.call-start = ((), (), s32[]{:S(2)}) async-start(), calls=%async_computation.11 | async-start | bytes 28311552 | tf_op jit(solution)/shard_map/all_gather | solution.py:720
  177.1 30.8 %all-to-all-start.1 = ((bf16[32,128,128]{2,1,0:T(8,128)(2,1)}), bf16[32,128,128]{2,1,0:T(8,128)(2,1)S(1)}, u32[]{:S(2)}, u32[]{:S(2)}) async-start(bf16[32,128,128]{2,1,0:T(8,128)(2,1)} %bitcast.17), calls=%async_computation.1 | async-start | bytes 2097152 | tf_op jit(solution)/shard_map/all_to_all | solution.py:724
  236.3 22.6 %collective-permute-start.12 = (bf16[128,2048]{1,0:T(8,128)(2,1)}, bf16[128,2048]{1,0:T(8,128)(2,1)S(1)}, u32[]{:S(2)}, u32[]{:S(2)}) collective-permute-start(bf16[128,2048]{1,0:T(8,128)(2,1)} %collective-permute-done.11.refs_3_), channel_id=1, source_target_pairs={{2,1},{1,0},{6,5},{5,4},{10,9},{9,8},{14,13},{13,12},{18,17},{17,1... | collective-permute-start | bytes 1572872 | tf_op jit(solution)/shard_map/ppermute | solution.py:528
  258.9 22.3 %collective-permute-start.13 = (bf16[128,2048]{1,0:T(8,128)(2,1)S(1)}, bf16[128,2048]{1,0:T(8,128)(2,1)}, u32[]{:S(2)}, u32[]{:S(2)}) collective-permute-start(bf16[128,2048]{1,0:T(8,128)(2,1)S(1)} %broadcast_select_fusion.2), channel_id=1, source_target_pairs={{2,3},{1,0},{6,7},{5,4},{10,11},{9,8},{14,15},{13,12},{18,19},{17,... | collective-permute-start | bytes 1572872 | tf_op jit(solution)/shard_map/ppermute | solution.py:534
  329.6 50.6 %all-to-all-start.2 = ((bf16[4,128,2048]{2,1,0:T(8,128)(2,1)}), bf16[4,128,2048]{2,1,0:T(8,128)(2,1)}, u32[]{:S(2)}, u32[]{:S(2)}) async-start(bf16[4,128,2048]{2,1,0:T(8,128)(2,1)} %bitcast.176), calls=%async_computation.2 | async-start | bytes 4194304 | tf_op jit(solution)/shard_map/all_to_all | solution.py:476
  380.2 52.4 %all-to-all-start.3 = ((bf16[4,128,2048]{2,1,0:T(8,128)(2,1)}), bf16[4,128,2048]{2,1,0:T(8,128)(2,1)}, u32[]{:S(2)}, u32[]{:S(2)}) async-start(bf16[4,128,2048]{2,1,0:T(8,128)(2,1)} %bitcast.175), calls=%async_computation.3 | async-start | bytes 4194304 | tf_op jit(solution)/shard_map/all_to_all | solution.py:476
  388.0 234.1 %reduce-scatter.4.cloned.1.call-start = ((), (), s32[]{:S(2)}) async-start(), calls=%async_computation.12 | async-start | bytes 9437184 | tf_op jit(solution)/shard_map/reduce_scatter | solution.py:790
  444.8 278.9 %reduce-scatter.6.cloned.1.call-start = ((), (), s32[]{:S(2)}) async-start(), calls=%async_computation.13 | async-start | bytes 28311552 | tf_op jit(solution)/shard_map/reduce_scatter | solution.py:764
  453.7 33.0 %all-to-all-start.4 = ((bf16[32,128,128]{2,1,0:T(8,128)(2,1)}), bf16[32,128,128]{2,1,0:T(8,128)(2,1)S(1)}, u32[]{:S(2)}, u32[]{:S(2)}) async-start(bf16[32,128,128]{2,1,0:T(8,128)(2,1)} %bitcast.33), calls=%async_computation.4 | async-start | bytes 2097152 | tf_op jit(solution)/shard_map/all_to_all | solution.py:786
  491.6 62.9 %collective-permute-start.14 = (bf16[2,128,2048]{2,1,0:T(8,128)(2,1)}, bf16[2,128,2048]{2,1,0:T(8,128)(2,1)}, u32[]{:S(2)}, u32[]{:S(2)}) collective-permute-start(bf16[2,128,2048]{2,1,0:T(8,128)(2,1)} %get-tuple-element.200), channel_id=1, source_target_pairs={{0,1},{1,0},{2,3},{3,2},{4,5},{5,4},{6,7},{7,6},{8,9},{9,8},{10,11... | collective-permute-start | bytes 3145736 | tf_op jit(solution)/shard_map/ppermute | solution.py:591
  491.6 62.9 %collective-permute-start.15 = (bf16[2,128,2048]{2,1,0:T(8,128)(2,1)}, bf16[2,128,2048]{2,1,0:T(8,128)(2,1)}, u32[]{:S(2)}, u32[]{:S(2)}) collective-permute-start(bf16[2,128,2048]{2,1,0:T(8,128)(2,1)} %get-tuple-element.198), channel_id=1, source_target_pairs={{0,2},{1,3},{2,0},{3,1},{4,6},{5,7},{6,4},{7,5},{8,10},{9,11},{10,... | collective-permute-start | bytes 3145736 | tf_op jit(solution)/shard_map/ppermute | solution.py:591
  554.8 49.2 %collective-permute-start.16 = (bf16[2,128,2048]{2,1,0:T(8,128)(2,1)}, bf16[2,128,2048]{2,1,0:T(8,128)(2,1)}, u32[]{:S(2)}, u32[]{:S(2)}) collective-permute-start(bf16[2,128,2048]{2,1,0:T(8,128)(2,1)} %get-tuple-element.199), channel_id=1, source_target_pairs={{0,3},{1,2},{2,1},{3,0},{4,7},{5,6},{6,5},{7,4},{8,11},{9,10},{10,... | collective-permute-start | bytes 3145736 | tf_op jit(solution)/shard_map/ppermute | solution.py:591
  564.8 78.5 %all-to-all-start.5 = ((bf16[8,528,384]{2,1,0:T(8,128)(2,1)}), bf16[8,528,384]{2,1,0:T(8,128)(2,1)}, u32[]{:S(2)}, u32[]{:S(2)}) async-start(bf16[8,528,384]{2,1,0:T(8,128)(2,1)} %fusion.9), calls=%async_computation.5 | async-start | bytes 6488064 | tf_op jit(solution)/shard_map/all_to_all | solution.py:803
  569.4 219.0 %reduce-scatter.8.cloned.1.call-start = ((), (), s32[]{:S(2)}) async-start(), calls=%async_computation.14 | async-start | bytes 7077888 | tf_op jit(solution)/shard_map/reduce_scatter | solution.py:869
  606.8 27.0 %collective-permute-start.18 = (bf16[2,128,2048]{2,1,0:T(8,128)(2,1)S(1)}, bf16[2,128,2048]{2,1,0:T(8,128)(2,1)}, u32[]{:S(2)}, u32[]{:S(2)}) collective-permute-start(bf16[2,128,2048]{2,1,0:T(8,128)(2,1)S(1)} %bitcast.145), channel_id=1, source_target_pairs={{0,1},{1,2},{2,3},{4,5},{5,6},{6,7},{8,9},{9,10},{10,11},{12,13},{... | collective-permute-start | bytes 3145736 | tf_op jit(solution)/shard_map/ppermute | solution.py:520
  610.5 26.5 %collective-permute-start.19 = (bf16[2,128,2048]{2,1,0:T(8,128)(2,1)S(1)}, bf16[2,128,2048]{2,1,0:T(8,128)(2,1)}, u32[]{:S(2)}, u32[]{:S(2)}) collective-permute-start(bf16[2,128,2048]{2,1,0:T(8,128)(2,1)S(1)} %bitcast.146), channel_id=1, source_target_pairs={{3,2},{2,1},{1,0},{7,6},{6,5},{5,4},{11,10},{10,9},{9,8},{15,14},{... | collective-permute-start | bytes 3145736 | tf_op jit(solution)/shard_map/ppermute | solution.py:521
  657.0 29.4 %collective-permute-start.20 = (bf16[320,2048]{1,0:T(8,128)(2,1)S(1)}, bf16[320,2048]{1,0:T(8,128)(2,1)S(1)}, u32[]{:S(2)}, u32[]{:S(2)}) collective-permute-start(bf16[320,2048]{1,0:T(8,128)(2,1)S(1)} %pad_maximum_fusion.2), channel_id=1, source_target_pairs={{0,1},{3,2},{4,5},{7,6},{8,9},{11,10},{12,13},{15,14},{16,17},{19,... | collective-permute-start | bytes 3932168 | tf_op jit(solution)/shard_map/ppermute | solution.py:493
  658.3 23.5 %collective-permute-start.21 = (bf16[2,128,2048]{2,1,0:T(8,128)(2,1)}, bf16[2,128,2048]{2,1,0:T(8,128)(2,1)S(1)}, u32[]{:S(2)}, u32[]{:S(2)}) collective-permute-start(bf16[2,128,2048]{2,1,0:T(8,128)(2,1)} %collective-permute-done.18), channel_id=1, source_target_pairs={{1,2},{2,3},{5,6},{6,7},{9,10},{10,11},{13,14},{14,15},{17,18},{18... | collective-permute-start | bytes 3145736 | tf_op jit(solution)/shard_map/ppermute | solution.py:527
  662.1 23.7 %collective-permute-start.22 = (bf16[2,128,2048]{2,1,0:T(8,128)(2,1)}, bf16[2,128,2048]{2,1,0:T(8,128)(2,1)S(1)}, u32[]{:S(2)}, u32[]{:S(2)}) collective-permute-start(bf16[2,128,2048]{2,1,0:T(8,128)(2,1)} %collective-permute-done.19), channel_id=1, source_target_pairs={{2,1},{1,0},{6,5},{5,4},{10,9},{9,8},{14,13},{13,12},{18,17},{17,1... | collective-permute-start | bytes 3145736 | tf_op jit(solution)/shard_map/ppermute | solution.py:528
  691.9 28.5 %collective-permute-start.24 = (bf16[320,2048]{1,0:T(8,128)(2,1)}, bf16[320,2048]{1,0:T(8,128)(2,1)}, u32[]{:S(2)}, u32[]{:S(2)}) collective-permute-start(bf16[320,2048]{1,0:T(8,128)(2,1)} %add_convert_fusion.2), channel_id=1, source_target_pairs={{1,2},{2,1},{5,6},{6,5},{9,10},{10,9},{13,14},{14,13},{17,18},{18,... | collective-permute-start | bytes 3932168 | tf_op jit(solution)/shard_map/ppermute | solution.py:498
  695.4 28.3 %collective-permute-start.23 = (bf16[320,2048]{1,0:T(8,128)(2,1)}, bf16[320,2048]{1,0:T(8,128)(2,1)}, u32[]{:S(2)}, u32[]{:S(2)}) collective-permute-start(bf16[320,2048]{1,0:T(8,128)(2,1)} %pad_maximum_fusion.5), channel_id=1, source_target_pairs={{0,1},{3,2},{4,5},{7,6},{8,9},{11,10},{12,13},{15,14},{16,17},{19,... | collective-permute-start | bytes 3932168 | tf_op jit(solution)/shard_map/ppermute | solution.py:498
  740.6 24.5 %collective-permute-start.28 = (bf16[320,2048]{1,0:T(8,128)(2,1)S(1)}, bf16[320,2048]{1,0:T(8,128)(2,1)S(1)}, u32[]{:S(2)}, u32[]{:S(2)}) collective-permute-start(bf16[320,2048]{1,0:T(8,128)(2,1)S(1)} %fusion.22), channel_id=1, source_target_pairs={{1,0},{2,3},{5,4},{6,7},{9,8},{10,11},{13,12},{14,15},{17,16},{18,... | collective-permute-start | bytes 3932168 | tf_op jit(solution)/shard_map/ppermute | solution.py:507
  744.4 27.7 %collective-permute-start.27 = (bf16[320,2048]{1,0:T(8,128)(2,1)S(1)}, bf16[320,2048]{1,0:T(8,128)(2,1)S(1)}, u32[]{:S(2)}, u32[]{:S(2)}) collective-permute-start(bf16[320,2048]{1,0:T(8,128)(2,1)S(1)} %add_convert_fusion.1), channel_id=1, source_target_pairs={{1,2},{2,1},{5,6},{6,5},{9,10},{10,9},{13,14},{14,13},{17,18},{18,... | collective-permute-start | bytes 3932168 | tf_op jit(solution)/shard_map/ppermute | solution.py:506
  746.8 28.2 %collective-permute-start.26 = (bf16[320,2048]{1,0:T(8,128)(2,1)S(1)}, bf16[320,2048]{1,0:T(8,128)(2,1)S(1)}, u32[]{:S(2)}, u32[]{:S(2)}) collective-permute-start(bf16[320,2048]{1,0:T(8,128)(2,1)S(1)} %copy-done.27), channel_id=1, source_target_pairs={{0,1},{3,2},{4,5},{7,6},{8,9},{11,10},{12,13},{15,14},{16,17},{19,... | collective-permute-start | bytes 3932168 | tf_op jit(solution)/shard_map/ppermute | solution.py:505
  779.4 28.9 %collective-permute-start.29 = (bf16[2,128,2048]{2,1,0:T(8,128)(2,1)}, bf16[2,128,2048]{2,1,0:T(8,128)(2,1)}, u32[]{:S(2)}, u32[]{:S(2)}) collective-permute-start(bf16[2,128,2048]{2,1,0:T(8,128)(2,1)} %bitcast.63), channel_id=1, source_target_pairs={{0,1},{1,2},{2,3},{4,5},{5,6},{6,7},{8,9},{9,10},{10,11},{12,13},{... | collective-permute-start | bytes 3145736 | tf_op jit(solution)/shard_map/ppermute | solution.py:520
  782.0 29.8 %collective-permute-start.30 = (bf16[2,128,2048]{2,1,0:T(8,128)(2,1)}, bf16[2,128,2048]{2,1,0:T(8,128)(2,1)}, u32[]{:S(2)}, u32[]{:S(2)}) collective-permute-start(bf16[2,128,2048]{2,1,0:T(8,128)(2,1)} %bitcast.63), channel_id=1, source_target_pairs={{3,2},{2,1},{1,0},{7,6},{6,5},{5,4},{11,10},{10,9},{9,8},{15,14},{... | collective-permute-start | bytes 3145736 | tf_op jit(solution)/shard_map/ppermute | solution.py:521
  808.3 36.3 %collective-permute-start.31 = (bf16[2,128,2048]{2,1,0:T(8,128)(2,1)}, bf16[2,128,2048]{2,1,0:T(8,128)(2,1)}, u32[]{:S(2)}, u32[]{:S(2)}) collective-permute-start(bf16[2,128,2048]{2,1,0:T(8,128)(2,1)} %collective-permute-done.29), channel_id=1, source_target_pairs={{1,2},{2,3},{5,6},{6,7},{9,10},{10,11},{13,14},{14,15},{17,18},{18... | collective-permute-start | bytes 3145736 | tf_op jit(solution)/shard_map/ppermute | solution.py:527
  811.8 32.8 %collective-permute-start.32 = (bf16[2,128,2048]{2,1,0:T(8,128)(2,1)}, bf16[2,128,2048]{2,1,0:T(8,128)(2,1)}, u32[]{:S(2)}, u32[]{:S(2)}) collective-permute-start(bf16[2,128,2048]{2,1,0:T(8,128)(2,1)} %collective-permute-done.30), channel_id=1, source_target_pairs={{2,1},{1,0},{6,5},{5,4},{10,9},{9,8},{14,13},{13,12},{18,17},{17,1... | collective-permute-start | bytes 3145736 | tf_op jit(solution)/shard_map/ppermute | solution.py:528
  845.9 35.8 %collective-permute-start.38 = (bf16[2,128,2048]{2,1,0:T(8,128)(2,1)S(1)}, bf16[2,128,2048]{2,1,0:T(8,128)(2,1)S(1)}, u32[]{:S(2)}, u32[]{:S(2)}) collective-permute-start(bf16[2,128,2048]{2,1,0:T(8,128)(2,1)S(1)} %broadcast_select_fusion), channel_id=1, source_target_pairs={{2,3},{1,0},{6,7},{5,4},{10,11},{9,8},{14,15},{13,12},{18,19},{17,... | collective-permute-start | bytes 3145736 | tf_op jit(solution)/shard_map/ppermute | solution.py:534
  (81 other events, 1316.3 us)
Sparse Core Ops, SparseCore 0:
  10.1 47.8 all-gather.3
  78.0 79.0 all-gather.5
  159.6 136.6 all-gather.7
  444.9 76.5 reduce-scatter.3
  525.3 192.7 reduce-scatter.5
  723.8 62.7 reduce-scatter.7

commit v4 on v3

--- a/solution.py
+++ b/solution.py
@@ -293,6 +293,42 @@
     )
 
 
+def projection_kernel(n_ref, w_ref, out_ref):
+    heads, parts, block, columns = out_ref.shape
+    lane = lax.broadcasted_iota(jnp.int32, (1, columns), 1)
+    factor = jnp.where(lane < HD, QUERY_FACTOR, 1.0)
+    for part in range(parts):
+        rows = pl.ds(part * block, block)
+        result = dot(n_ref[rows, :], w_ref[...])
+        for head in range(heads):
+            out_ref[head, part] = (
+                result[:, head * columns : (head + 1) * columns] * factor
+            ).astype(LOW)
+
+
+def project(normed, weight, local_heads, parts):
+    rows, width = normed.shape
+    columns = 3 * HD
+    heads = 2
+    return pl.pallas_call(
+        projection_kernel,
+        out_shape=jax.ShapeDtypeStruct((local_heads, parts, rows // parts, columns), LOW),
+        grid=(local_heads // heads,),
+        in_specs=[
+            pl.BlockSpec((rows, width), lambda j: (0, 0), pipeline_mode=pl.Buffered(1)),
+            pl.BlockSpec((width, heads * columns), lambda j: (0, j)),
+        ],
+        out_specs=pl.BlockSpec((heads, parts, rows // parts, columns), lambda j: (j, 0, 0, 0)),
+        compiler_params=pltpu.CompilerParams(vmem_limit_bytes=56 * 2**20),
+        cost_estimate=pl.CostEstimate(
+            flops=2 * rows * width * local_heads * columns,
+            bytes_accessed=2 * (rows * width + (rows + width) * local_heads * columns),
+            transcendentals=0,
+        ),
+        name="projection",
+    )(normed, weight)
+
+
 def ffn_kernel(pieces, table, *refs):
     given = refs[:pieces]
     c_ref, gate_w, up_w, down_w = refs[pieces : pieces + 4]
@@ -322,7 +358,7 @@
         total[...] = jnp.zeros_like(total)
         each(lambda copy: copy.wait())
 
-    chunk = min(256, rows)
+    chunk = min(512, rows)
     for at in range(0, rows, chunk):
         here = pl.ds(at, chunk)
         gate = dot(normed_ref[here, :], gate_w[...])
@@ -585,15 +621,9 @@
 
 
 def direct_terms(terms):
-    at = lax.axis_index("head")
     count = lax.axis_size("head")
-    return [lax.dynamic_index_in_dim(terms, at, 1, False)] + [
-        lax.ppermute(
-            lax.dynamic_index_in_dim(terms, at ^ k, 1, False),
-            "head",
-            [(j, j ^ k) for j in range(count)],
-        )
-        for k in range(1, count)
+    return terms[:1] + [
+        lax.ppermute(terms[k], "head", [(j, j ^ k) for j in range(count)]) for k in range(1, count)
     ]
 
 
@@ -699,19 +729,13 @@
 
     ints, floats = attention_scalars(seq_lengths, total_rows, part)
 
-    gain_values, out_rows = lax.optimization_barrier((gain_values, out_rows))
+    gain_values, out_rows, ffn_shard_low = lax.optimization_barrier(
+        (gain_values, out_rows, ffn_shard_low)
+    )
     residual = tokens.astype(WIDE)
     scale_one = lax.rsqrt(jnp.mean(residual * residual, axis=-1, keepdims=True) + EPS)
     normed_one = (residual * scale_one * gain_values[0]).astype(LOW)
-    column = jnp.arange(3 * head_width, dtype=jnp.int32) % (3 * HD)
-    column_factor = jnp.where(column < HD, QUERY_FACTOR, 1.0).astype(WIDE)
-    projected = (dot(normed_one, qkv_weight) * column_factor).astype(LOW)
-
-    sent = (
-        projected.reshape(parts, block, local_heads, 3 * HD)
-        .transpose(2, 0, 1, 3)
-        .reshape(seq_count, block, 3 * HD)
-    )
+    sent = project(normed_one, qkv_weight, local_heads, parts).reshape(seq_count, block, 3 * HD)
     out_weight = lax.all_gather(after(out_rows, sent), "seq", axis=0, tiled=True)
     qkv = lax.all_to_all(sent, "seq", split_axis=0, concat_axis=0, tiled=True)
     head_queries = qkv[:, :, :HD]
@@ -792,9 +816,12 @@
     ffn_part = jnp.stack(
         [dot(hidden_a, down_weight, NT).astype(LOW), dot(hidden_b, down_weight, NT).astype(LOW)]
     )
-    ffn_terms = direct_terms(
-        after(ffn_part, head_grads).reshape(2, head_count, quarter_rows, width)
-    )
+    ffn_part = ffn_part.reshape(2, head_count, quarter_rows, width)
+    ffn_terms = [
+        lax.dynamic_index_in_dim(ffn_part, head_index ^ k, 1, False) for k in range(head_count)
+    ]
+    ffn_terms, head_grads = lax.optimization_barrier((ffn_terms, head_grads))
+    ffn_terms = direct_terms(ffn_terms)
     early_terms, late_terms = ffn_terms[:3], ffn_terms[3:]
     q_grad, *kv_grads = attention_backward(sizes, ints, floats, head_queries, head_grads, key_values)
     kv_grads, early_terms = lax.optimization_barrier((kv_grads, early_terms))

time: 903 us -> 884 us (0.979)
  local copies, waits for them, and re-layouts: 70.8 us -> 57.6 us
  matrix products: 62.6 us -> 50.9 us
    dot_general x8 -> x7, matrix products: 62.6 us -> 50.9 us  [dot(): return lax.dot_general(left, right, dims, preferred_element_type=WIDE)]
    pallas_call x0 -> x1, Pallas kernels: none -> 11.1 us  [project(): pl.pallas_call(projection_kernel, out_shape=jax.ShapeDtypeStruct((local_h...]
    unnamed x133 -> x121, local copies, waits for them, and re-layouts: 20.4 us -> 18.9 us
  transfers between devices with their start and end apart: 50 -> 50, of which waited for: 34 -> 35; matrix products, arithmetic and copies ran while one was open for 18% -> 19% of each run, Pallas kernels for 21% -> 21%
where the time goes in v4:
time: 884 us; the launch traced here: 873 us
  waiting for transfers between devices  231 us (26%)
  Pallas kernels  228 us (26%)
  starting transfers between devices  124 us (14%)
  other arithmetic  92.2 us (10%)
  blocking collectives  61.5 us (7%)
  local copies, waits for them, and re-layouts  57.6 us (7%)
  matrix products  50.9 us (6%)
  between operations  28.1 us (3%)
    pallas_call x2, Pallas kernels, feed_forward(): pl.pallas_call(functools.partial(ffn_kernel, len(pieces)), out_shape=[ful...  65.1 us
    pallas_call x1, Pallas kernels, attention_backward(): pl.pallas_call(functools.partial(backward_kernel, sizes), out_shape=[jax....  62.1 us
    all_to_all x1, blocking collectives, per_device(): qkv = lax.all_to_all(sent, 'seq', split_axis=0, concat_axis=0, tiled=True)  52.6 us
    dot_general x7, matrix products, dot(): return lax.dot_general(left, right, dims, preferred_element_type=WIDE)  50.9 us
    pallas_call x1, Pallas kernels, feed_forward_wgrad(): pl.pallas_call(functools.partial(ffn_wgrad_kernel, steps), out_shape=jax....  37.7 us
    pallas_call x1, Pallas kernels, attention_forward(): pl.pallas_call(functools.partial(forward_kernel, sizes), out_shape=[jax.S...  35.7 us
    ppermute x3, waiting for transfers between devices, direct_terms(): lax.ppermute(terms[k], 'head', [(j, j ^ k) for j in range(count)])  33.4 us
    dynamic_update_slice x12, other arithmetic, line_gather_wide(): lax.dynamic_update_slice(full, jnp.where(there, part, piece).astype(WIDE)...  31 us
  transfers between devices with their start and end apart: 50, of which 35 were waited for; matrix products, arithmetic and copies ran while one was open for 19% of the time, Pallas kernels for 21%

profile of v4, /device:TPU:8, one launch (start us, length us, event | category | flops | bytes accessed | tf_op | source)
XLA Modules:
  0.0 873.3 jit_solution(2828009105644326452)
XLA Ops:
  24.6 8.9 %all_gather.12 = bf16[2,2048]{1,0:T(2,128)(2,1)S(1)} all-gather(bf16[2,256]{1,0:T(2,128)(2,1)S(1)} %get-tuple-element.193), channel_id=1, replica_groups=mesh['seq'=8,'head'=4] {'seq'}, dimensions={1}, use_global_device_ids=true | all-gather | bytes 9216 | tf_op jit(solution)/shard_map/all_gather | solution.py:724
  44.5 12.7 %all-gather.4.cloned.1.call-done.w_ref = bf16[2048,1536]{1,0:T(8,128)(2,1)} async-done(((bf16[256,1536]{1,0:T(8,128)(2,1)}), bf16[2048,1536]{1,0:T(8,128)(2,1)}) %all-gather.4.cloned.1.call-update) | async-done | bytes 6291472 | tf_op jit(solution)/shard_map/all_gather | solution.py:725
  57.2 11.1 %projection.1 = bf16[4,2,512,384]{3,2,1,0:T(8,128)(2,1)} custom-call(bf16[1024,2048]{1,0:T(8,128)(2,1)} %fusion.2.n_ref, bf16[2048,1536]{1,0:T(8,128)(2,1)} %all-gather.4.cloned.1.call-done.w_ref), custom_call_target="tpu_custom_call" | custom-call | flops 6442450944 | bytes 13631488 | tf_op jit(solution)/shard_map/projection/pallas_call | solution.py:313
  68.4 52.6 %all_to_all.38 = bf16[8,512,384]{2,1,0:T(8,128)(2,1)S(1)} all-to-all(bf16[8,512,384]{2,1,0:T(8,128)(2,1)} %bitcast.164), channel_id=1, replica_groups=mesh['seq'=8,'head'=4] {'seq'}, dimensions={0} | all-to-all | bytes 6291456 | tf_op jit(solution)/shard_map/all_to_all | solution.py:740
  129.0 35.7 %attention_forward.1 = (bf16[8,512,128]{2,1,0:T(8,128)(2,1)}, f32[8,1,512]{2,1,0:T(1,128)S(1)}) custom-call(s32[2]{0:T(128)S(1)} %pad_add_fusion.ints, f32[6]{0:T(128)S(1)} %reshape.369.floats, bf16[8,512,128]{2,1,0:T(8,128)(2,1)S(1)} %slice.199.q_ref, bf16[8,512,256]{2,1,0:T(8,128)(2,1)S(1)} %slice.200.rest_0_, ...), custom_call_target="tpu_custom_call" | custom-call | flops 17179869184 | bytes 8388608 | tf_op jit(solution)/shard_map/attention_forward/pallas_call | solution.py:135
  171.1 24.9 %all-to-all-done.1 = bf16[32,128,128]{2,1,0:T(8,128)(2,1)S(1)} async-done(((bf16[32,128,128]{2,1,0:T(8,128)(2,1)}), bf16[32,128,128]{2,1,0:T(8,128)(2,1)S(1)}, u32[]{:S(2)}, u32[]{:S(2)}) %all-to-all-start.1) | async-done | bytes 1048608 | tf_op jit(solution)/shard_map/all_to_all | solution.py:748
  197.8 6.2 multiply_reduce_fusion.1
  252.6 5.6 collective-permute-done.7.refs_4_
  269.4 8.8 %collective-permute-done.8.refs_5_ = bf16[128,2048]{1,0:T(8,128)(2,1)} collective-permute-done((bf16[128,2048]{1,0:T(8,128)(2,1)S(1)}, bf16[128,2048]{1,0:T(8,128)(2,1)}, u32[]{:S(2)}, u32[]{:S(2)}) %collective-permute-start.8) | collective-permute-done | bytes 524320 | tf_op jit(solution)/shard_map/ppermute | solution.py:570
  278.2 8.5 all-gather.8.cloned.1.call-done.refs_7_.refs_8_.refs_9_
  286.7 32.5 %feed_forward.2 = (bf16[512,2048]{1,0:T(8,128)(2,1)}, bf16[512,2048]{1,0:T(8,128)(2,1)}, bf16[512,2048]{1,0:T(8,128)(2,1)}, bf16[512,2048]{1,0:T(8,128)(2,1)}, bf16[512,2048]{1,0:T(8,128)(2,1)}) custom-call(s32[4]{0:T(128)} %compare_select_fusion.3.table, bf16[128,2048]{1,0:T(8,128)(2,1)} %copy-done.35, bf16[128,2048]{1,0:T(8,128)(2,1)} %collective-permute-done.4.refs_1_, ...), custom_call_target="tpu_custom_call" | custom-call | flops 21474836480 | bytes 25165824 | tf_op jit(solution)/shard_map/feed_forward/pallas_call | solution.py:389
  324.3 32.6 %feed_forward.3 = (bf16[512,2048]{1,0:T(8,128)(2,1)}, bf16[512,2048]{1,0:T(8,128)(2,1)}, bf16[512,2048]{1,0:T(8,128)(2,1)}, bf16[512,2048]{1,0:T(8,128)(2,1)}, bf16[512,2048]{1,0:T(8,128)(2,1)}) custom-call(s32[4]{0:T(128)} %compare_select_fusion.3.table, bf16[128,2048]{1,0:T(8,128)(2,1)} %copy-done.34, bf16[128,2048]{1,0:T(8,128)(2,1)} %collective-permute-done.9.refs_1_, ...), custom_call_target="tpu_custom_call" | custom-call | flops 21474836480 | bytes 25165824 | tf_op jit(solution)/shard_map/feed_forward/pallas_call | solution.py:389
  356.9 12.9 %all-to-all-done.2 = bf16[4,128,2048]{2,1,0:T(8,128)(2,1)} async-done(((bf16[4,128,2048]{2,1,0:T(8,128)(2,1)}), bf16[4,128,2048]{2,1,0:T(8,128)(2,1)}, u32[]{:S(2)}, u32[]{:S(2)}) %all-to-all-start.2) | async-done | bytes 2097184 | tf_op jit(solution)/shard_map/all_to_all | solution.py:512
  369.8 7.8 all-to-all-start.3
  382.4 37.7 %feed_forward_wgrad.1 = bf16[2048,6144]{1,0:T(8,128)(2,1)} custom-call(bf16[512,2048]{1,0:T(8,128)(2,1)} %get-tuple-element.122.n_a, bf16[512,2048]{1,0:T(8,128)(2,1)} %get-tuple-element.123.n_b, bf16[1024,2048]{1,0:T(8,128)(2,1)} %c_ref.1, bf16[512,2048]{1,0:T(8,128)(2,1)} %get-tuple-element.124.gate_a, bf16[512,2048]{1,0:T(8,128)(2,1)} %get-tuple-element.125.gate_b, ...), custom_call_target="tpu_custom_call" | custom-call | flops 2097152 | bytes 2097152 | tf_op jit(solution)/shard_map/feed_forward_wgrad/pallas_call | solution.py:456
  428.6 5.8 convolution_convert_fusion.1
  435.6 5.7 convolution_convert_fusion.3
  443.4 6.8 all-to-all-start.4
  450.2 8.7 fusion.13
  459.0 8.8 %fusion.10 = bf16[512,2048]{1,0:T(8,128)(2,1)S(1)} fusion(bf16[512,2048]{1,0:T(8,128)(2,1)S(1)} %copy-done.36, bf16[2048,6144]{1,0:T(8,128)(2,1)} %all-gather.8.cloned.1.call-done.refs_7_.refs_8_.refs_9_), kind=kOutput, calls=%fused_computation.30 | convolution fusion | flops 4296015872 | bytes 12582912 | tf_op jit(solution)/shard_map/dot_general | solution.py:35
  469.9 6.6 all-to-all-done.4
  477.7 62.1 %attention_backward.1 = (bf16[8,512,128]{2,1,0:T(8,128)(2,1)}, bf16[8,512,256]{2,1,0:T(8,128)(2,1)}, bf16[8,512,256]{2,1,0:T(8,128)(2,1)}) custom-call(s32[2]{0:T(128)} %copy-done.11, f32[6]{0:T(128)} %copy-done.10, bf16[8,512,128]{2,1,0:T(8,128)(2,1)} %copy-done.9, bf16[8,512,128]{2,1,0:T(8,128)(2,1)} %bitcast.175, bf16[8,512,256]{2,1,0:T(8,128)(2,1)} %copy-done.6, ...), custom_call_target="tpu_custom_call" | custom-call | flops 214748364800 | bytes 16777216 | tf_op jit(solution)/shard_map/attention_backward/pallas_call | solution.py:249
  555.5 33.4 %collective-permute-done.16 = bf16[2,128,2048]{2,1,0:T(8,128)(2,1)} collective-permute-done((bf16[2,128,2048]{2,1,0:T(8,128)(2,1)}, bf16[2,128,2048]{2,1,0:T(8,128)(2,1)}, u32[]{:S(2)}, u32[]{:S(2)}) %collective-permute-start.16) | collective-permute-done | bytes 1048608 | tf_op jit(solution)/shard_map/ppermute | solution.py:626
  610.2 9.0 %collective-permute-done.18 = bf16[2,128,2048]{2,1,0:T(8,128)(2,1)} collective-permute-done((bf16[2,128,2048]{2,1,0:T(8,128)(2,1)S(1)}, bf16[2,128,2048]{2,1,0:T(8,128)(2,1)}, u32[]{:S(2)}, u32[]{:S(2)}) %collective-permute-start.18) | collective-permute-done | bytes 1048608 | tf_op jit(solution)/shard_map/ppermute | solution.py:556
  633.0 6.9 convolution_convert_fusion.2
  649.5 13.2 %collective-permute-done.21 = bf16[2,128,2048]{2,1,0:T(8,128)(2,1)S(1)} collective-permute-done((bf16[2,128,2048]{2,1,0:T(8,128)(2,1)}, bf16[2,128,2048]{2,1,0:T(8,128)(2,1)S(1)}, u32[]{:S(2)}, u32[]{:S(2)}) %collective-permute-start.21) | collective-permute-done | bytes 1048608 | tf_op jit(solution)/shard_map/ppermute | solution.py:563
  677.9 8.8 %convolution_convert_fusion = bf16[2048,1536]{1,0:T(8,128)(2,1)} fusion(bf16[1024,2048]{1,0:T(8,128)(2,1)S(1)} %copy-done.25, bf16[1024,1536]{1,0:T(8,128)(2,1)S(1)} %bitcast.163), kind=kOutput, calls=%fused_computation.5 | convolution fusion | flops 6445596672 | bytes 13631488 | tf_op jit(solution)/shard_map/dot_general | solution.py:35
  689.8 12.3 %collective-permute-done.24 = bf16[320,2048]{1,0:T(8,128)(2,1)} collective-permute-done((bf16[320,2048]{1,0:T(8,128)(2,1)}, bf16[320,2048]{1,0:T(8,128)(2,1)}, u32[]{:S(2)}, u32[]{:S(2)}) %collective-permute-start.24) | collective-permute-done | bytes 1310752 | tf_op jit(solution)/shard_map/ppermute | solution.py:534
  737.9 11.9 %collective-permute-done.28 = bf16[320,2048]{1,0:T(8,128)(2,1)S(1)} collective-permute-done((bf16[320,2048]{1,0:T(8,128)(2,1)S(1)}, bf16[320,2048]{1,0:T(8,128)(2,1)S(1)}, u32[]{:S(2)}, u32[]{:S(2)}) %collective-permute-start.28) | collective-permute-done | bytes 1310752 | tf_op jit(solution)/shard_map/ppermute | solution.py:543
  749.8 7.3 collective-permute-done.27
  811.3 6.3 collective-permute-done.36
  839.2 12.1 %adam.3 = (f32[3,256,2048]{2,1,0:T(8,128)}, f32[3,256,2048]{2,1,0:T(8,128)}, f32[3,256,2048]{2,1,0:T(8,128)}, f32[3,256,2048]{2,1,0:T(8,128)}, bf16[3,256,2048]{2,1,0:T(8,128)(2,1)}) custom-call(f32[1]{0:T(128)} %bitcast.68.clip, bf16[256,6144]{1,0:T(8,128)(2,1)S(1)} %copy-done, f32[3,256,2048]{2,1,0:T(8,128)S(1)} %copy-done.2, ...), custom_call_target="tpu_custom_call" | custom-call | flops 31457280 | bytes 50331648 | tf_op jit(solution)/shard_map/adam/pallas_call | solution.py:493
  (330 shorter events, 321.0 us)
Async XLA Ops:
  7.2 50.0 %all-gather.4.cloned.1.call-start = ((), (), s32[]{:S(2)}) async-start(), calls=%async_computation.9 | async-start | bytes 7077888 | tf_op jit(solution)/shard_map/all_gather | solution.py:725
  10.3 187.4 %all-gather.6.cloned.1.call-start = ((), (), s32[]{:S(2)}) async-start(), calls=%async_computation.10 | async-start | bytes 9437184 | tf_op jit(solution)/shard_map/all_gather | solution.py:739
  11.7 22.9 %collective-permute-start.1 = (bf16[256,512]{0,1:T(8,128)(2,1)S(1)}, bf16[256,512]{0,1:T(8,128)(2,1)}, u32[]{:S(2)}, u32[]{:S(2)}) collective-permute-start(bf16[256,512]{0,1:T(8,128)(2,1)S(1)} %bitcast.173), channel_id=1, source_target_pairs={{0,2},{1,3},{2,0},{3,1},{4,6},{5,7},{6,4},{7,5},{8,10},{9,11},{10,... | collective-permute-start | bytes 786440 | tf_op jit(solution)/shard_map/ppermute | solution.py:635
  14.7 23.2 %collective-permute-start.2 = (bf16[256,512]{0,1:T(8,128)(2,1)S(1)}, bf16[256,512]{0,1:T(8,128)(2,1)}, u32[]{:S(2)}, u32[]{:S(2)}) collective-permute-start(bf16[256,512]{0,1:T(8,128)(2,1)S(1)} %bitcast.174), channel_id=1, source_target_pairs={{0,3},{1,2},{2,1},{3,0},{4,7},{5,6},{6,5},{7,4},{8,11},{9,10},{10,... | collective-permute-start | bytes 786440 | tf_op jit(solution)/shard_map/ppermute | solution.py:635
  68.3 218.3 %all-gather.8.cloned.1.call-start = ((), (), s32[]{:S(2)}) async-start(), calls=%async_computation.11 | async-start | bytes 28311552 | tf_op jit(solution)/shard_map/all_gather | solution.py:744
  164.8 31.3 %all-to-all-start.1 = ((bf16[32,128,128]{2,1,0:T(8,128)(2,1)}), bf16[32,128,128]{2,1,0:T(8,128)(2,1)S(1)}, u32[]{:S(2)}, u32[]{:S(2)}) async-start(bf16[32,128,128]{2,1,0:T(8,128)(2,1)} %bitcast.19), calls=%async_computation.1 | async-start | bytes 2097152 | tf_op jit(solution)/shard_map/all_to_all | solution.py:748
  224.4 22.6 %collective-permute-start.12 = (bf16[128,2048]{1,0:T(8,128)(2,1)}, bf16[128,2048]{1,0:T(8,128)(2,1)S(1)}, u32[]{:S(2)}, u32[]{:S(2)}) collective-permute-start(bf16[128,2048]{1,0:T(8,128)(2,1)} %collective-permute-done.11.refs_3_), channel_id=1, source_target_pairs={{2,1},{1,0},{6,5},{5,4},{10,9},{9,8},{14,13},{13,12},{18,17},{17,1... | collective-permute-start | bytes 1572872 | tf_op jit(solution)/shard_map/ppermute | solution.py:564
  247.1 22.3 %collective-permute-start.13 = (bf16[128,2048]{1,0:T(8,128)(2,1)S(1)}, bf16[128,2048]{1,0:T(8,128)(2,1)}, u32[]{:S(2)}, u32[]{:S(2)}) collective-permute-start(bf16[128,2048]{1,0:T(8,128)(2,1)S(1)} %broadcast_select_fusion.2), channel_id=1, source_target_pairs={{2,3},{1,0},{6,7},{5,4},{10,11},{9,8},{14,15},{13,12},{18,19},{17,... | collective-permute-start | bytes 1572872 | tf_op jit(solution)/shard_map/ppermute | solution.py:570
  319.2 50.6 %all-to-all-start.2 = ((bf16[4,128,2048]{2,1,0:T(8,128)(2,1)}), bf16[4,128,2048]{2,1,0:T(8,128)(2,1)}, u32[]{:S(2)}, u32[]{:S(2)}) async-start(bf16[4,128,2048]{2,1,0:T(8,128)(2,1)} %bitcast.171), calls=%async_computation.2 | async-start | bytes 4194304 | tf_op jit(solution)/shard_map/all_to_all | solution.py:512
  369.8 52.4 %all-to-all-start.3 = ((bf16[4,128,2048]{2,1,0:T(8,128)(2,1)}), bf16[4,128,2048]{2,1,0:T(8,128)(2,1)}, u32[]{:S(2)}, u32[]{:S(2)}) async-start(bf16[4,128,2048]{2,1,0:T(8,128)(2,1)} %bitcast.170), calls=%async_computation.3 | async-start | bytes 4194304 | tf_op jit(solution)/shard_map/all_to_all | solution.py:512
  377.6 229.8 %reduce-scatter.4.cloned.1.call-start = ((), (), s32[]{:S(2)}) async-start(), calls=%async_computation.12 | async-start | bytes 9437184 | tf_op jit(solution)/shard_map/reduce_scatter | solution.py:814
  434.4 270.1 %reduce-scatter.6.cloned.1.call-start = ((), (), s32[]{:S(2)}) async-start(), calls=%async_computation.13 | async-start | bytes 28311552 | tf_op jit(solution)/shard_map/reduce_scatter | solution.py:788
  443.4 33.2 %all-to-all-start.4 = ((bf16[32,128,128]{2,1,0:T(8,128)(2,1)}), bf16[32,128,128]{2,1,0:T(8,128)(2,1)S(1)}, u32[]{:S(2)}, u32[]{:S(2)}) async-start(bf16[32,128,128]{2,1,0:T(8,128)(2,1)} %bitcast.31), calls=%async_computation.4 | async-start | bytes 2097152 | tf_op jit(solution)/shard_map/all_to_all | solution.py:810
  476.6 63.2 %collective-permute-start.14 = (bf16[2,128,2048]{2,1,0:T(8,128)(2,1)}, bf16[2,128,2048]{2,1,0:T(8,128)(2,1)}, u32[]{:S(2)}, u32[]{:S(2)}) collective-permute-start(bf16[2,128,2048]{2,1,0:T(8,128)(2,1)} %get-tuple-element.135), channel_id=1, source_target_pairs={{0,1},{1,0},{2,3},{3,2},{4,5},{5,4},{6,7},{7,6},{8,9},{9,8},{10,11... | collective-permute-start | bytes 3145736 | tf_op jit(solution)/shard_map/ppermute | solution.py:626
  476.6 63.2 %collective-permute-start.15 = (bf16[2,128,2048]{2,1,0:T(8,128)(2,1)}, bf16[2,128,2048]{2,1,0:T(8,128)(2,1)}, u32[]{:S(2)}, u32[]{:S(2)}) collective-permute-start(bf16[2,128,2048]{2,1,0:T(8,128)(2,1)} %get-tuple-element.136), channel_id=1, source_target_pairs={{0,2},{1,3},{2,0},{3,1},{4,6},{5,7},{6,4},{7,5},{8,10},{9,11},{10,... | collective-permute-start | bytes 3145736 | tf_op jit(solution)/shard_map/ppermute | solution.py:626
  540.1 48.8 %collective-permute-start.16 = (bf16[2,128,2048]{2,1,0:T(8,128)(2,1)}, bf16[2,128,2048]{2,1,0:T(8,128)(2,1)}, u32[]{:S(2)}, u32[]{:S(2)}) collective-permute-start(bf16[2,128,2048]{2,1,0:T(8,128)(2,1)} %get-tuple-element.140), channel_id=1, source_target_pairs={{0,3},{1,2},{2,1},{3,0},{4,7},{5,6},{6,5},{7,4},{8,11},{9,10},{10,... | collective-permute-start | bytes 3145736 | tf_op jit(solution)/shard_map/ppermute | solution.py:626
  550.9 75.9 %all-to-all-start.5 = ((bf16[8,528,384]{2,1,0:T(8,128)(2,1)}), bf16[8,528,384]{2,1,0:T(8,128)(2,1)}, u32[]{:S(2)}, u32[]{:S(2)}) async-start(bf16[8,528,384]{2,1,0:T(8,128)(2,1)} %fusion.9), calls=%async_computation.5 | async-start | bytes 6488064 | tf_op jit(solution)/shard_map/all_to_all | solution.py:830
  555.5 218.4 %reduce-scatter.8.cloned.1.call-start = ((), (), s32[]{:S(2)}) async-start(), calls=%async_computation.14 | async-start | bytes 7077888 | tf_op jit(solution)/shard_map/reduce_scatter | solution.py:896
  591.8 27.4 %collective-permute-start.18 = (bf16[2,128,2048]{2,1,0:T(8,128)(2,1)S(1)}, bf16[2,128,2048]{2,1,0:T(8,128)(2,1)}, u32[]{:S(2)}, u32[]{:S(2)}) collective-permute-start(bf16[2,128,2048]{2,1,0:T(8,128)(2,1)S(1)} %bitcast.140), channel_id=1, source_target_pairs={{0,1},{1,2},{2,3},{4,5},{5,6},{6,7},{8,9},{9,10},{10,11},{12,13},{... | collective-permute-start | bytes 3145736 | tf_op jit(solution)/shard_map/ppermute | solution.py:556
  595.8 26.5 %collective-permute-start.19 = (bf16[2,128,2048]{2,1,0:T(8,128)(2,1)S(1)}, bf16[2,128,2048]{2,1,0:T(8,128)(2,1)}, u32[]{:S(2)}, u32[]{:S(2)}) collective-permute-start(bf16[2,128,2048]{2,1,0:T(8,128)(2,1)S(1)} %bitcast.141), channel_id=1, source_target_pairs={{3,2},{2,1},{1,0},{7,6},{6,5},{5,4},{11,10},{10,9},{9,8},{15,14},{... | collective-permute-start | bytes 3145736 | tf_op jit(solution)/shard_map/ppermute | solution.py:557
  640.4 28.6 %collective-permute-start.20 = (bf16[320,2048]{1,0:T(8,128)(2,1)S(1)}, bf16[320,2048]{1,0:T(8,128)(2,1)S(1)}, u32[]{:S(2)}, u32[]{:S(2)}) collective-permute-start(bf16[320,2048]{1,0:T(8,128)(2,1)S(1)} %pad_maximum_fusion.1), channel_id=1, source_target_pairs={{0,1},{3,2},{4,5},{7,6},{8,9},{11,10},{12,13},{15,14},{16,17},{19,... | collective-permute-start | bytes 3932168 | tf_op jit(solution)/shard_map/ppermute | solution.py:529
  643.4 23.3 %collective-permute-start.22 = (bf16[2,128,2048]{2,1,0:T(8,128)(2,1)}, bf16[2,128,2048]{2,1,0:T(8,128)(2,1)S(1)}, u32[]{:S(2)}, u32[]{:S(2)}) collective-permute-start(bf16[2,128,2048]{2,1,0:T(8,128)(2,1)} %collective-permute-done.19), channel_id=1, source_target_pairs={{2,1},{1,0},{6,5},{5,4},{10,9},{9,8},{14,13},{13,12},{18,17},{17,1... | collective-permute-start | bytes 3145736 | tf_op jit(solution)/shard_map/ppermute | solution.py:564
  674.2 27.9 %collective-permute-start.24 = (bf16[320,2048]{1,0:T(8,128)(2,1)}, bf16[320,2048]{1,0:T(8,128)(2,1)}, u32[]{:S(2)}, u32[]{:S(2)}) collective-permute-start(bf16[320,2048]{1,0:T(8,128)(2,1)} %add_convert_fusion.2), channel_id=1, source_target_pairs={{1,2},{2,1},{5,6},{6,5},{9,10},{10,9},{13,14},{14,13},{17,18},{18,... | collective-permute-start | bytes 3932168 | tf_op jit(solution)/shard_map/ppermute | solution.py:534
  676.4 27.8 %collective-permute-start.23 = (bf16[320,2048]{1,0:T(8,128)(2,1)}, bf16[320,2048]{1,0:T(8,128)(2,1)}, u32[]{:S(2)}, u32[]{:S(2)}) collective-permute-start(bf16[320,2048]{1,0:T(8,128)(2,1)} %pad_maximum_fusion.4), channel_id=1, source_target_pairs={{0,1},{3,2},{4,5},{7,6},{8,9},{11,10},{12,13},{15,14},{16,17},{19,... | collective-permute-start | bytes 3932168 | tf_op jit(solution)/shard_map/ppermute | solution.py:534
  720.1 29.7 %collective-permute-start.28 = (bf16[320,2048]{1,0:T(8,128)(2,1)S(1)}, bf16[320,2048]{1,0:T(8,128)(2,1)S(1)}, u32[]{:S(2)}, u32[]{:S(2)}) collective-permute-start(bf16[320,2048]{1,0:T(8,128)(2,1)S(1)} %fusion.16), channel_id=1, source_target_pairs={{1,0},{2,3},{5,4},{6,7},{9,8},{10,11},{13,12},{14,15},{17,16},{18,... | collective-permute-start | bytes 3932168 | tf_op jit(solution)/shard_map/ppermute | solution.py:543
  724.1 32.9 %collective-permute-start.27 = (bf16[320,2048]{1,0:T(8,128)(2,1)S(1)}, bf16[320,2048]{1,0:T(8,128)(2,1)S(1)}, u32[]{:S(2)}, u32[]{:S(2)}) collective-permute-start(bf16[320,2048]{1,0:T(8,128)(2,1)S(1)} %add_convert_fusion.1), channel_id=1, source_target_pairs={{1,2},{2,1},{5,6},{6,5},{9,10},{10,9},{13,14},{14,13},{17,18},{18,... | collective-permute-start | bytes 3932168 | tf_op jit(solution)/shard_map/ppermute | solution.py:542
  728.4 32.0 %collective-permute-start.26 = (bf16[320,2048]{1,0:T(8,128)(2,1)S(1)}, bf16[320,2048]{1,0:T(8,128)(2,1)S(1)}, u32[]{:S(2)}, u32[]{:S(2)}) collective-permute-start(bf16[320,2048]{1,0:T(8,128)(2,1)S(1)} %copy-done.22), channel_id=1, source_target_pairs={{0,1},{3,2},{4,5},{7,6},{8,9},{11,10},{12,13},{15,14},{16,17},{19,... | collective-permute-start | bytes 3932168 | tf_op jit(solution)/shard_map/ppermute | solution.py:541
  764.8 25.7 %collective-permute-start.29 = (bf16[2,128,2048]{2,1,0:T(8,128)(2,1)}, bf16[2,128,2048]{2,1,0:T(8,128)(2,1)}, u32[]{:S(2)}, u32[]{:S(2)}) collective-permute-start(bf16[2,128,2048]{2,1,0:T(8,128)(2,1)} %bitcast.60), channel_id=1, source_target_pairs={{0,1},{1,2},{2,3},{4,5},{5,6},{6,7},{8,9},{9,10},{10,11},{12,13},{... | collective-permute-start | bytes 3145736 | tf_op jit(solution)/shard_map/ppermute | solution.py:556
  767.0 27.1 %collective-permute-start.30 = (bf16[2,128,2048]{2,1,0:T(8,128)(2,1)}, bf16[2,128,2048]{2,1,0:T(8,128)(2,1)}, u32[]{:S(2)}, u32[]{:S(2)}) collective-permute-start(bf16[2,128,2048]{2,1,0:T(8,128)(2,1)} %bitcast.60), channel_id=1, source_target_pairs={{3,2},{2,1},{1,0},{7,6},{6,5},{5,4},{11,10},{10,9},{9,8},{15,14},{... | collective-permute-start | bytes 3145736 | tf_op jit(solution)/shard_map/ppermute | solution.py:557
  790.5 34.5 %collective-permute-start.31 = (bf16[2,128,2048]{2,1,0:T(8,128)(2,1)}, bf16[2,128,2048]{2,1,0:T(8,128)(2,1)}, u32[]{:S(2)}, u32[]{:S(2)}) collective-permute-start(bf16[2,128,2048]{2,1,0:T(8,128)(2,1)} %collective-permute-done.29), channel_id=1, source_target_pairs={{1,2},{2,3},{5,6},{6,7},{9,10},{10,11},{13,14},{14,15},{17,18},{18... | collective-permute-start | bytes 3145736 | tf_op jit(solution)/shard_map/ppermute | solution.py:563
  794.1 30.9 %collective-permute-start.32 = (bf16[2,128,2048]{2,1,0:T(8,128)(2,1)}, bf16[2,128,2048]{2,1,0:T(8,128)(2,1)}, u32[]{:S(2)}, u32[]{:S(2)}) collective-permute-start(bf16[2,128,2048]{2,1,0:T(8,128)(2,1)} %collective-permute-done.30), channel_id=1, source_target_pairs={{2,1},{1,0},{6,5},{5,4},{10,9},{9,8},{14,13},{13,12},{18,17},{17,1... | collective-permute-start | bytes 3145736 | tf_op jit(solution)/shard_map/ppermute | solution.py:564
  826.3 35.8 %collective-permute-start.38 = (bf16[2,128,2048]{2,1,0:T(8,128)(2,1)S(1)}, bf16[2,128,2048]{2,1,0:T(8,128)(2,1)S(1)}, u32[]{:S(2)}, u32[]{:S(2)}) collective-permute-start(bf16[2,128,2048]{2,1,0:T(8,128)(2,1)S(1)} %broadcast_select_fusion), channel_id=1, source_target_pairs={{2,3},{1,0},{6,7},{5,4},{10,11},{9,8},{14,15},{13,12},{18,19},{17,... | collective-permute-start | bytes 3145736 | tf_op jit(solution)/shard_map/ppermute | solution.py:570
  (75 other events, 1202.1 us)
Sparse Core Ops, SparseCore 0:
  10.4 46.6 all-gather.3
  68.5 79.0 all-gather.5
  150.0 136.5 all-gather.7
  434.5 76.5 reduce-scatter.3
  515.0 189.5 reduce-scatter.5
  708.7 61.7 reduce-scatter.7

commit v5 on v4

--- a/solution.py
+++ b/solution.py
@@ -487,7 +487,7 @@
 
 def adam_arrays(clip_factor, grad, first, second, master):
     arrays, rows, columns = master.shape
-    step = min(rows, max(16, 2**17 // columns))
+    step = min(rows, max(16, 2**18 // columns))
     state = pl.BlockSpec((None, step, columns), lambda a, i, *_: (a, i, 0))
     wide = jax.ShapeDtypeStruct(master.shape, WIDE)
     return pl.pallas_call(

time: 884 us -> 883 us (level)
  no operation moved by 1% of the time
where the time goes in v5:
time: 883 us; the launch traced here: 872 us
  waiting for transfers between devices  231 us (26%)
  Pallas kernels  227 us (26%)
  starting transfers between devices  124 us (14%)
  other arithmetic  92.2 us (10%)
  blocking collectives  61.5 us (7%)
  local copies, waits for them, and re-layouts  57.6 us (7%)
  matrix products  50.9 us (6%)
  between operations  28.1 us (3%)
    pallas_call x2, Pallas kernels, feed_forward(): pl.pallas_call(functools.partial(ffn_kernel, len(pieces)), out_shape=[ful...  65.1 us
    pallas_call x1, Pallas kernels, attention_backward(): pl.pallas_call(functools.partial(backward_kernel, sizes), out_shape=[jax....  62.1 us
    all_to_all x1, blocking collectives, per_device(): qkv = lax.all_to_all(sent, 'seq', split_axis=0, concat_axis=0, tiled=True)  52.6 us
    dot_general x7, matrix products, dot(): return lax.dot_general(left, right, dims, preferred_element_type=WIDE)  50.9 us
    pallas_call x1, Pallas kernels, feed_forward_wgrad(): pl.pallas_call(functools.partial(ffn_wgrad_kernel, steps), out_shape=jax....  37.7 us
    pallas_call x1, Pallas kernels, attention_forward(): pl.pallas_call(functools.partial(forward_kernel, sizes), out_shape=[jax.S...  35.7 us
    ppermute x3, waiting for transfers between devices, direct_terms(): lax.ppermute(terms[k], 'head', [(j, j ^ k) for j in range(count)])  33.4 us
    dynamic_update_slice x12, other arithmetic, line_gather_wide(): lax.dynamic_update_slice(full, jnp.where(there, part, piece).astype(WIDE)...  31 us
  transfers between devices with their start and end apart: 50, of which 35 were waited for; matrix products, arithmetic and copies ran while one was open for 19% of the time, Pallas kernels for 21%

profile of v5, /device:TPU:8, one launch (start us, length us, event | category | flops | bytes accessed | tf_op | source)
XLA Modules:
  0.0 872.3 jit_solution(4264546057402437996)
XLA Ops:
  24.6 8.9 %all_gather.12 = bf16[2,2048]{1,0:T(2,128)(2,1)S(1)} all-gather(bf16[2,256]{1,0:T(2,128)(2,1)S(1)} %get-tuple-element.193), channel_id=1, replica_groups=mesh['seq'=8,'head'=4] {'seq'}, dimensions={1}, use_global_device_ids=true | all-gather | bytes 9216 | tf_op jit(solution)/shard_map/all_gather | solution.py:724
  44.5 12.7 %all-gather.4.cloned.1.call-done.w_ref = bf16[2048,1536]{1,0:T(8,128)(2,1)} async-done(((bf16[256,1536]{1,0:T(8,128)(2,1)}), bf16[2048,1536]{1,0:T(8,128)(2,1)}) %all-gather.4.cloned.1.call-update) | async-done | bytes 6291472 | tf_op jit(solution)/shard_map/all_gather | solution.py:725
  57.2 11.1 %projection.1 = bf16[4,2,512,384]{3,2,1,0:T(8,128)(2,1)} custom-call(bf16[1024,2048]{1,0:T(8,128)(2,1)} %fusion.2.n_ref, bf16[2048,1536]{1,0:T(8,128)(2,1)} %all-gather.4.cloned.1.call-done.w_ref), custom_call_target="tpu_custom_call" | custom-call | flops 6442450944 | bytes 13631488 | tf_op jit(solution)/shard_map/projection/pallas_call | solution.py:313
  68.4 52.6 %all_to_all.38 = bf16[8,512,384]{2,1,0:T(8,128)(2,1)S(1)} all-to-all(bf16[8,512,384]{2,1,0:T(8,128)(2,1)} %bitcast.164), channel_id=1, replica_groups=mesh['seq'=8,'head'=4] {'seq'}, dimensions={0} | all-to-all | bytes 6291456 | tf_op jit(solution)/shard_map/all_to_all | solution.py:740
  129.0 35.7 %attention_forward.1 = (bf16[8,512,128]{2,1,0:T(8,128)(2,1)}, f32[8,1,512]{2,1,0:T(1,128)S(1)}) custom-call(s32[2]{0:T(128)S(1)} %pad_add_fusion.ints, f32[6]{0:T(128)S(1)} %reshape.369.floats, bf16[8,512,128]{2,1,0:T(8,128)(2,1)S(1)} %slice.199.q_ref, bf16[8,512,256]{2,1,0:T(8,128)(2,1)S(1)} %slice.200.rest_0_, ...), custom_call_target="tpu_custom_call" | custom-call | flops 17179869184 | bytes 8388608 | tf_op jit(solution)/shard_map/attention_forward/pallas_call | solution.py:135
  171.1 24.9 %all-to-all-done.1 = bf16[32,128,128]{2,1,0:T(8,128)(2,1)S(1)} async-done(((bf16[32,128,128]{2,1,0:T(8,128)(2,1)}), bf16[32,128,128]{2,1,0:T(8,128)(2,1)S(1)}, u32[]{:S(2)}, u32[]{:S(2)}) %all-to-all-start.1) | async-done | bytes 1048608 | tf_op jit(solution)/shard_map/all_to_all | solution.py:748
  197.8 6.2 multiply_reduce_fusion.1
  252.6 5.6 collective-permute-done.7.refs_4_
  269.4 8.8 %collective-permute-done.8.refs_5_ = bf16[128,2048]{1,0:T(8,128)(2,1)} collective-permute-done((bf16[128,2048]{1,0:T(8,128)(2,1)S(1)}, bf16[128,2048]{1,0:T(8,128)(2,1)}, u32[]{:S(2)}, u32[]{:S(2)}) %collective-permute-start.8) | collective-permute-done | bytes 524320 | tf_op jit(solution)/shard_map/ppermute | solution.py:570
  278.2 8.5 all-gather.8.cloned.1.call-done.refs_7_.refs_8_.refs_9_
  286.7 32.5 %feed_forward.2 = (bf16[512,2048]{1,0:T(8,128)(2,1)}, bf16[512,2048]{1,0:T(8,128)(2,1)}, bf16[512,2048]{1,0:T(8,128)(2,1)}, bf16[512,2048]{1,0:T(8,128)(2,1)}, bf16[512,2048]{1,0:T(8,128)(2,1)}) custom-call(s32[4]{0:T(128)} %compare_select_fusion.3.table, bf16[128,2048]{1,0:T(8,128)(2,1)} %copy-done.35, bf16[128,2048]{1,0:T(8,128)(2,1)} %collective-permute-done.4.refs_1_, ...), custom_call_target="tpu_custom_call" | custom-call | flops 21474836480 | bytes 25165824 | tf_op jit(solution)/shard_map/feed_forward/pallas_call | solution.py:389
  324.3 32.6 %feed_forward.3 = (bf16[512,2048]{1,0:T(8,128)(2,1)}, bf16[512,2048]{1,0:T(8,128)(2,1)}, bf16[512,2048]{1,0:T(8,128)(2,1)}, bf16[512,2048]{1,0:T(8,128)(2,1)}, bf16[512,2048]{1,0:T(8,128)(2,1)}) custom-call(s32[4]{0:T(128)} %compare_select_fusion.3.table, bf16[128,2048]{1,0:T(8,128)(2,1)} %copy-done.34, bf16[128,2048]{1,0:T(8,128)(2,1)} %collective-permute-done.9.refs_1_, ...), custom_call_target="tpu_custom_call" | custom-call | flops 21474836480 | bytes 25165824 | tf_op jit(solution)/shard_map/feed_forward/pallas_call | solution.py:389
  356.9 12.9 %all-to-all-done.2 = bf16[4,128,2048]{2,1,0:T(8,128)(2,1)} async-done(((bf16[4,128,2048]{2,1,0:T(8,128)(2,1)}), bf16[4,128,2048]{2,1,0:T(8,128)(2,1)}, u32[]{:S(2)}, u32[]{:S(2)}) %all-to-all-start.2) | async-done | bytes 2097184 | tf_op jit(solution)/shard_map/all_to_all | solution.py:512
  369.8 7.8 all-to-all-start.3
  382.4 37.7 %feed_forward_wgrad.1 = bf16[2048,6144]{1,0:T(8,128)(2,1)} custom-call(bf16[512,2048]{1,0:T(8,128)(2,1)} %get-tuple-element.122.n_a, bf16[512,2048]{1,0:T(8,128)(2,1)} %get-tuple-element.123.n_b, bf16[1024,2048]{1,0:T(8,128)(2,1)} %c_ref.1, bf16[512,2048]{1,0:T(8,128)(2,1)} %get-tuple-element.124.gate_a, bf16[512,2048]{1,0:T(8,128)(2,1)} %get-tuple-element.125.gate_b, ...), custom_call_target="tpu_custom_call" | custom-call | flops 2097152 | bytes 2097152 | tf_op jit(solution)/shard_map/feed_forward_wgrad/pallas_call | solution.py:456
  428.6 5.8 convolution_convert_fusion.1
  435.6 5.7 convolution_convert_fusion.3
  443.4 6.8 all-to-all-start.4
  450.2 8.7 fusion.13
  459.0 8.8 %fusion.10 = bf16[512,2048]{1,0:T(8,128)(2,1)S(1)} fusion(bf16[512,2048]{1,0:T(8,128)(2,1)S(1)} %copy-done.36, bf16[2048,6144]{1,0:T(8,128)(2,1)} %all-gather.8.cloned.1.call-done.refs_7_.refs_8_.refs_9_), kind=kOutput, calls=%fused_computation.30 | convolution fusion | flops 4296015872 | bytes 12582912 | tf_op jit(solution)/shard_map/dot_general | solution.py:35
  469.9 6.6 all-to-all-done.4
  477.7 62.1 %attention_backward.1 = (bf16[8,512,128]{2,1,0:T(8,128)(2,1)}, bf16[8,512,256]{2,1,0:T(8,128)(2,1)}, bf16[8,512,256]{2,1,0:T(8,128)(2,1)}) custom-call(s32[2]{0:T(128)} %copy-done.11, f32[6]{0:T(128)} %copy-done.10, bf16[8,512,128]{2,1,0:T(8,128)(2,1)} %copy-done.9, bf16[8,512,128]{2,1,0:T(8,128)(2,1)} %bitcast.175, bf16[8,512,256]{2,1,0:T(8,128)(2,1)} %copy-done.6, ...), custom_call_target="tpu_custom_call" | custom-call | flops 214748364800 | bytes 16777216 | tf_op jit(solution)/shard_map/attention_backward/pallas_call | solution.py:249
  555.5 33.4 %collective-permute-done.16 = bf16[2,128,2048]{2,1,0:T(8,128)(2,1)} collective-permute-done((bf16[2,128,2048]{2,1,0:T(8,128)(2,1)}, bf16[2,128,2048]{2,1,0:T(8,128)(2,1)}, u32[]{:S(2)}, u32[]{:S(2)}) %collective-permute-start.16) | collective-permute-done | bytes 1048608 | tf_op jit(solution)/shard_map/ppermute | solution.py:626
  610.2 9.0 %collective-permute-done.18 = bf16[2,128,2048]{2,1,0:T(8,128)(2,1)} collective-permute-done((bf16[2,128,2048]{2,1,0:T(8,128)(2,1)S(1)}, bf16[2,128,2048]{2,1,0:T(8,128)(2,1)}, u32[]{:S(2)}, u32[]{:S(2)}) %collective-permute-start.18) | collective-permute-done | bytes 1048608 | tf_op jit(solution)/shard_map/ppermute | solution.py:556
  633.0 6.9 convolution_convert_fusion.2
  649.5 13.2 %collective-permute-done.21 = bf16[2,128,2048]{2,1,0:T(8,128)(2,1)S(1)} collective-permute-done((bf16[2,128,2048]{2,1,0:T(8,128)(2,1)}, bf16[2,128,2048]{2,1,0:T(8,128)(2,1)S(1)}, u32[]{:S(2)}, u32[]{:S(2)}) %collective-permute-start.21) | collective-permute-done | bytes 1048608 | tf_op jit(solution)/shard_map/ppermute | solution.py:563
  677.9 8.8 %convolution_convert_fusion = bf16[2048,1536]{1,0:T(8,128)(2,1)} fusion(bf16[1024,2048]{1,0:T(8,128)(2,1)S(1)} %copy-done.25, bf16[1024,1536]{1,0:T(8,128)(2,1)S(1)} %bitcast.163), kind=kOutput, calls=%fused_computation.5 | convolution fusion | flops 6445596672 | bytes 13631488 | tf_op jit(solution)/shard_map/dot_general | solution.py:35
  689.8 12.3 %collective-permute-done.24 = bf16[320,2048]{1,0:T(8,128)(2,1)} collective-permute-done((bf16[320,2048]{1,0:T(8,128)(2,1)}, bf16[320,2048]{1,0:T(8,128)(2,1)}, u32[]{:S(2)}, u32[]{:S(2)}) %collective-permute-start.24) | collective-permute-done | bytes 1310752 | tf_op jit(solution)/shard_map/ppermute | solution.py:534
  737.9 11.9 %collective-permute-done.28 = bf16[320,2048]{1,0:T(8,128)(2,1)S(1)} collective-permute-done((bf16[320,2048]{1,0:T(8,128)(2,1)S(1)}, bf16[320,2048]{1,0:T(8,128)(2,1)S(1)}, u32[]{:S(2)}, u32[]{:S(2)}) %collective-permute-start.28) | collective-permute-done | bytes 1310752 | tf_op jit(solution)/shard_map/ppermute | solution.py:543
  749.8 7.3 collective-permute-done.27
  811.3 6.3 collective-permute-done.36
  839.2 11.1 %adam.3 = (f32[3,256,2048]{2,1,0:T(8,128)}, f32[3,256,2048]{2,1,0:T(8,128)}, f32[3,256,2048]{2,1,0:T(8,128)}, f32[3,256,2048]{2,1,0:T(8,128)}, bf16[3,256,2048]{2,1,0:T(8,128)(2,1)}) custom-call(f32[1]{0:T(128)} %bitcast.68.clip, bf16[256,6144]{1,0:T(8,128)(2,1)S(1)} %copy-done, f32[3,256,2048]{2,1,0:T(8,128)S(1)} %copy-done.2, ...), custom_call_target="tpu_custom_call" | custom-call | flops 31457280 | bytes 50331648 | tf_op jit(solution)/shard_map/adam/pallas_call | solution.py:493
  (330 shorter events, 321.0 us)
Async XLA Ops:
  7.2 50.0 %all-gather.4.cloned.1.call-start = ((), (), s32[]{:S(2)}) async-start(), calls=%async_computation.9 | async-start | bytes 7077888 | tf_op jit(solution)/shard_map/all_gather | solution.py:725
  10.3 187.4 %all-gather.6.cloned.1.call-start = ((), (), s32[]{:S(2)}) async-start(), calls=%async_computation.10 | async-start | bytes 9437184 | tf_op jit(solution)/shard_map/all_gather | solution.py:739
  11.7 22.9 %collective-permute-start.1 = (bf16[256,512]{0,1:T(8,128)(2,1)S(1)}, bf16[256,512]{0,1:T(8,128)(2,1)}, u32[]{:S(2)}, u32[]{:S(2)}) collective-permute-start(bf16[256,512]{0,1:T(8,128)(2,1)S(1)} %bitcast.173), channel_id=1, source_target_pairs={{0,2},{1,3},{2,0},{3,1},{4,6},{5,7},{6,4},{7,5},{8,10},{9,11},{10,... | collective-permute-start | bytes 786440 | tf_op jit(solution)/shard_map/ppermute | solution.py:635
  14.7 23.2 %collective-permute-start.2 = (bf16[256,512]{0,1:T(8,128)(2,1)S(1)}, bf16[256,512]{0,1:T(8,128)(2,1)}, u32[]{:S(2)}, u32[]{:S(2)}) collective-permute-start(bf16[256,512]{0,1:T(8,128)(2,1)S(1)} %bitcast.174), channel_id=1, source_target_pairs={{0,3},{1,2},{2,1},{3,0},{4,7},{5,6},{6,5},{7,4},{8,11},{9,10},{10,... | collective-permute-start | bytes 786440 | tf_op jit(solution)/shard_map/ppermute | solution.py:635
  68.3 218.3 %all-gather.8.cloned.1.call-start = ((), (), s32[]{:S(2)}) async-start(), calls=%async_computation.11 | async-start | bytes 28311552 | tf_op jit(solution)/shard_map/all_gather | solution.py:744
  164.8 31.3 %all-to-all-start.1 = ((bf16[32,128,128]{2,1,0:T(8,128)(2,1)}), bf16[32,128,128]{2,1,0:T(8,128)(2,1)S(1)}, u32[]{:S(2)}, u32[]{:S(2)}) async-start(bf16[32,128,128]{2,1,0:T(8,128)(2,1)} %bitcast.19), calls=%async_computation.1 | async-start | bytes 2097152 | tf_op jit(solution)/shard_map/all_to_all | solution.py:748
  224.4 22.6 %collective-permute-start.12 = (bf16[128,2048]{1,0:T(8,128)(2,1)}, bf16[128,2048]{1,0:T(8,128)(2,1)S(1)}, u32[]{:S(2)}, u32[]{:S(2)}) collective-permute-start(bf16[128,2048]{1,0:T(8,128)(2,1)} %collective-permute-done.11.refs_3_), channel_id=1, source_target_pairs={{2,1},{1,0},{6,5},{5,4},{10,9},{9,8},{14,13},{13,12},{18,17},{17,1... | collective-permute-start | bytes 1572872 | tf_op jit(solution)/shard_map/ppermute | solution.py:564
  247.1 22.3 %collective-permute-start.13 = (bf16[128,2048]{1,0:T(8,128)(2,1)S(1)}, bf16[128,2048]{1,0:T(8,128)(2,1)}, u32[]{:S(2)}, u32[]{:S(2)}) collective-permute-start(bf16[128,2048]{1,0:T(8,128)(2,1)S(1)} %broadcast_select_fusion.2), channel_id=1, source_target_pairs={{2,3},{1,0},{6,7},{5,4},{10,11},{9,8},{14,15},{13,12},{18,19},{17,... | collective-permute-start | bytes 1572872 | tf_op jit(solution)/shard_map/ppermute | solution.py:570
  319.2 50.6 %all-to-all-start.2 = ((bf16[4,128,2048]{2,1,0:T(8,128)(2,1)}), bf16[4,128,2048]{2,1,0:T(8,128)(2,1)}, u32[]{:S(2)}, u32[]{:S(2)}) async-start(bf16[4,128,2048]{2,1,0:T(8,128)(2,1)} %bitcast.171), calls=%async_computation.2 | async-start | bytes 4194304 | tf_op jit(solution)/shard_map/all_to_all | solution.py:512
  369.8 52.4 %all-to-all-start.3 = ((bf16[4,128,2048]{2,1,0:T(8,128)(2,1)}), bf16[4,128,2048]{2,1,0:T(8,128)(2,1)}, u32[]{:S(2)}, u32[]{:S(2)}) async-start(bf16[4,128,2048]{2,1,0:T(8,128)(2,1)} %bitcast.170), calls=%async_computation.3 | async-start | bytes 4194304 | tf_op jit(solution)/shard_map/all_to_all | solution.py:512
  377.6 229.8 %reduce-scatter.4.cloned.1.call-start = ((), (), s32[]{:S(2)}) async-start(), calls=%async_computation.12 | async-start | bytes 9437184 | tf_op jit(solution)/shard_map/reduce_scatter | solution.py:814
  434.4 270.1 %reduce-scatter.6.cloned.1.call-start = ((), (), s32[]{:S(2)}) async-start(), calls=%async_computation.13 | async-start | bytes 28311552 | tf_op jit(solution)/shard_map/reduce_scatter | solution.py:788
  443.4 33.2 %all-to-all-start.4 = ((bf16[32,128,128]{2,1,0:T(8,128)(2,1)}), bf16[32,128,128]{2,1,0:T(8,128)(2,1)S(1)}, u32[]{:S(2)}, u32[]{:S(2)}) async-start(bf16[32,128,128]{2,1,0:T(8,128)(2,1)} %bitcast.31), calls=%async_computation.4 | async-start | bytes 2097152 | tf_op jit(solution)/shard_map/all_to_all | solution.py:810
  476.6 63.2 %collective-permute-start.14 = (bf16[2,128,2048]{2,1,0:T(8,128)(2,1)}, bf16[2,128,2048]{2,1,0:T(8,128)(2,1)}, u32[]{:S(2)}, u32[]{:S(2)}) collective-permute-start(bf16[2,128,2048]{2,1,0:T(8,128)(2,1)} %get-tuple-element.135), channel_id=1, source_target_pairs={{0,1},{1,0},{2,3},{3,2},{4,5},{5,4},{6,7},{7,6},{8,9},{9,8},{10,11... | collective-permute-start | bytes 3145736 | tf_op jit(solution)/shard_map/ppermute | solution.py:626
  476.6 63.2 %collective-permute-start.15 = (bf16[2,128,2048]{2,1,0:T(8,128)(2,1)}, bf16[2,128,2048]{2,1,0:T(8,128)(2,1)}, u32[]{:S(2)}, u32[]{:S(2)}) collective-permute-start(bf16[2,128,2048]{2,1,0:T(8,128)(2,1)} %get-tuple-element.136), channel_id=1, source_target_pairs={{0,2},{1,3},{2,0},{3,1},{4,6},{5,7},{6,4},{7,5},{8,10},{9,11},{10,... | collective-permute-start | bytes 3145736 | tf_op jit(solution)/shard_map/ppermute | solution.py:626
  540.1 48.8 %collective-permute-start.16 = (bf16[2,128,2048]{2,1,0:T(8,128)(2,1)}, bf16[2,128,2048]{2,1,0:T(8,128)(2,1)}, u32[]{:S(2)}, u32[]{:S(2)}) collective-permute-start(bf16[2,128,2048]{2,1,0:T(8,128)(2,1)} %get-tuple-element.140), channel_id=1, source_target_pairs={{0,3},{1,2},{2,1},{3,0},{4,7},{5,6},{6,5},{7,4},{8,11},{9,10},{10,... | collective-permute-start | bytes 3145736 | tf_op jit(solution)/shard_map/ppermute | solution.py:626
  550.9 75.9 %all-to-all-start.5 = ((bf16[8,528,384]{2,1,0:T(8,128)(2,1)}), bf16[8,528,384]{2,1,0:T(8,128)(2,1)}, u32[]{:S(2)}, u32[]{:S(2)}) async-start(bf16[8,528,384]{2,1,0:T(8,128)(2,1)} %fusion.9), calls=%async_computation.5 | async-start | bytes 6488064 | tf_op jit(solution)/shard_map/all_to_all | solution.py:830
  555.5 218.4 %reduce-scatter.8.cloned.1.call-start = ((), (), s32[]{:S(2)}) async-start(), calls=%async_computation.14 | async-start | bytes 7077888 | tf_op jit(solution)/shard_map/reduce_scatter | solution.py:896
  591.8 27.4 %collective-permute-start.18 = (bf16[2,128,2048]{2,1,0:T(8,128)(2,1)S(1)}, bf16[2,128,2048]{2,1,0:T(8,128)(2,1)}, u32[]{:S(2)}, u32[]{:S(2)}) collective-permute-start(bf16[2,128,2048]{2,1,0:T(8,128)(2,1)S(1)} %bitcast.140), channel_id=1, source_target_pairs={{0,1},{1,2},{2,3},{4,5},{5,6},{6,7},{8,9},{9,10},{10,11},{12,13},{... | collective-permute-start | bytes 3145736 | tf_op jit(solution)/shard_map/ppermute | solution.py:556
  595.8 26.5 %collective-permute-start.19 = (bf16[2,128,2048]{2,1,0:T(8,128)(2,1)S(1)}, bf16[2,128,2048]{2,1,0:T(8,128)(2,1)}, u32[]{:S(2)}, u32[]{:S(2)}) collective-permute-start(bf16[2,128,2048]{2,1,0:T(8,128)(2,1)S(1)} %bitcast.141), channel_id=1, source_target_pairs={{3,2},{2,1},{1,0},{7,6},{6,5},{5,4},{11,10},{10,9},{9,8},{15,14},{... | collective-permute-start | bytes 3145736 | tf_op jit(solution)/shard_map/ppermute | solution.py:557
  640.4 28.6 %collective-permute-start.20 = (bf16[320,2048]{1,0:T(8,128)(2,1)S(1)}, bf16[320,2048]{1,0:T(8,128)(2,1)S(1)}, u32[]{:S(2)}, u32[]{:S(2)}) collective-permute-start(bf16[320,2048]{1,0:T(8,128)(2,1)S(1)} %pad_maximum_fusion.1), channel_id=1, source_target_pairs={{0,1},{3,2},{4,5},{7,6},{8,9},{11,10},{12,13},{15,14},{16,17},{19,... | collective-permute-start | bytes 3932168 | tf_op jit(solution)/shard_map/ppermute | solution.py:529
  643.4 23.3 %collective-permute-start.22 = (bf16[2,128,2048]{2,1,0:T(8,128)(2,1)}, bf16[2,128,2048]{2,1,0:T(8,128)(2,1)S(1)}, u32[]{:S(2)}, u32[]{:S(2)}) collective-permute-start(bf16[2,128,2048]{2,1,0:T(8,128)(2,1)} %collective-permute-done.19), channel_id=1, source_target_pairs={{2,1},{1,0},{6,5},{5,4},{10,9},{9,8},{14,13},{13,12},{18,17},{17,1... | collective-permute-start | bytes 3145736 | tf_op jit(solution)/shard_map/ppermute | solution.py:564
  674.2 27.9 %collective-permute-start.24 = (bf16[320,2048]{1,0:T(8,128)(2,1)}, bf16[320,2048]{1,0:T(8,128)(2,1)}, u32[]{:S(2)}, u32[]{:S(2)}) collective-permute-start(bf16[320,2048]{1,0:T(8,128)(2,1)} %add_convert_fusion.2), channel_id=1, source_target_pairs={{1,2},{2,1},{5,6},{6,5},{9,10},{10,9},{13,14},{14,13},{17,18},{18,... | collective-permute-start | bytes 3932168 | tf_op jit(solution)/shard_map/ppermute | solution.py:534
  676.4 27.8 %collective-permute-start.23 = (bf16[320,2048]{1,0:T(8,128)(2,1)}, bf16[320,2048]{1,0:T(8,128)(2,1)}, u32[]{:S(2)}, u32[]{:S(2)}) collective-permute-start(bf16[320,2048]{1,0:T(8,128)(2,1)} %pad_maximum_fusion.4), channel_id=1, source_target_pairs={{0,1},{3,2},{4,5},{7,6},{8,9},{11,10},{12,13},{15,14},{16,17},{19,... | collective-permute-start | bytes 3932168 | tf_op jit(solution)/shard_map/ppermute | solution.py:534
  720.1 29.7 %collective-permute-start.28 = (bf16[320,2048]{1,0:T(8,128)(2,1)S(1)}, bf16[320,2048]{1,0:T(8,128)(2,1)S(1)}, u32[]{:S(2)}, u32[]{:S(2)}) collective-permute-start(bf16[320,2048]{1,0:T(8,128)(2,1)S(1)} %fusion.16), channel_id=1, source_target_pairs={{1,0},{2,3},{5,4},{6,7},{9,8},{10,11},{13,12},{14,15},{17,16},{18,... | collective-permute-start | bytes 3932168 | tf_op jit(solution)/shard_map/ppermute | solution.py:543
  724.1 32.9 %collective-permute-start.27 = (bf16[320,2048]{1,0:T(8,128)(2,1)S(1)}, bf16[320,2048]{1,0:T(8,128)(2,1)S(1)}, u32[]{:S(2)}, u32[]{:S(2)}) collective-permute-start(bf16[320,2048]{1,0:T(8,128)(2,1)S(1)} %add_convert_fusion.1), channel_id=1, source_target_pairs={{1,2},{2,1},{5,6},{6,5},{9,10},{10,9},{13,14},{14,13},{17,18},{18,... | collective-permute-start | bytes 3932168 | tf_op jit(solution)/shard_map/ppermute | solution.py:542
  728.4 32.0 %collective-permute-start.26 = (bf16[320,2048]{1,0:T(8,128)(2,1)S(1)}, bf16[320,2048]{1,0:T(8,128)(2,1)S(1)}, u32[]{:S(2)}, u32[]{:S(2)}) collective-permute-start(bf16[320,2048]{1,0:T(8,128)(2,1)S(1)} %copy-done.22), channel_id=1, source_target_pairs={{0,1},{3,2},{4,5},{7,6},{8,9},{11,10},{12,13},{15,14},{16,17},{19,... | collective-permute-start | bytes 3932168 | tf_op jit(solution)/shard_map/ppermute | solution.py:541
  764.8 25.7 %collective-permute-start.29 = (bf16[2,128,2048]{2,1,0:T(8,128)(2,1)}, bf16[2,128,2048]{2,1,0:T(8,128)(2,1)}, u32[]{:S(2)}, u32[]{:S(2)}) collective-permute-start(bf16[2,128,2048]{2,1,0:T(8,128)(2,1)} %bitcast.60), channel_id=1, source_target_pairs={{0,1},{1,2},{2,3},{4,5},{5,6},{6,7},{8,9},{9,10},{10,11},{12,13},{... | collective-permute-start | bytes 3145736 | tf_op jit(solution)/shard_map/ppermute | solution.py:556
  767.0 27.1 %collective-permute-start.30 = (bf16[2,128,2048]{2,1,0:T(8,128)(2,1)}, bf16[2,128,2048]{2,1,0:T(8,128)(2,1)}, u32[]{:S(2)}, u32[]{:S(2)}) collective-permute-start(bf16[2,128,2048]{2,1,0:T(8,128)(2,1)} %bitcast.60), channel_id=1, source_target_pairs={{3,2},{2,1},{1,0},{7,6},{6,5},{5,4},{11,10},{10,9},{9,8},{15,14},{... | collective-permute-start | bytes 3145736 | tf_op jit(solution)/shard_map/ppermute | solution.py:557
  790.5 34.5 %collective-permute-start.31 = (bf16[2,128,2048]{2,1,0:T(8,128)(2,1)}, bf16[2,128,2048]{2,1,0:T(8,128)(2,1)}, u32[]{:S(2)}, u32[]{:S(2)}) collective-permute-start(bf16[2,128,2048]{2,1,0:T(8,128)(2,1)} %collective-permute-done.29), channel_id=1, source_target_pairs={{1,2},{2,3},{5,6},{6,7},{9,10},{10,11},{13,14},{14,15},{17,18},{18... | collective-permute-start | bytes 3145736 | tf_op jit(solution)/shard_map/ppermute | solution.py:563
  794.1 30.9 %collective-permute-start.32 = (bf16[2,128,2048]{2,1,0:T(8,128)(2,1)}, bf16[2,128,2048]{2,1,0:T(8,128)(2,1)}, u32[]{:S(2)}, u32[]{:S(2)}) collective-permute-start(bf16[2,128,2048]{2,1,0:T(8,128)(2,1)} %collective-permute-done.30), channel_id=1, source_target_pairs={{2,1},{1,0},{6,5},{5,4},{10,9},{9,8},{14,13},{13,12},{18,17},{17,1... | collective-permute-start | bytes 3145736 | tf_op jit(solution)/shard_map/ppermute | solution.py:564
  826.3 34.9 %collective-permute-start.38 = (bf16[2,128,2048]{2,1,0:T(8,128)(2,1)S(1)}, bf16[2,128,2048]{2,1,0:T(8,128)(2,1)S(1)}, u32[]{:S(2)}, u32[]{:S(2)}) collective-permute-start(bf16[2,128,2048]{2,1,0:T(8,128)(2,1)S(1)} %broadcast_select_fusion), channel_id=1, source_target_pairs={{2,3},{1,0},{6,7},{5,4},{10,11},{9,8},{14,15},{13,12},{18,19},{17,... | collective-permute-start | bytes 3145736 | tf_op jit(solution)/shard_map/ppermute | solution.py:570
  (75 other events, 1198.2 us)
Sparse Core Ops, SparseCore 0:
  10.4 46.6 all-gather.3
  68.5 79.0 all-gather.5
  150.0 136.5 all-gather.7
  434.5 76.5 reduce-scatter.3
  515.0 189.5 reduce-scatter.5
  708.7 61.7 reduce-scatter.7
